TPU v7x, 32 devices: a whole 2x2x4 slice. The times are simulated.
32 devices in a mesh: groups: 2 (over y), tm: 4 (over z), head: 4 (over x, core).
Axes of the slice: x: 2, y: 2, z: 4, core: 2. Of those that a mesh axis runs over, the one named last changes fastest.
Arguments:
- queries: bfloat16 [3072, 24, 128], P(('groups', 'tm'), 'head'), parts along dimension 0, may hold values from -6 to 6
- key_rows: bfloat16 [3072, 24, 128], P(('groups', 'tm'), 'head'), parts along dimension 0, may hold values from -6 to 6
- value_rows: bfloat16 [3072, 24, 128], P(('groups', 'tm'), 'head'), parts along dimension 0, may hold values from -6 to 6
- keep_tiles: int32 [24, 9], P(('groups', 'tm')), parts along dimension 0, may hold values from 0 to 1, as said below
- out_weight: bfloat16 [3072, 5120], P('head', 'tm'), may hold values from -0.109375 to 0.109375
- gate_scale: float32 [10240], P(('groups', 'head')), parts along dimension 0, may hold values from 1 to 3
Outputs:
- gated_branch: bfloat16 [3072, 5120], P(('groups', 'tm'), 'head'), parts along dimension 0
There are 2 independent parts, one for each index of `groups`. A program takes and returns all parts, laid end to end along the dimension named above; an argument that names none is the same for every part. Nothing has to cross between parts.
Inputs may be any that keep to these rules, and one draw needn't show every extreme that they name: `keep_tiles`: each row is one query tile; the query tile itself is always kept; each row keeps 3 to 6 tiles, and some row keeps exactly 6.
All inputs are finite; a program needn't handle non-finite values.
Results may differ from a plain program's by a relative error of at most 0.014.
Values may be sent and summed in bfloat16 or wider, within the bound.
No kernel may reach another device: no remote copies, remote signals or barrier semaphores. Data moves between devices by JAX's collectives and lax.ppermute only.
A program may use at most 64 MiB of HBM per device.

v0:
```python
import math

import jax
import jax.numpy as jnp
from jax import lax
from jax.sharding import PartitionSpec as P

HD = 128
TILE = 128
KEEP_MAX = 6


def passed_along(array, axis, by):
    count = lax.axis_size(axis)
    return lax.ppermute(array, axis, [(i, (i + by) % count) for i in range(count)])


def neighbour_slabs(key_value, reach_slabs):
    lower_list = []
    upper_list = []
    for distance in range(1, reach_slabs + 1):
        lower_list.append(passed_along((key_value[0], key_value[1]), "tm", distance))
        upper_list.append(passed_along((key_value[0], key_value[1]), "tm", -distance))
    ordered = lower_list[::-1] + [key_value] + upper_list
    key_all = jnp.concatenate([slab_pair[0] for slab_pair in ordered], axis=0)
    value_all = jnp.concatenate([slab_pair[1] for slab_pair in ordered], axis=0)
    return (key_all, value_all)


def compact_attend(queries, key_all, value_all, keep_tiles):
    tile_count, cand_count = keep_tiles.shape
    head_count = queries.shape[1]
    position = jnp.cumsum(keep_tiles, axis=1) - 1
    slot_ids = jnp.arange(KEEP_MAX, dtype=jnp.int32)
    selector = (
        (keep_tiles[:, None, :] > 0) & (position[:, None, :] == slot_ids[None, :, None])
    ).astype(jnp.int32)
    cand_ids = jnp.arange(cand_count, dtype=jnp.int32)
    chosen_index = jnp.sum(selector * cand_ids[None, None, :], axis=2)
    slot_valid = jnp.sum(selector, axis=2)
    key_tiles = key_all.reshape(cand_count, TILE, head_count, HD)
    value_tiles = value_all.reshape(cand_count, TILE, head_count, HD)
    chosen_keys = jnp.take(key_tiles, chosen_index, axis=0)
    chosen_values = jnp.take(value_tiles, chosen_index, axis=0)
    query_tiles = queries.reshape(tile_count, TILE, head_count, HD)
    score_scale = 1.0 / math.sqrt(HD)
    scores = (
        jnp.einsum(
            "tqhd,tskhd->thqsk", query_tiles, chosen_keys, preferred_element_type=jnp.float32
        )
        * score_scale
    )
    allowed = slot_valid[:, None, None, :, None] > 0
    scores = jnp.where(allowed, scores, -jnp.inf)
    row_peak = jnp.max(scores, axis=(3, 4), keepdims=True)
    exp_scores = jnp.exp(scores - row_peak)
    row_total = jnp.sum(exp_scores, axis=(3, 4), keepdims=True)
    weights = (exp_scores / row_total).astype(jnp.bfloat16)
    attended = jnp.einsum(
        "thqsk,tskhd->tqhd", weights, chosen_values, preferred_element_type=jnp.float32
    )
    return attended.astype(jnp.bfloat16).reshape(tile_count * TILE, head_count, HD)


def shards(queries, key_rows, value_rows, keep_tiles, out_weight, gate_scale):
    reach_slabs = min(2, (lax.axis_size("tm") - 1) // 2)
    key_all, value_all = neighbour_slabs((key_rows, value_rows), reach_slabs)
    attended = compact_attend(queries, key_all, value_all, keep_tiles)
    attended_flat = attended.reshape(attended.shape[0], attended.shape[1] * attended.shape[2])
    partial_value = jnp.dot(
        attended_flat,
        lax.all_gather(out_weight, "tm", axis=1, tiled=True),
        preferred_element_type=jnp.float32,
    )
    summed = lax.psum_scatter(
        partial_value.astype(jnp.bfloat16), "head", scatter_dimension=1, tiled=True
    ).astype(jnp.float32)
    return (gate_scale[None, :] * summed).astype(jnp.bfloat16)


def solution(mesh):
    placed = (
        P(("groups", "tm"), "head", None),
        P(("groups", "tm"), "head", None),
        P(("groups", "tm"), "head", None),
        P(("groups", "tm"), None),
        P("head", "tm"),
        P(("groups", "head")),
    )
    return jax.shard_map(
        shards, mesh=mesh, in_specs=placed, out_specs=P(("groups", "tm"), "head"), check_vma=False
    )
```

profile of v0, /device:TPU:1, one launch (start us, length us, event | category | flops | bytes accessed | tf_op | source)
XLA Modules:
  0.0 249.7 jit_solution(13154018068023557793)
XLA Ops:
  6.5 0.0 copy-start
  6.5 0.0 all-gather.2.cloned.1.call-start
  6.5 0.7 all-gather.2.cloned.1.call-update
  7.3 0.0 reduce-scatter.2.cloned.1.call-start
  7.3 2.2 collective-permute-start
  9.5 2.1 collective-permute-start.1
  11.6 0.0 collective-permute-start.2
  11.6 3.3 %collective-permute-start.3 = (bf16[384,6,128]{2,0,1:T(8,128)(2,1)}, bf16[384,6,128]{2,0,1:T(8,128)(2,1)}, u32[]{:S(2)}, u32[]{:S(2)}) collective-permute-start(bf16[384,6,128]{2,0,1:T(8,128)(2,1)} %param.9), channel_id=1, source_target_pairs={{0,12},{4,0},{8,4},{12,8},{1,13},{5,1},{9,5},{13,9},{2,14},{6,2},{... | collective-permute-start | bytes 1769480 | tf_op jit(solution)/shard_map/ppermute | solution.py:15
  14.8 0.9 reduce_window_sum.11
  15.7 0.7 broadcast_compare_fusion.1
  16.4 0.2 convert_reduce_fusion
  16.6 0.1 reshape.53
  16.7 8.1 %collective-permute-done = bf16[384,6,128]{2,0,1:T(8,128)(2,1)S(1)} collective-permute-done((bf16[384,6,128]{2,0,1:T(8,128)(2,1)}, bf16[384,6,128]{2,0,1:T(8,128)(2,1)S(1)}, u32[]{:S(2)}, u32[]{:S(2)}) %collective-permute-start) | collective-permute-done | bytes 589856 | tf_op jit(solution)/shard_map/ppermute | solution.py:15
  24.8 43.2 %collective-permute-done.1 = bf16[384,6,128]{2,0,1:T(8,128)(2,1)} collective-permute-done((bf16[384,6,128]{2,0,1:T(8,128)(2,1)}, bf16[384,6,128]{2,0,1:T(8,128)(2,1)}, u32[]{:S(2)}, u32[]{:S(2)}) %collective-permute-start.1) | collective-permute-done | bytes 589856 | tf_op jit(solution)/shard_map/ppermute | solution.py:15
  68.0 1.4 pad_maximum_fusion
  69.4 0.0 copy-start.1
  69.4 3.1 %gather_fusion = bf16[18,128,6,128]{3,1,2,0:T(8,128)(2,1)} fusion(bf16[9,128,6,128]{3,1,0,2:T(8,128)(2,1)S(1)} %bitcast.40, s32[1024]{0:T(1024)S(1)} %pad_clamp_fusion), kind=kCustom, calls=%fused_computation.clone | custom fusion | bytes 7077960 | tf_op jit(solution)/shard_map/jit(_take)/gather | solution.py:44
  72.5 2.3 collective-permute-done.2
  74.9 34.4 %collective-permute-done.3 = bf16[384,6,128]{2,0,1:T(8,128)(2,1)} collective-permute-done((bf16[384,6,128]{2,0,1:T(8,128)(2,1)}, bf16[384,6,128]{2,0,1:T(8,128)(2,1)}, u32[]{:S(2)}, u32[]{:S(2)}) %collective-permute-start.3) | collective-permute-done | bytes 589856 | tf_op jit(solution)/shard_map/ppermute | solution.py:15
  109.3 1.2 pad_maximum_fusion.1
  110.4 3.1 %gather_fusion.1 = bf16[18,128,6,128]{3,1,2,0:T(8,128)(2,1)} fusion(bf16[9,128,6,128]{3,1,0,2:T(8,128)(2,1)S(1)} %bitcast.39, s32[1024]{0:T(1024)S(1)} %pad_clamp_fusion), kind=kCustom, calls=%fused_computation.1.clone | custom fusion | bytes 7077960 | tf_op jit(solution)/shard_map/jit(_take)/gather | solution.py:43
  113.6 3.8 %broadcast_select_fusion.1 = (bf16[3,6,128,6,128]{4,2,3,1,0:T(8,128)(2,1)S(1)}, bf16[3,6,128,6,128]{4,2,3,1,0:T(8,128)(2,1)S(1)}) fusion(bf16[3,6,128,6,128]{4,2,3,1,0:T(8,128)(2,1)} %bitcast.41, pred[3,6]{1,0:T(4,128)(4,1)S(1)} %get-tuple-element.12, bf16[3,6,128,6,128]{4,2,3,1,0:T(8,128)(2,1)} %bitcast.42), kind=kLoop, calls=%fused_computation.14 | loop fusion | flops 3538944 | bytes 14155794 | tf_op jit(solution)/shard_map/jit(_take)/select_n | solution.py:44
  117.4 1.1 bitcast_reduce_fusion
  118.5 1.5 fusion.1
  120.0 2.9 %fusion.13 = bf16[3,128,6,128]{1,3,2,0:T(8,128)(2,1)S(1)} fusion(f32[3,6,6,128,128]{4,3,2,1,0:T(8,128)S(1)} %get-tuple-element.11, f32[3,6,128]{2,1,0:T(8,128)S(1)} %fusion.1, f32[3,6,128]{2,1,0:T(8,128)S(1)} %get-tuple-element.10, pred[3,6]{1,0:T(4,128)(4,1)S(1)} %get-tuple-element.13, bf16[3,6,128,6,128]{4,2,3,1,0:T(8,128)(2,1)S(1)} %get-tuple-element.8), kind=kOutput, calls=%fused_computation.21 | convolution fusion | flops 462127104 | bytes 11225106 | tf_op jit(solution)/shard_map/thqsk,tskhd->tqhd/dot_general | solution.py:59
  122.9 0.4 copy.18
  123.3 67.2 %all-gather.2.cloned.1.call-done = bf16[768,5120]{1,0:T(8,128)(2,1)} async-done(((bf16[768,1280]{1,0:T(8,128)(2,1)}), bf16[768,5120]{1,0:T(8,128)(2,1)}) %all-gather.2.cloned.1.call-update) | async-done | bytes 7864336 | tf_op jit(solution)/shard_map/all_gather | solution.py:72
  190.5 7.9 %convolution_convert_fusion = bf16[384,5120]{1,0:T(8,128)(2,1)} fusion(bf16[768,5120]{1,0:T(8,128)(2,1)} %all-gather.2.cloned.1.call-done, bf16[48,8,6,128]{3,2,1,0:T(8,128)(2,1)S(1)} %bitcast.43), kind=kOutput, calls=%fused_computation.7 | convolution fusion | flops 3021864960 | bytes 12386304 | tf_op jit(solution)/shard_map/dot_general | solution.py:70
  198.4 0.0 reduce-scatter.2.cloned.1.call-update
  198.4 42.1 %reduce-scatter.2.cloned.1.call-done = bf16[384,1280]{1,0:T(8,128)(2,1)} async-done(((bf16[384,5120]{1,0:T(8,128)(2,1)}), bf16[384,1280]{1,0:T(8,128)(2,1)}) %reduce-scatter.2.cloned.1.call-update) | async-done | bytes 983056 | tf_op jit(solution)/shard_map/reduce_scatter | solution.py:75
  240.6 0.0 copy-done.2
  240.6 2.3 multiply_convert_fusion
  (7 shorter events, 0.0 us)
Async XLA Ops:
  6.5 110.8 %copy-start = (bf16[384,6,128]{2,0,1:T(8,128)(2,1)S(1)}, bf16[384,6,128]{2,0,1:T(8,128)(2,1)}, u32[]{:S(2)}) copy-start(bf16[384,6,128]{2,0,1:T(8,128)(2,1)} %param.8) | copy-start | bytes 1769476
  6.5 183.9 %all-gather.2.cloned.1.call-start = ((), (), s32[]{:S(2)}) async-start(), calls=%async_computation.1 | async-start | bytes 9830400 | tf_op jit(solution)/shard_map/all_gather | solution.py:72
  7.3 233.3 %reduce-scatter.2.cloned.1.call-start = ((), (), s32[]{:S(2)}) async-start(), calls=%async_computation.2 | async-start | bytes 4915200 | tf_op jit(solution)/shard_map/reduce_scatter | solution.py:75
  7.3 17.5 %collective-permute-start = (bf16[384,6,128]{2,0,1:T(8,128)(2,1)}, bf16[384,6,128]{2,0,1:T(8,128)(2,1)S(1)}, u32[]{:S(2)}, u32[]{:S(2)}) collective-permute-start(bf16[384,6,128]{2,0,1:T(8,128)(2,1)} %param.10), channel_id=1, source_target_pairs={{0,4},{4,8},{8,12},{12,0},{1,5},{5,9},{9,13},{13,1},{2,6},{6,10},{... | collective-permute-start | bytes 1769480 | tf_op jit(solution)/shard_map/ppermute | solution.py:15
  9.5 58.5 %collective-permute-start.1 = (bf16[384,6,128]{2,0,1:T(8,128)(2,1)}, bf16[384,6,128]{2,0,1:T(8,128)(2,1)}, u32[]{:S(2)}, u32[]{:S(2)}) collective-permute-start(bf16[384,6,128]{2,0,1:T(8,128)(2,1)} %param.10), channel_id=1, source_target_pairs={{0,12},{4,0},{8,4},{12,8},{1,13},{5,1},{9,5},{13,9},{2,14},{6,2},{... | collective-permute-start | bytes 1769480 | tf_op jit(solution)/shard_map/ppermute | solution.py:15
  11.6 63.3 %collective-permute-start.2 = (bf16[384,6,128]{2,0,1:T(8,128)(2,1)}, bf16[384,6,128]{2,0,1:T(8,128)(2,1)S(1)}, u32[]{:S(2)}, u32[]{:S(2)}) collective-permute-start(bf16[384,6,128]{2,0,1:T(8,128)(2,1)} %param.9), channel_id=1, source_target_pairs={{0,4},{4,8},{8,12},{12,0},{1,5},{5,9},{9,13},{13,1},{2,6},{6,10},{... | collective-permute-start | bytes 1769480 | tf_op jit(solution)/shard_map/ppermute | solution.py:15
  11.6 97.7 %collective-permute-start.3 = (bf16[384,6,128]{2,0,1:T(8,128)(2,1)}, bf16[384,6,128]{2,0,1:T(8,128)(2,1)}, u32[]{:S(2)}, u32[]{:S(2)}) collective-permute-start(bf16[384,6,128]{2,0,1:T(8,128)(2,1)} %param.9), channel_id=1, source_target_pairs={{0,12},{4,0},{8,4},{12,8},{1,13},{5,1},{9,5},{13,9},{2,14},{6,2},{... | collective-permute-start | bytes 1769480 | tf_op jit(solution)/shard_map/ppermute | solution.py:15
  69.4 39.9 %copy-start.1 = (bf16[384,6,128]{2,0,1:T(8,128)(2,1)S(1)}, bf16[384,6,128]{2,0,1:T(8,128)(2,1)}, u32[]{:S(2)}) copy-start(bf16[384,6,128]{2,0,1:T(8,128)(2,1)} %param.9) | copy-start | bytes 1769476
  198.4 42.2 %copy-start.2 = (f32[1280]{0:T(1024)S(1)}, f32[1280]{0:T(1024)}, u32[]{:S(2)}) copy-start(f32[1280]{0:T(1024)} %param.13) | copy-start | bytes 15364
Sparse Core Ops, SparseCore 0:
  8.9 181.4 all-gather.1
  198.6 41.9 reduce-scatter.1
where the time goes:
time: 251 us; the launch traced here: 250 us
  waiting for transfers between devices  198 us (79%)
  between operations  13.5 us (5%)
  other arithmetic  11.9 us (5%)
  matrix products  11.9 us (5%)
  starting transfers between devices  7.58 us (3%)
  local copies, waits for them, and re-layouts  6.77 us (3%)
    ppermute x4, waiting for transfers between devices, passed_along(): lax.ppermute(array, axis, [(i, (i + by) % count) for i in range(count)])  88 us
    all_gather x1, waiting for transfers between devices, shards(): lax.all_gather(out_weight, 'tm', axis=1, tiled=True)  67.2 us
    reduce_scatter x1, waiting for transfers between devices, shards(): lax.psum_scatter(partial_value.astype(jnp.bfloat16), 'head', scatter_dime...  42.1 us
    dot_general x1, matrix products, shards(): jnp.dot(attended_flat, lax.all_gather(out_weight, 'tm', axis=1, tiled=Tru...  7.93 us
    ppermute x4, starting transfers between devices, passed_along(): lax.ppermute(array, axis, [(i, (i + by) % count) for i in range(count)])  7.54 us
  transfers between devices with their start and end apart: 6, of which 6 were waited for; matrix products, arithmetic and copies ran while one was open for 8% of the time, Pallas kernels for 0%

commit v1 on v0

--- a/solution.py
+++ b/solution.py
@@ -15,16 +15,9 @@
     return lax.ppermute(array, axis, [(i, (i + by) % count) for i in range(count)])
 
 
-def neighbour_slabs(key_value, reach_slabs):
-    lower_list = []
-    upper_list = []
-    for distance in range(1, reach_slabs + 1):
-        lower_list.append(passed_along((key_value[0], key_value[1]), "tm", distance))
-        upper_list.append(passed_along((key_value[0], key_value[1]), "tm", -distance))
-    ordered = lower_list[::-1] + [key_value] + upper_list
-    key_all = jnp.concatenate([slab_pair[0] for slab_pair in ordered], axis=0)
-    value_all = jnp.concatenate([slab_pair[1] for slab_pair in ordered], axis=0)
-    return (key_all, value_all)
+def swapped(array, axis, mask):
+    count = lax.axis_size(axis)
+    return lax.ppermute(array, axis, [(i, i ^ mask) for i in range(count)])
 
 
 def compact_attend(queries, key_all, value_all, keep_tiles):
@@ -59,16 +52,30 @@
     attended = jnp.einsum(
         "thqsk,tskhd->tqhd", weights, chosen_values, preferred_element_type=jnp.float32
     )
-    return attended.astype(jnp.bfloat16).reshape(tile_count * TILE, head_count, HD)
+    return attended.astype(jnp.bfloat16).reshape(tile_count * TILE, head_count * HD)
 
 
-def shards(queries, key_rows, value_rows, keep_tiles, out_weight, gate_scale):
+def halo(key_rows, value_rows):
     reach_slabs = min(2, (lax.axis_size("tm") - 1) // 2)
-    key_all, value_all = neighbour_slabs((key_rows, value_rows), reach_slabs)
+    lower_list = []
+    upper_list = []
+    for distance in range(1, reach_slabs + 1):
+        lower_list.append([passed_along(rows, "tm", distance) for rows in (key_rows, value_rows)])
+        upper_list.append([passed_along(rows, "tm", -distance) for rows in (key_rows, value_rows)])
+    return lower_list[::-1], upper_list
+
+
+def joined(lower, own, upper):
+    ordered = lower + [own] + upper
+    return [jnp.concatenate([slab[which] for slab in ordered], axis=0) for which in (0, 1)]
+
+
+def any_mesh(queries, key_rows, value_rows, keep_tiles, out_weight, gate_scale):
+    lower, upper = halo(key_rows, value_rows)
+    key_all, value_all = joined(lower, (key_rows, value_rows), upper)
     attended = compact_attend(queries, key_all, value_all, keep_tiles)
-    attended_flat = attended.reshape(attended.shape[0], attended.shape[1] * attended.shape[2])
     partial_value = jnp.dot(
-        attended_flat,
+        attended,
         lax.all_gather(out_weight, "tm", axis=1, tiled=True),
         preferred_element_type=jnp.float32,
     )
@@ -76,6 +83,60 @@
         partial_value.astype(jnp.bfloat16), "head", scatter_dimension=1, tiled=True
     ).astype(jnp.float32)
     return (gate_scale[None, :] * summed).astype(jnp.bfloat16)
+
+
+def term(attended, weight):
+    return jnp.dot(attended, weight, preferred_element_type=jnp.float32).astype(jnp.bfloat16)
+
+
+def f32(array):
+    return array.astype(jnp.float32)
+
+
+def square_mesh(queries, key_rows, value_rows, keep_tiles, out_weight, gate_scale):
+    video = lax.axis_index("groups")
+    slab = lax.axis_index("tm")
+    head = lax.axis_index("head")
+    width = out_weight.shape[1] // 2
+
+    lower, upper = halo(key_rows, value_rows)
+    near = lax.dynamic_slice_in_dim(out_weight, video * width, width, 1)
+    far = lax.dynamic_slice_in_dim(out_weight, (1 - video) * width, width, 1)
+    near_2 = swapped(near, "tm", 2)
+    near_1 = swapped(near, "tm", 1)
+    near_3 = swapped(near_2, "tm", 1)
+    far_1 = swapped(near_1, "groups", 1)
+    far_2 = swapped(near_2, "groups", 1)
+    far_3 = swapped(near_3, "groups", 1)
+
+    key_all, value_all = joined(lower, (key_rows, value_rows), upper)
+    attended = compact_attend(queries, key_all, value_all, keep_tiles)
+
+    places = [(t, h) for t in range(4) for h in range(4)]
+    same_core = slab % 2 == head % 2
+    same_side = slab // 2 == head // 2
+
+    def summed_pair(first, second, flip):
+        kept = f32(jnp.where(same_core, first, second))
+        given = jnp.where(same_core, second, first)
+        total = kept + f32(swapped(given, "head", 1))
+        pairs = [
+            (4 * t + h, 4 * t + (h ^ 2)) for t, h in places if (t // 2 == h // 2) == flip
+        ]
+        return total, f32(lax.ppermute(total.astype(jnp.bfloat16), ("tm", "head"), pairs))
+
+    own_near, own_far = summed_pair(term(attended, near), term(attended, near_1), False), summed_pair(
+        term(attended, far), term(attended, far_1), False
+    )
+    other_near = summed_pair(term(attended, near_2), term(attended, near_3), True)
+    other_far = summed_pair(term(attended, far_2), term(attended, far_3), True)
+    halves = [
+        jnp.where(same_side, own[0] + own[1], other[0] + other[1])
+        for own, other in ((own_near, other_near), (own_far, other_far))
+    ]
+    ordered = [jnp.where(video == i, halves[0], halves[1]) for i in (0, 1)]
+    projected = jnp.concatenate(ordered, axis=1)
+    return (gate_scale[None, :] * projected).astype(jnp.bfloat16)
 
 
 def solution(mesh):
@@ -87,6 +148,11 @@
         P("head", "tm"),
         P(("groups", "head")),
     )
+    sizes = (mesh.shape["groups"], mesh.shape["tm"], mesh.shape["head"])
     return jax.shard_map(
-        shards, mesh=mesh, in_specs=placed, out_specs=P(("groups", "tm"), "head"), check_vma=False
+        square_mesh if sizes == (2, 4, 4) else any_mesh,
+        mesh=mesh,
+        in_specs=placed,
+        out_specs=P(("groups", "tm"), "head"),
+        check_vma=False,
     )

time: 251 us -> 202 us (0.80)
  waiting for transfers between devices: 198 us -> 124 us
  starting transfers between devices: 7.58 us -> 31.8 us
  between operations: 13.5 us -> 0.29 us
  other arithmetic: 11.9 us -> 20.7 us
  local copies, waits for them, and re-layouts: 6.77 us -> 10.7 us
    ppermute x0 -> x14, waiting for transfers between devices: none -> 87.2 us  [the longest x10 75.4 us: swapped(): return lax.ppermute(array, axis, [(i, i ^ mask) for i in range(count)])]
    all_gather x1 -> x0, waiting for transfers between devices: 67.2 us -> none  [shards(): lax.all_gather(out_weight, 'tm', axis=1, tiled=True)]
    ppermute x4, waiting for transfers between devices: 88 us -> 37.3 us  [passed_along(): lax.ppermute(array, axis, [(i, (i + by) % count) for i in range(count)])]
    reduce_scatter x1 -> x0, waiting for transfers between devices: 42.1 us -> none  [shards(): lax.psum_scatter(partial_value.astype(jnp.bfloat16), 'head', scatter_dime...]
    ppermute x0 -> x14, starting transfers between devices: none -> 24.4 us  [the longest x4 12.2 us: summed_pair(): lax.ppermute(total.astype(jnp.bfloat16), ('tm', 'head'), pairs)]
    select_n x0 -> x2, other arithmetic: none -> 3.6 us  [square_mesh(): ordered = [jnp.where(video == i, halves[0], halves[1]) for i in (0, 1)]]
    convert_element_type x1 -> x5, other arithmetic: 2.31 us -> 4.93 us  [the longest x4 3.87 us: summed_pair(): total.astype(jnp.bfloat16)]
    concatenate x2, other arithmetic: 2.54 us -> 5.07 us  [joined(): jnp.concatenate([slab[which] for slab in ordered], axis=0)]
  transfers between devices with their start and end apart: 6 -> 18, of which waited for: 6 -> 12; matrix products, arithmetic and copies ran while one was open for 8% -> 20% of each run, Pallas kernels for 0% -> 0%
where the time goes in v1:
time: 202 us; the launch traced here: 201 us
  waiting for transfers between devices  124 us (61%)
  starting transfers between devices  31.8 us (16%)
  other arithmetic  20.7 us (10%)
  matrix products  12.6 us (6%)
  local copies, waits for them, and re-layouts  10.7 us (5%)
    ppermute x10, waiting for transfers between devices, swapped(): return lax.ppermute(array, axis, [(i, i ^ mask) for i in range(count)])  75.4 us
    ppermute x4, waiting for transfers between devices, passed_along(): lax.ppermute(array, axis, [(i, (i + by) % count) for i in range(count)])  37.3 us
    ppermute x4, starting transfers between devices, summed_pair(): lax.ppermute(total.astype(jnp.bfloat16), ('tm', 'head'), pairs)  12.2 us
    ppermute x10, starting transfers between devices, swapped(): return lax.ppermute(array, axis, [(i, i ^ mask) for i in range(count)])  12.1 us
    ppermute x4, waiting for transfers between devices, summed_pair(): lax.ppermute(total.astype(jnp.bfloat16), ('tm', 'head'), pairs)  11.8 us
    dot_general x8, matrix products, term(): jnp.dot(attended, weight, preferred_element_type=jnp.float32)  8.66 us
    ppermute x4, starting transfers between devices, passed_along(): lax.ppermute(array, axis, [(i, (i + by) % count) for i in range(count)])  7.47 us
    concatenate x2, other arithmetic, joined(): jnp.concatenate([slab[which] for slab in ordered], axis=0)  5.07 us
  transfers between devices with their start and end apart: 18, of which 12 were waited for; matrix products, arithmetic and copies ran while one was open for 20% of the time, Pallas kernels for 0%

profile of v1, /device:TPU:1, one launch (start us, length us, event | category | flops | bytes accessed | tf_op | source)
XLA Modules:
  0.0 200.6 jit_solution(7908807906663864996)
XLA Ops:
  0.0 2.1 %collective-permute-start = (bf16[384,6,128]{2,0,1:T(8,128)(2,1)}, bf16[384,6,128]{2,0,1:T(8,128)(2,1)S(1)}, u32[]{:S(2)}, u32[]{:S(2)}) collective-permute-start(bf16[384,6,128]{2,0,1:T(8,128)(2,1)} %param.10), channel_id=1, source_target_pairs={{0,4},{4,8},{8,12},{12,0},{1,5},{5,9},{9,13},{13,1},{2,6},{6,10},{... | collective-permute-start | bytes 1769480 | tf_op jit(solution)/shard_map/ppermute | solution.py:15
  2.1 2.1 %collective-permute-start.1 = (bf16[384,6,128]{2,0,1:T(8,128)(2,1)}, bf16[384,6,128]{2,0,1:T(8,128)(2,1)}, u32[]{:S(2)}, u32[]{:S(2)}) collective-permute-start(bf16[384,6,128]{2,0,1:T(8,128)(2,1)} %param.10), channel_id=1, source_target_pairs={{0,12},{4,0},{8,4},{12,8},{1,13},{5,1},{9,5},{13,9},{2,14},{6,2},{... | collective-permute-start | bytes 1769480 | tf_op jit(solution)/shard_map/ppermute | solution.py:15
  4.2 3.3 %collective-permute-start.3 = (bf16[384,6,128]{2,0,1:T(8,128)(2,1)}, bf16[384,6,128]{2,0,1:T(8,128)(2,1)}, u32[]{:S(2)}, u32[]{:S(2)}) collective-permute-start(bf16[384,6,128]{2,0,1:T(8,128)(2,1)} %param.9), channel_id=1, source_target_pairs={{0,12},{4,0},{8,4},{12,8},{1,13},{5,1},{9,5},{13,9},{2,14},{6,2},{... | collective-permute-start | bytes 1769480 | tf_op jit(solution)/shard_map/ppermute | solution.py:15
  10.4 7.1 %collective-permute-done = bf16[384,6,128]{2,0,1:T(8,128)(2,1)S(1)} collective-permute-done((bf16[384,6,128]{2,0,1:T(8,128)(2,1)}, bf16[384,6,128]{2,0,1:T(8,128)(2,1)S(1)}, u32[]{:S(2)}, u32[]{:S(2)}) %collective-permute-start) | collective-permute-done | bytes 589856 | tf_op jit(solution)/shard_map/ppermute | solution.py:15
  17.7 12.1 %collective-permute-done.1 = bf16[384,6,128]{2,0,1:T(8,128)(2,1)} collective-permute-done((bf16[384,6,128]{2,0,1:T(8,128)(2,1)}, bf16[384,6,128]{2,0,1:T(8,128)(2,1)}, u32[]{:S(2)}, u32[]{:S(2)}) %collective-permute-start.1) | collective-permute-done | bytes 589856 | tf_op jit(solution)/shard_map/ppermute | solution.py:15
  29.7 2.6 %pad_maximum_fusion = bf16[1152,6,128]{2,0,1:T(8,128)(2,1)} fusion(bf16[384,6,128]{2,0,1:T(8,128)(2,1)} %collective-permute-done.1, bf16[384,6,128]{2,0,1:T(8,128)(2,1)} %param.10, bf16[384,6,128]{2,0,1:T(8,128)(2,1)S(1)} %collective-permute-done), kind=kLoop, calls=%fused_computation.17 | loop fusion | flops 5308416 | bytes 3538944 | tf_op jit(solution)/shard_map/concatenate | solution.py:70
  32.3 4.6 %gather_fusion = bf16[18,128,6,128]{3,1,2,0:T(8,128)(2,1)} fusion(bf16[9,128,6,128]{3,1,0,2:T(8,128)(2,1)} %bitcast.67, s32[1024]{0:T(1024)S(1)} %pad_clamp_fusion), kind=kCustom, calls=%fused_computation.clone | custom fusion | bytes 7077960 | tf_op jit(solution)/shard_map/jit(_take)/gather | solution.py:37
  36.9 5.9 %collective-permute-done.2 = bf16[384,6,128]{2,0,1:T(8,128)(2,1)S(1)} collective-permute-done((bf16[384,6,128]{2,0,1:T(8,128)(2,1)}, bf16[384,6,128]{2,0,1:T(8,128)(2,1)S(1)}, u32[]{:S(2)}, u32[]{:S(2)}) %collective-permute-start.2) | collective-permute-done | bytes 589856 | tf_op jit(solution)/shard_map/ppermute | solution.py:15
  42.8 12.2 %collective-permute-done.3 = bf16[384,6,128]{2,0,1:T(8,128)(2,1)} collective-permute-done((bf16[384,6,128]{2,0,1:T(8,128)(2,1)}, bf16[384,6,128]{2,0,1:T(8,128)(2,1)}, u32[]{:S(2)}, u32[]{:S(2)}) %collective-permute-start.3) | collective-permute-done | bytes 589856 | tf_op jit(solution)/shard_map/ppermute | solution.py:15
  55.0 2.5 %pad_maximum_fusion.1 = bf16[1152,6,128]{2,0,1:T(8,128)(2,1)} fusion(bf16[384,6,128]{2,0,1:T(8,128)(2,1)} %collective-permute-done.3, bf16[384,6,128]{2,0,1:T(8,128)(2,1)S(1)} %copy-done.10, bf16[384,6,128]{2,0,1:T(8,128)(2,1)S(1)} %collective-permute-done.2), kind=kLoop, calls=%fused_computation.18 | loop fusion | flops 5308416 | bytes 3538944 | tf_op jit(solution)/shard_map/concatenate | solution.py:70
  57.5 4.5 %gather_fusion.1 = bf16[18,128,6,128]{3,1,2,0:T(8,128)(2,1)} fusion(bf16[9,128,6,128]{3,1,0,2:T(8,128)(2,1)} %bitcast.66, s32[1024]{0:T(1024)S(1)} %pad_clamp_fusion), kind=kCustom, calls=%fused_computation.1.clone | custom fusion | bytes 7077960 | tf_op jit(solution)/shard_map/jit(_take)/gather | solution.py:36
  62.0 3.8 %broadcast_select_fusion.1 = (bf16[3,6,128,6,128]{4,2,3,1,0:T(8,128)(2,1)S(1)}, bf16[3,6,128,6,128]{4,2,3,1,0:T(8,128)(2,1)S(1)}) fusion(bf16[3,6,128,6,128]{4,2,3,1,0:T(8,128)(2,1)} %bitcast.68, pred[3,6]{1,0:T(4,128)(4,1)S(1)} %get-tuple-element.23, bf16[3,6,128,6,128]{4,2,3,1,0:T(8,128)(2,1)} %bitcast.69), kind=kLoop, calls=%fused_computation.13 | loop fusion | flops 3538944 | bytes 14155794 | tf_op jit(solution)/shard_map/jit(_take)/select_n | solution.py:37
  66.9 1.5 fusion.1
  68.4 2.9 %fusion.14 = bf16[3,128,6,128]{1,3,2,0:T(8,128)(2,1)S(1)} fusion(f32[3,6,6,128,128]{4,3,2,1,0:T(8,128)S(1)} %get-tuple-element.14, f32[3,6,128]{2,1,0:T(8,128)S(1)} %fusion.1, f32[3,6,128]{2,1,0:T(8,128)S(1)} %get-tuple-element.13, pred[3,6]{1,0:T(4,128)(4,1)S(1)} %get-tuple-element.24, bf16[3,6,128,6,128]{4,2,3,1,0:T(8,128)(2,1)S(1)} %get-tuple-element.11), kind=kOutput, calls=%fused_computation.29 | convolution fusion | flops 462127104 | bytes 11225106 | tf_op jit(solution)/shard_map/thqsk,tskhd->tqhd/dot_general | solution.py:52
  71.8 22.8 %collective-permute-done.7 = bf16[768,640]{1,0:T(8,128)(2,1)} collective-permute-done((bf16[768,640]{1,0:T(8,128)(2,1)}, bf16[768,640]{1,0:T(8,128)(2,1)}, u32[]{:S(2)}, u32[]{:S(2)}) %collective-permute-start.7) | collective-permute-done | bytes 983072 | tf_op jit(solution)/shard_map/ppermute | solution.py:20
  94.6 3.4 %collective-permute-start.8 = (bf16[768,640]{1,0:T(8,128)(2,1)}, bf16[768,640]{1,0:T(8,128)(2,1)S(1)}, u32[]{:S(2)}, u32[]{:S(2)}) collective-permute-start(bf16[768,640]{1,0:T(8,128)(2,1)} %collective-permute-done.7), channel_id=1, source_target_pairs={{0,4},{4,0},{8,12},{12,8},{1,5},{5,1},{9,13},{13,9},{2,6},{6,2},{1... | collective-permute-start | bytes 2949128 | tf_op jit(solution)/shard_map/ppermute | solution.py:20
  97.9 1.8 convolution_convert_fusion.7
  99.8 1.8 broadcast_select_fusion.9
  101.6 1.6 collective-permute-start.5
  105.4 1.9 convolution_convert_fusion.5
  107.3 11.8 %collective-permute-done.8 = bf16[768,640]{1,0:T(8,128)(2,1)S(1)} collective-permute-done((bf16[768,640]{1,0:T(8,128)(2,1)}, bf16[768,640]{1,0:T(8,128)(2,1)S(1)}, u32[]{:S(2)}, u32[]{:S(2)}) %collective-permute-start.8) | collective-permute-done | bytes 983072 | tf_op jit(solution)/shard_map/ppermute | solution.py:20
  120.7 1.5 collective-permute-start.6
  122.9 2.5 %collective-permute-start.9 = (bf16[384,640]{1,0:T(8,128)(2,1)S(1)}, bf16[384,640]{1,0:T(8,128)(2,1)S(1)}, u32[]{:S(2)}, u32[]{:S(2)}) collective-permute-start(bf16[384,640]{1,0:T(8,128)(2,1)S(1)} %get-tuple-element.19), channel_id=1, source_target_pairs={{0,1},{1,0},{2,3},{3,2},{4,5},{5,4},{6,7},{7,6},{8,9},{9,8},{10,11... | collective-permute-start | bytes 1474568 | tf_op jit(solution)/shard_map/ppermute | solution.py:20
  125.3 1.4 collective-permute-done.11
  127.4 1.4 collective-permute-start.12
  128.8 19.1 %collective-permute-done.14 = bf16[768,640]{1,0:T(8,128)(2,1)S(1)} collective-permute-done((bf16[768,640]{1,0:T(8,128)(2,1)}, bf16[768,640]{1,0:T(8,128)(2,1)S(1)}, u32[]{:S(2)}, u32[]{:S(2)}) %collective-permute-start.14) | collective-permute-done | bytes 983072 | tf_op jit(solution)/shard_map/ppermute | solution.py:20
  148.5 20.4 %collective-permute-done.15 = bf16[768,640]{1,0:T(8,128)(2,1)S(1)} collective-permute-done((bf16[768,640]{1,0:T(8,128)(2,1)S(1)}, bf16[768,640]{1,0:T(8,128)(2,1)S(1)}, u32[]{:S(2)}, u32[]{:S(2)}) %collective-permute-start.15) | collective-permute-done | bytes 983072 | tf_op jit(solution)/shard_map/ppermute | solution.py:20
  171.4 3.9 %collective-permute-start.10 = (bf16[384,640]{1,0:T(8,128)(2,1)}, bf16[384,640]{1,0:T(8,128)(2,1)}, u32[]{:S(2)}, u32[]{:S(2)}) collective-permute-start(bf16[384,640]{1,0:T(8,128)(2,1)} %fusion.19), channel_id=1, source_target_pairs={{0,2},{1,3},{4,6},{5,7},{10,8},{11,9},{14,12},{15,13},{16,18},{17,... | collective-permute-start | bytes 1474568 | tf_op jit(solution)/shard_map/ppermute | solution.py:126
  178.6 5.6 %collective-permute-start.17 = (bf16[384,640]{1,0:T(8,128)(2,1)}, bf16[384,640]{1,0:T(8,128)(2,1)}, u32[]{:S(2)}, u32[]{:S(2)}) collective-permute-start(bf16[384,640]{1,0:T(8,128)(2,1)} %fusion.21), channel_id=1, source_target_pairs={{0,2},{1,3},{4,6},{5,7},{10,8},{11,9},{14,12},{15,13},{16,18},{17,... | collective-permute-start | bytes 1474568 | tf_op jit(solution)/shard_map/ppermute | solution.py:126
  185.4 5.5 %collective-permute-done.13 = bf16[384,640]{1,0:T(8,128)(2,1)} collective-permute-done((bf16[384,640]{1,0:T(8,128)(2,1)}, bf16[384,640]{1,0:T(8,128)(2,1)}, u32[]{:S(2)}, u32[]{:S(2)}) %collective-permute-start.13) | collective-permute-done | bytes 491552 | tf_op jit(solution)/shard_map/ppermute | solution.py:126
  191.0 5.0 %collective-permute-done.17 = bf16[384,640]{1,0:T(8,128)(2,1)} collective-permute-done((bf16[384,640]{1,0:T(8,128)(2,1)}, bf16[384,640]{1,0:T(8,128)(2,1)}, u32[]{:S(2)}, u32[]{:S(2)}) %collective-permute-start.17) | collective-permute-done | bytes 491552 | tf_op jit(solution)/shard_map/ppermute | solution.py:126
  195.9 3.5 %broadcast_select_fusion.11 = (f32[384,640]{1,0:T(8,128)S(1)}, f32[384,640]{1,0:T(8,128)S(1)}, f32[384,640]{1,0:T(8,128)S(1)}) fusion(pred[]{:T(512)S(6)} %eq.28, bf16[384,640]{1,0:T(8,128)(2,1)} %collective-permute-done.17, bf16[384,640]{1,0:T(8,128)(2,1)} %copy-done.9, bf16[384,640]{1,0:T(8,128)(2,1)} %copy-done.4, bf16[384,640]{1,0:T(8,128)(2,1)} %copy-done.5, ...), kind=kLoop, calls=%fused_computation.59 | loop fusion | flops 6635520 | bytes 10813443 | tf_op jit(solution)/shard_map/jit(_where)/select_n | solution.py:137
  (64 shorter events, 18.6 us)
Async XLA Ops:
  0.0 7.5 %copy-start = (bf16[768,1280]{1,0:T(8,128)(2,1)S(1)}, bf16[768,1280]{1,0:T(8,128)(2,1)}, u32[]{:S(2)}) copy-start(bf16[768,1280]{1,0:T(8,128)(2,1)} %param.12) | copy-start | bytes 5898244
  0.0 17.5 %collective-permute-start = (bf16[384,6,128]{2,0,1:T(8,128)(2,1)}, bf16[384,6,128]{2,0,1:T(8,128)(2,1)S(1)}, u32[]{:S(2)}, u32[]{:S(2)}) collective-permute-start(bf16[384,6,128]{2,0,1:T(8,128)(2,1)} %param.10), channel_id=1, source_target_pairs={{0,4},{4,8},{8,12},{12,0},{1,5},{5,9},{9,13},{13,1},{2,6},{6,10},{... | collective-permute-start | bytes 1769480 | tf_op jit(solution)/shard_map/ppermute | solution.py:15
  2.1 27.6 %collective-permute-start.1 = (bf16[384,6,128]{2,0,1:T(8,128)(2,1)}, bf16[384,6,128]{2,0,1:T(8,128)(2,1)}, u32[]{:S(2)}, u32[]{:S(2)}) collective-permute-start(bf16[384,6,128]{2,0,1:T(8,128)(2,1)} %param.10), channel_id=1, source_target_pairs={{0,12},{4,0},{8,4},{12,8},{1,13},{5,1},{9,5},{13,9},{2,14},{6,2},{... | collective-permute-start | bytes 1769480 | tf_op jit(solution)/shard_map/ppermute | solution.py:15
  4.2 38.6 %collective-permute-start.2 = (bf16[384,6,128]{2,0,1:T(8,128)(2,1)}, bf16[384,6,128]{2,0,1:T(8,128)(2,1)S(1)}, u32[]{:S(2)}, u32[]{:S(2)}) collective-permute-start(bf16[384,6,128]{2,0,1:T(8,128)(2,1)} %param.9), channel_id=1, source_target_pairs={{0,4},{4,8},{8,12},{12,0},{1,5},{5,9},{9,13},{13,1},{2,6},{6,10},{... | collective-permute-start | bytes 1769480 | tf_op jit(solution)/shard_map/ppermute | solution.py:15
  4.2 50.8 %collective-permute-start.3 = (bf16[384,6,128]{2,0,1:T(8,128)(2,1)}, bf16[384,6,128]{2,0,1:T(8,128)(2,1)}, u32[]{:S(2)}, u32[]{:S(2)}) collective-permute-start(bf16[384,6,128]{2,0,1:T(8,128)(2,1)} %param.9), channel_id=1, source_target_pairs={{0,12},{4,0},{8,4},{12,8},{1,13},{5,1},{9,5},{13,9},{2,14},{6,2},{... | collective-permute-start | bytes 1769480 | tf_op jit(solution)/shard_map/ppermute | solution.py:15
  8.5 91.3 %collective-permute-start.4 = (bf16[768,640]{1,0:T(8,128)(2,1)}, bf16[768,640]{1,0:T(8,128)(2,1)}, u32[]{:S(2)}, u32[]{:S(2)}) collective-permute-start(bf16[768,640]{1,0:T(8,128)(2,1)} %constant_dynamic-slice_fusion), channel_id=1, source_target_pairs={{0,4},{4,0},{8,12},{12,8},{1,5},{5,1},{9,13},{13,9},{2,6},{6,2},{1... | collective-permute-start | bytes 2949128 | tf_op jit(solution)/shard_map/ppermute | solution.py:20
  17.5 77.1 %collective-permute-start.7 = (bf16[768,640]{1,0:T(8,128)(2,1)}, bf16[768,640]{1,0:T(8,128)(2,1)}, u32[]{:S(2)}, u32[]{:S(2)}) collective-permute-start(bf16[768,640]{1,0:T(8,128)(2,1)} %constant_dynamic-slice_fusion), channel_id=1, source_target_pairs={{0,8},{4,12},{8,0},{12,4},{1,9},{5,13},{9,1},{13,5},{2,10},{6,14},... | collective-permute-start | bytes 2949128 | tf_op jit(solution)/shard_map/ppermute | solution.py:20
  32.3 22.7 %copy-start.10 = (bf16[384,6,128]{2,0,1:T(8,128)(2,1)S(1)}, bf16[384,6,128]{2,0,1:T(8,128)(2,1)}, u32[]{:S(2)}) copy-start(bf16[384,6,128]{2,0,1:T(8,128)(2,1)} %param.9) | copy-start | bytes 1769476
  62.0 3.8 %copy-start.12 = (bf16[384,6,128]{2,0,1:T(8,128)(2,1)S(1)}, bf16[384,6,128]{2,0,1:T(8,128)(2,1)}, u32[]{:S(2)}) copy-start(bf16[384,6,128]{2,0,1:T(8,128)(2,1)} %param.8) | copy-start | bytes 1769476
  94.6 24.4 %collective-permute-start.8 = (bf16[768,640]{1,0:T(8,128)(2,1)}, bf16[768,640]{1,0:T(8,128)(2,1)S(1)}, u32[]{:S(2)}, u32[]{:S(2)}) collective-permute-start(bf16[768,640]{1,0:T(8,128)(2,1)} %collective-permute-done.7), channel_id=1, source_target_pairs={{0,4},{4,0},{8,12},{12,8},{1,5},{5,1},{9,13},{13,9},{2,6},{6,2},{1... | collective-permute-start | bytes 2949128 | tf_op jit(solution)/shard_map/ppermute | solution.py:20
  101.6 18.1 %collective-permute-start.5 = (bf16[384,640]{1,0:T(8,128)(2,1)S(1)}, bf16[384,640]{1,0:T(8,128)(2,1)S(1)}, u32[]{:S(2)}, u32[]{:S(2)}) collective-permute-start(bf16[384,640]{1,0:T(8,128)(2,1)S(1)} %get-tuple-element.21), channel_id=1, source_target_pairs={{0,1},{1,0},{2,3},{3,2},{4,5},{5,4},{6,7},{7,6},{8,9},{9,8},{10,11... | collective-permute-start | bytes 1474568 | tf_op jit(solution)/shard_map/ppermute | solution.py:20
  103.2 23.5 %collective-permute-start.11 = (bf16[768,640]{1,0:T(8,128)(2,1)}, bf16[768,640]{1,0:T(8,128)(2,1)S(1)}, u32[]{:S(2)}, u32[]{:S(2)}) collective-permute-start(bf16[768,640]{1,0:T(8,128)(2,1)} %collective-permute-done.4), channel_id=1, source_target_pairs={{0,16},{16,0},{1,17},{17,1},{2,18},{18,2},{3,19},{19,3},{4,20},{20... | collective-permute-start | bytes 2949128 | tf_op jit(solution)/shard_map/ppermute | solution.py:20
  105.1 42.7 %collective-permute-start.14 = (bf16[768,640]{1,0:T(8,128)(2,1)}, bf16[768,640]{1,0:T(8,128)(2,1)S(1)}, u32[]{:S(2)}, u32[]{:S(2)}) collective-permute-start(bf16[768,640]{1,0:T(8,128)(2,1)} %collective-permute-done.7), channel_id=1, source_target_pairs={{0,16},{16,0},{1,17},{17,1},{2,18},{18,2},{3,19},{19,3},{4,20},{20... | collective-permute-start | bytes 2949128 | tf_op jit(solution)/shard_map/ppermute | solution.py:20
  107.2 63.2 %copy-start.1 = (bf16[384,640]{1,0:T(8,128)(2,1)}, bf16[384,640]{1,0:T(8,128)(2,1)S(1)}, u32[]{:S(2)}) copy-start(bf16[384,640]{1,0:T(8,128)(2,1)S(1)} %convolution_convert_fusion.5) | copy-start | bytes 1474564
  119.0 49.9 %collective-permute-start.15 = (bf16[768,640]{1,0:T(8,128)(2,1)S(1)}, bf16[768,640]{1,0:T(8,128)(2,1)S(1)}, u32[]{:S(2)}, u32[]{:S(2)}) collective-permute-start(bf16[768,640]{1,0:T(8,128)(2,1)S(1)} %collective-permute-done.8), channel_id=1, source_target_pairs={{0,16},{16,0},{1,17},{17,1},{2,18},{18,2},{3,19},{19,3},{4,20},{20... | collective-permute-start | bytes 2949128 | tf_op jit(solution)/shard_map/ppermute | solution.py:20
  119.7 1.0 copy-start.6
  120.7 63.5 %collective-permute-start.6 = (bf16[384,640]{1,0:T(8,128)(2,1)}, bf16[384,640]{1,0:T(8,128)(2,1)}, u32[]{:S(2)}, u32[]{:S(2)}) collective-permute-start(bf16[384,640]{1,0:T(8,128)(2,1)} %fusion.18), channel_id=1, source_target_pairs={{2,0},{3,1},{6,4},{7,5},{8,10},{9,11},{12,14},{13,15},{18,16},{19,... | collective-permute-start | bytes 1474568 | tf_op jit(solution)/shard_map/ppermute | solution.py:126
  122.8 47.6 %copy-start.2 = (bf16[384,640]{1,0:T(8,128)(2,1)}, bf16[384,640]{1,0:T(8,128)(2,1)S(1)}, u32[]{:S(2)}) copy-start(bf16[384,640]{1,0:T(8,128)(2,1)S(1)} %get-tuple-element.20) | copy-start | bytes 1474564
  122.9 47.6 %collective-permute-start.9 = (bf16[384,640]{1,0:T(8,128)(2,1)S(1)}, bf16[384,640]{1,0:T(8,128)(2,1)S(1)}, u32[]{:S(2)}, u32[]{:S(2)}) collective-permute-start(bf16[384,640]{1,0:T(8,128)(2,1)S(1)} %get-tuple-element.19), channel_id=1, source_target_pairs={{0,1},{1,0},{2,3},{3,2},{4,5},{5,4},{6,7},{7,6},{8,9},{9,8},{10,11... | collective-permute-start | bytes 1474568 | tf_op jit(solution)/shard_map/ppermute | solution.py:20
  127.4 48.0 %copy-start.3 = (bf16[384,640]{1,0:T(8,128)(2,1)}, bf16[384,640]{1,0:T(8,128)(2,1)S(1)}, u32[]{:S(2)}) copy-start(bf16[384,640]{1,0:T(8,128)(2,1)S(1)} %get-tuple-element.18) | copy-start | bytes 1474564
  127.4 47.9 %collective-permute-start.12 = (bf16[384,640]{1,0:T(8,128)(2,1)S(1)}, bf16[384,640]{1,0:T(8,128)(2,1)S(1)}, u32[]{:S(2)}, u32[]{:S(2)}) collective-permute-start(bf16[384,640]{1,0:T(8,128)(2,1)S(1)} %get-tuple-element.17), channel_id=1, source_target_pairs={{0,1},{1,0},{2,3},{3,2},{4,5},{5,4},{6,7},{7,6},{8,9},{9,8},{10,11... | collective-permute-start | bytes 1474568 | tf_op jit(solution)/shard_map/ppermute | solution.py:20
  148.4 30.1 %copy-start.4 = (bf16[384,640]{1,0:T(8,128)(2,1)}, bf16[384,640]{1,0:T(8,128)(2,1)S(1)}, u32[]{:S(2)}) copy-start(bf16[384,640]{1,0:T(8,128)(2,1)S(1)} %convolution_convert_fusion.1) | copy-start | bytes 1474564
  169.5 8.1 %copy-start.5 = (bf16[384,640]{1,0:T(8,128)(2,1)}, bf16[384,640]{1,0:T(8,128)(2,1)S(1)}, u32[]{:S(2)}) copy-start(bf16[384,640]{1,0:T(8,128)(2,1)S(1)} %get-tuple-element.16) | copy-start | bytes 1474564
  169.5 8.1 %collective-permute-start.16 = (bf16[384,640]{1,0:T(8,128)(2,1)S(1)}, bf16[384,640]{1,0:T(8,128)(2,1)S(1)}, u32[]{:S(2)}, u32[]{:S(2)}) collective-permute-start(bf16[384,640]{1,0:T(8,128)(2,1)S(1)} %get-tuple-element.15), channel_id=1, source_target_pairs={{0,1},{1,0},{2,3},{3,2},{4,5},{5,4},{6,7},{7,6},{8,9},{9,8},{10,11... | collective-permute-start | bytes 1474568 | tf_op jit(solution)/shard_map/ppermute | solution.py:20
  170.4 8.1 %copy-start.7 = (bf16[384,640]{1,0:T(8,128)(2,1)}, bf16[384,640]{1,0:T(8,128)(2,1)S(1)}, u32[]{:S(2)}) copy-start(bf16[384,640]{1,0:T(8,128)(2,1)S(1)} %collective-permute-done.9) | copy-start | bytes 1474564
  171.4 14.0 %collective-permute-start.10 = (bf16[384,640]{1,0:T(8,128)(2,1)}, bf16[384,640]{1,0:T(8,128)(2,1)}, u32[]{:S(2)}, u32[]{:S(2)}) collective-permute-start(bf16[384,640]{1,0:T(8,128)(2,1)} %fusion.19), channel_id=1, source_target_pairs={{0,2},{1,3},{4,6},{5,7},{10,8},{11,9},{14,12},{15,13},{16,18},{17,... | collective-permute-start | bytes 1474568 | tf_op jit(solution)/shard_map/ppermute | solution.py:126
  175.3 3.3 %copy-start.8 = (bf16[384,640]{1,0:T(8,128)(2,1)}, bf16[384,640]{1,0:T(8,128)(2,1)S(1)}, u32[]{:S(2)}) copy-start(bf16[384,640]{1,0:T(8,128)(2,1)S(1)} %collective-permute-done.12) | copy-start | bytes 1474564
  176.3 14.7 %collective-permute-start.13 = (bf16[384,640]{1,0:T(8,128)(2,1)}, bf16[384,640]{1,0:T(8,128)(2,1)}, u32[]{:S(2)}, u32[]{:S(2)}) collective-permute-start(bf16[384,640]{1,0:T(8,128)(2,1)} %fusion.20), channel_id=1, source_target_pairs={{2,0},{3,1},{6,4},{7,5},{8,10},{9,11},{12,14},{13,15},{18,16},{19,... | collective-permute-start | bytes 1474568 | tf_op jit(solution)/shard_map/ppermute | solution.py:126
  177.6 1.0 copy-start.9
  178.6 17.4 %collective-permute-start.17 = (bf16[384,640]{1,0:T(8,128)(2,1)}, bf16[384,640]{1,0:T(8,128)(2,1)}, u32[]{:S(2)}, u32[]{:S(2)}) collective-permute-start(bf16[384,640]{1,0:T(8,128)(2,1)} %fusion.21), channel_id=1, source_target_pairs={{0,2},{1,3},{4,6},{5,7},{10,8},{11,9},{14,12},{15,13},{16,18},{17,... | collective-permute-start | bytes 1474568 | tf_op jit(solution)/shard_map/ppermute | solution.py:126
  184.2 15.4 %copy-start.11 = (f32[1280]{0:T(1024)S(1)}, f32[1280]{0:T(1024)}, u32[]{:S(2)}) copy-start(f32[1280]{0:T(1024)} %param.13) | copy-start | bytes 15364

commit v2 on v1

v2 whole, which is shorter than its diff:
```python
import functools
import math

import jax
import jax.numpy as jnp
from jax import lax
from jax.experimental import pallas as pl
from jax.experimental.pallas import tpu as pltpu
from jax.sharding import PartitionSpec as P

TILE = 128
CUT = 256


def passed_along(array, axis, by):
    count = lax.axis_size(axis)
    return lax.ppermute(array, axis, [(i, (i + by) % count) for i in range(count)])


def swapped(array, axis, mask):
    count = lax.axis_size(axis)
    return lax.ppermute(array, axis, [(i, i ^ mask) for i in range(count)])


def attend_kernel(reach, score_scale, keep_ref, queries_ref, *refs):
    key_refs, value_refs, out_ref = refs[: 2 * reach + 1], refs[2 * reach + 1 : -1], refs[-1]
    tiles = queries_ref.shape[1] // TILE
    scale = score_scale * math.log2(math.e)
    for tile in range(tiles):
        query_tile = queries_ref[0, tile * TILE : (tile + 1) * TILE]
        scores = []
        for slab, key_ref in enumerate(key_refs):
            raw = lax.dot_general(
                query_tile, key_ref[0], (((1,), (1,)), ((), ())), preferred_element_type=jnp.float32
            )
            keep = keep_ref[tile : tile + 1, slab * tiles * TILE : (slab + 1) * tiles * TILE]
            scores.append(jnp.where(keep > 0, raw, -jnp.inf))
        peak = scores[0].max(axis=1, keepdims=True)
        for block in scores[1:]:
            peak = jnp.maximum(peak, block.max(axis=1, keepdims=True))
        total, out = 0.0, 0.0
        for block, value_ref in zip(scores, value_refs):
            weights = jnp.exp2((block - peak) * scale)
            total = total + weights.sum(axis=1, keepdims=True)
            out = out + jnp.dot(
                weights.astype(jnp.bfloat16), value_ref[0], preferred_element_type=jnp.float32
            )
        out_ref[tile * TILE : (tile + 1) * TILE] = (out / total).astype(out_ref.dtype)


def attend(queries, key_slabs, value_slabs, keep_tiles):
    rows, head_count, depth = queries.shape
    by_head = [rows_of.transpose(1, 0, 2) for rows_of in (queries, *key_slabs, *value_slabs)]
    keep = jnp.repeat(keep_tiles.astype(jnp.float32), TILE, axis=1)
    block = pl.BlockSpec((1, rows, depth), lambda head: (head, 0, 0))
    return pl.pallas_call(
        functools.partial(attend_kernel, len(key_slabs) // 2, 1.0 / math.sqrt(depth)),
        grid=(head_count,),
        out_shape=jax.ShapeDtypeStruct((rows, head_count * depth), jnp.bfloat16),
        in_specs=[pl.BlockSpec(keep.shape, lambda head: (0, 0))] + [block] * len(by_head),
        out_specs=pl.BlockSpec((rows, depth), lambda head: (0, head)),
        compiler_params=pltpu.CompilerParams(vmem_limit_bytes=32 * 2**20),
        cost_estimate=pl.CostEstimate(flops=2 * 10**10, bytes_accessed=10**7, transcendentals=0),
        name="attend",
    )(keep, *by_head)


def halo(key_rows, value_rows):
    reach_slabs = min(2, (lax.axis_size("tm") - 1) // 2)
    lower_list = []
    upper_list = []
    for distance in range(1, reach_slabs + 1):
        lower_list.append([passed_along(rows, "tm", distance) for rows in (key_rows, value_rows)])
        upper_list.append([passed_along(rows, "tm", -distance) for rows in (key_rows, value_rows)])
    return lower_list[::-1], upper_list


def all_slabs(lower, own, upper):
    ordered = lower + [own] + upper
    return [[slab[which] for slab in ordered] for which in (0, 1)]


def any_mesh(queries, key_rows, value_rows, keep_tiles, out_weight, gate_scale):
    lower, upper = halo(key_rows, value_rows)
    key_slabs, value_slabs = all_slabs(lower, (key_rows, value_rows), upper)
    attended = attend(queries, key_slabs, value_slabs, keep_tiles)
    partial_value = jnp.dot(
        attended,
        lax.all_gather(out_weight, "tm", axis=1, tiled=True),
        preferred_element_type=jnp.float32,
    )
    summed = lax.psum_scatter(
        partial_value.astype(jnp.bfloat16), "head", scatter_dimension=1, tiled=True
    ).astype(jnp.float32)
    return (gate_scale[None, :] * summed).astype(jnp.bfloat16)


def after(array, *others):
    return lax.optimization_barrier((array, *others))[0]


def f32(array):
    return array.astype(jnp.float32)


SMEM = pl.BlockSpec(memory_space=pltpu.SMEM)
WHOLE = pl.BlockSpec(memory_space=pltpu.VMEM)
LATER = pl.BlockSpec(memory_space=pl.ANY)


def local_call(kernel, outs, flags, arrays, earlier, name, flops=0):
    def body(*refs):
        count = len(flags) + len(arrays)
        kernel(*refs[:count], *refs[count + len(earlier) :])

    moved = sum(array.size * array.dtype.itemsize for array in (*arrays, *outs))
    return pl.pallas_call(
        body,
        out_shape=outs,
        in_specs=[SMEM] * len(flags) + [WHOLE] * len(arrays) + [LATER] * len(earlier),
        out_specs=[WHOLE] * len(outs),
        compiler_params=pltpu.CompilerParams(vmem_limit_bytes=40 * 2**20),
        cost_estimate=pl.CostEstimate(flops=flops, bytes_accessed=moved, transcendentals=0),
        name=name,
    )(*[jnp.int32(flag).reshape(1) for flag in flags], *arrays, *earlier)


def terms(mine, other, blocks, earlier=()):
    rows, depth = mine.shape
    width = sum(part.shape[1] for part in blocks[0])
    weights = [part for block in blocks for part in block]

    def kernel(mine_ref, other_ref, *refs):
        weight_refs, out_ref = list(refs[:-1]), refs[-1]
        for index, block in enumerate(blocks):
            column = 0
            for part in block:
                weight_ref = weight_refs.pop(0)
                columns = slice(column, column + part.shape[1])
                for video, rows_ref in enumerate((mine_ref, other_ref)):
                    out_ref[index, video, :, columns] = jnp.dot(
                        rows_ref[...], weight_ref[...], preferred_element_type=jnp.float32
                    ).astype(out_ref.dtype)
                column += part.shape[1]

    out = jax.ShapeDtypeStruct((len(blocks), 2, rows, width), jnp.bfloat16)
    flops = 4 * rows * depth * width * len(blocks) * 100
    return local_call(kernel, [out], (), (mine, other, *weights), earlier, "terms", flops)[0]


def add_cores(pair, arrived, first, earlier=()):
    def kernel(first_ref, pair_ref, arrived_ref, kept_ref, given_ref):
        for index, out_ref in ((1 - first_ref[0], kept_ref), (first_ref[0], given_ref)):
            total = f32(pair_ref[index]) + f32(arrived_ref[index])
            out_ref[...] = total.astype(out_ref.dtype)

    outs = [jax.ShapeDtypeStruct(pair.shape[1:], kind) for kind in (jnp.float32, jnp.bfloat16)]
    return local_call(kernel, outs, (first,), (pair, arrived), earlier, "add_cores")


def add_chips(kept, arrived, earlier=()):
    def kernel(kept_ref, arrived_ref, near_ref, far_ref):
        near_ref[...] = kept_ref[0] + f32(arrived_ref[0])
        far_ref[...] = (kept_ref[1] + f32(arrived_ref[1])).astype(far_ref.dtype)

    outs = [jax.ShapeDtypeStruct(kept.shape[1:], kind) for kind in (jnp.float32, jnp.bfloat16)]
    return local_call(kernel, outs, (), (kept, arrived), earlier, "add_chips")


def gated(gate_scale, units, which, video):
    rows = units[0][0][0].shape[0]
    width = sum(near.shape[1] for near, _ in units[0])
    counts = [len(unit) for unit in units]

    def kernel(which_ref, video_ref, gate_ref, *refs):
        part_refs, out_ref = list(refs[:-1]), refs[-1]
        for unit, count in enumerate(counts):
            own = [(part_refs.pop(0), part_refs.pop(0)) for _ in range(count)]
            for place in (0, 1):

                @pl.when((which_ref[0] == unit) & (video_ref[0] == place))
                def _():
                    column = 0
                    for pair in own:
                        for side, part_ref in enumerate(pair):
                            start = (side ^ place) * width + column
                            columns = slice(start, start + part_ref.shape[1])
                            out_ref[:, columns] = (
                                gate_ref[:, columns] * f32(part_ref[...])
                            ).astype(out_ref.dtype)
                        column += pair[0].shape[1]

    parts = [array for unit in units for pair in unit for array in pair]
    out = jax.ShapeDtypeStruct((rows, 2 * width), jnp.bfloat16)
    arrays = (gate_scale.reshape(1, -1), *parts)
    return local_call(kernel, [out], (which, video), arrays, (), "gated")[0]


def square_mesh(queries, key_rows, value_rows, keep_tiles, out_weight, gate_scale):
    video = lax.axis_index("groups")
    slab = lax.axis_index("tm")
    head = lax.axis_index("head")
    width = out_weight.shape[1] // 2
    cut = width - CUT

    lower, upper = halo(key_rows, value_rows)
    block_0 = [
        lax.dynamic_slice_in_dim(out_weight, video * width + start, size, 1)
        for start, size in ((0, cut), (cut, width - cut))
    ]
    early, late = lax.optimization_barrier((*block_0, lower, upper))[:2]
    block_2 = [swapped(early, "tm", 2)]
    block_1 = [swapped(early, "tm", 1)]

    key_slabs, value_slabs = all_slabs(lower, (key_rows, value_rows), upper)
    mine = attend(queries, key_slabs, value_slabs, keep_tiles)
    mine, late, block_2[0], block_1[0] = lax.optimization_barrier(
        (mine, late, block_2[0], block_1[0])
    )
    other = swapped(mine, "groups", 1)
    block_2.append(swapped(late, "tm", 2))
    block_1.append(swapped(late, "tm", 1))
    block_3 = [swapped(block, "tm", 1) for block in block_2]

    places = [(g, t, h) for g in range(2) for t in range(4) for h in range(4)]
    same_side = slab // 2 == head // 2

    def sent(array, group_mask, head_mask, flip):
        pairs = [
            (16 * g + 4 * t + h, 16 * (g ^ group_mask) + 4 * t + (h ^ head_mask))
            for g, t, h in places
            if (t % 2 == h % 2) != flip
        ]
        return lax.ppermute(array, ("groups", "tm", "head"), pairs)

    terms_1 = terms(mine, other, [block_0, block_2], [block_3[0]])
    kept_1, given_1 = add_cores(terms_1, sent(terms_1, 0, 1, True), same_side)
    across_1 = sent(given_1, 0, 2, False)
    terms_2 = terms(mine, other, [[block_1[0]], [block_3[0]]], [])
    near_1, far_1 = add_chips(kept_1, across_1)
    kept_2, given_2 = add_cores(terms_2, sent(terms_2, 0, 1, False), same_side)
    across_2 = sent(given_2, 0, 2, True)
    terms_3 = terms(mine, other, [[block_1[1]], [block_3[1]]], [])
    far_1 = sent(far_1, 1, 0, False)
    kept_3, given_3 = add_cores(terms_3, sent(terms_3, 0, 1, False), same_side, [far_1])
    across_3 = sent(given_3, 0, 2, True)
    near_2, far_2 = add_chips(kept_2, across_2)
    near_3, far_3 = add_chips(kept_3, across_3, [far_1, far_2])
    far_2 = sent(far_2, 1, 0, True)
    far_3 = sent(far_3, 1, 0, True)
    units = [[(near_1, far_1)], [(near_2, far_2), (near_3, far_3)]]
    return gated(gate_scale, units, (slab ^ head) & 1, video)


def solution(mesh):
    placed = (
        P(("groups", "tm"), "head", None),
        P(("groups", "tm"), "head", None),
        P(("groups", "tm"), "head", None),
        P(("groups", "tm"), None),
        P("head", "tm"),
        P(("groups", "head")),
    )
    sizes = (mesh.shape["groups"], mesh.shape["tm"], mesh.shape["head"])
    return jax.shard_map(
        square_mesh if sizes == (2, 4, 4) else any_mesh,
        mesh=mesh,
        in_specs=placed,
        out_specs=P(("groups", "tm"), "head"),
        check_vma=False,
    )
```

time: 202 us -> 170 us (0.84)
  the two profiles are of different devices: /device:TPU:1 before, /device:TPU:0 now
where the time goes in v2:
time: 170 us
  waiting for transfers between devices  107 us (63%)
  starting transfers between devices  34.2 us (20%)
  Pallas kernels  23.1 us (14%)
  local copies, waits for them, and re-layouts  4.6 us (3%)
    ppermute x4, waiting for transfers between devices, passed_along(): lax.ppermute(array, axis, [(i, (i + by) % count) for i in range(count)])  45.5 us
    ppermute x7, waiting for transfers between devices, swapped(): return lax.ppermute(array, axis, [(i, i ^ mask) for i in range(count)])  34.6 us
    ppermute x9, waiting for transfers between devices, sent(): return lax.ppermute(array, ('groups', 'tm', 'head'), pairs)  26.9 us
    ppermute x9, starting transfers between devices, sent(): return lax.ppermute(array, ('groups', 'tm', 'head'), pairs)  15.9 us
    pallas_call x10, Pallas kernels, local_call(): pl.pallas_call(body, out_shape=outs, in_specs=[SMEM] * len(flags) + [WHOL...  12.9 us
    pallas_call x1, Pallas kernels, attend(): pl.pallas_call(functools.partial(attend_kernel, len(key_slabs) // 2, 1.0...  10.2 us
    ppermute x7, starting transfers between devices, swapped(): return lax.ppermute(array, axis, [(i, i ^ mask) for i in range(count)])  9.36 us
    ppermute x4, starting transfers between devices, passed_along(): lax.ppermute(array, axis, [(i, (i + by) % count) for i in range(count)])  8.94 us
  transfers between devices with their start and end apart: 20, of which 9 were waited for; matrix products, arithmetic and copies ran while one was open for 1% of the time, Pallas kernels for 12%

profile of v2, /device:TPU:0, one launch (start us, length us, event | category | flops | bytes accessed | tf_op | source)
XLA Modules:
  0.0 169.9 jit_solution(10397528021095191410)
XLA Ops:
  0.0 3.0 %collective-permute-start = (bf16[384,6,128]{2,0,1:T(8,128)(2,1)}, bf16[384,6,128]{2,0,1:T(8,128)(2,1)}, u32[]{:S(2)}, u32[]{:S(2)}) collective-permute-start(bf16[384,6,128]{2,0,1:T(8,128)(2,1)} %param.7), channel_id=1, source_target_pairs={{0,4},{4,8},{8,12},{12,0},{1,5},{5,9},{9,13},{13,1},{2,6},{6,10},{... | collective-permute-start | bytes 1769480 | tf_op jit(solution)/shard_map/ppermute | solution.py:17
  3.0 2.1 %collective-permute-start.1 = (bf16[384,6,128]{2,0,1:T(8,128)(2,1)}, bf16[384,6,128]{2,0,1:T(8,128)(2,1)}, u32[]{:S(2)}, u32[]{:S(2)}) collective-permute-start(bf16[384,6,128]{2,0,1:T(8,128)(2,1)} %param.7), channel_id=1, source_target_pairs={{0,12},{4,0},{8,4},{12,8},{1,13},{5,1},{9,5},{13,9},{2,14},{6,2},{... | collective-permute-start | bytes 1769480 | tf_op jit(solution)/shard_map/ppermute | solution.py:17
  5.1 3.8 %collective-permute-start.3 = (bf16[384,6,128]{2,0,1:T(8,128)(2,1)}, bf16[384,6,128]{2,0,1:T(8,128)(2,1)}, u32[]{:S(2)}, u32[]{:S(2)}) collective-permute-start(bf16[384,6,128]{2,0,1:T(8,128)(2,1)} %param.8), channel_id=1, source_target_pairs={{0,12},{4,0},{8,4},{12,8},{1,13},{5,1},{9,5},{13,9},{2,14},{6,2},{... | collective-permute-start | bytes 1769480 | tf_op jit(solution)/shard_map/ppermute | solution.py:17
  10.6 9.0 %collective-permute-done = bf16[384,6,128]{2,0,1:T(8,128)(2,1)} collective-permute-done((bf16[384,6,128]{2,0,1:T(8,128)(2,1)}, bf16[384,6,128]{2,0,1:T(8,128)(2,1)}, u32[]{:S(2)}, u32[]{:S(2)}) %collective-permute-start) | collective-permute-done | bytes 589856 | tf_op jit(solution)/shard_map/ppermute | solution.py:17
  19.6 12.8 %collective-permute-done.1 = bf16[384,6,128]{2,0,1:T(8,128)(2,1)} collective-permute-done((bf16[384,6,128]{2,0,1:T(8,128)(2,1)}, bf16[384,6,128]{2,0,1:T(8,128)(2,1)}, u32[]{:S(2)}, u32[]{:S(2)}) %collective-permute-start.1) | collective-permute-done | bytes 589856 | tf_op jit(solution)/shard_map/ppermute | solution.py:17
  32.4 12.5 %collective-permute-done.2 = bf16[384,6,128]{2,0,1:T(8,128)(2,1)} collective-permute-done((bf16[384,6,128]{2,0,1:T(8,128)(2,1)}, bf16[384,6,128]{2,0,1:T(8,128)(2,1)}, u32[]{:S(2)}, u32[]{:S(2)}) %collective-permute-start.2) | collective-permute-done | bytes 589856 | tf_op jit(solution)/shard_map/ppermute | solution.py:17
  44.9 11.2 %collective-permute-done.3 = bf16[384,6,128]{2,0,1:T(8,128)(2,1)} collective-permute-done((bf16[384,6,128]{2,0,1:T(8,128)(2,1)}, bf16[384,6,128]{2,0,1:T(8,128)(2,1)}, u32[]{:S(2)}, u32[]{:S(2)}) %collective-permute-start.3) | collective-permute-done | bytes 589856 | tf_op jit(solution)/shard_map/ppermute | solution.py:17
  56.1 1.1 collective-permute-start.5
  57.2 1.7 %collective-permute-start.4 = (bf16[768,384]{1,0:T(8,128)(2,1)S(1)}, bf16[768,384]{1,0:T(8,128)(2,1)}, u32[]{:S(2)}, u32[]{:S(2)}) collective-permute-start(bf16[768,384]{1,0:T(8,128)(2,1)S(1)} %constant_dynamic-slice_fusion.1.refs_2_), channel_id=1, source_target_pairs={{0,8},{4,12},{8,0},{12,4},{1,9},{5,13},{9,1},{13,5},{2,10},{6,14},... | collective-permute-start | bytes 1769480 | tf_op jit(solution)/shard_map/ppermute | solution.py:22
  58.9 10.2 %attend.1.refs_0_ = bf16[384,768]{1,0:T(8,128)(2,1)} custom-call(f32[3,1152]{1,0:T(4,128)S(1)} %bitcast.15, bf16[6,384,128]{2,1,0:T(8,128)(2,1)S(1)} %bitcast.16, bf16[6,384,128]{2,1,0:T(8,128)(2,1)} %bitcast.4.refs_0_, bf16[6,384,128]{2,1,0:T(8,128)(2,1)S(1)} %bitcast.17, bf16[6,384,128]{2,1,0:T(8,128)(2,1)} %bitcast.6.refs_2_, ...), custom_call_target="tpu_custom_call" | custom-call | flops 20000000000 | bytes 10000000 | tf_op jit(solution)/shard_map/attend/pallas_call | solution.py:56
  69.1 12.4 %collective-permute-done.5.refs_2_ = bf16[768,384]{1,0:T(8,128)(2,1)S(1)} collective-permute-done((bf16[768,384]{1,0:T(8,128)(2,1)S(1)}, bf16[768,384]{1,0:T(8,128)(2,1)S(1)}, u32[]{:S(2)}, u32[]{:S(2)}) %collective-permute-start.5) | collective-permute-done | bytes 589856 | tf_op jit(solution)/shard_map/ppermute | solution.py:22
  81.6 0.8 copy-done.8
  82.4 3.4 %collective-permute-done.4.refs_4_ = bf16[768,384]{1,0:T(8,128)(2,1)} collective-permute-done((bf16[768,384]{1,0:T(8,128)(2,1)S(1)}, bf16[768,384]{1,0:T(8,128)(2,1)}, u32[]{:S(2)}, u32[]{:S(2)}) %collective-permute-start.4) | collective-permute-done | bytes 589856 | tf_op jit(solution)/shard_map/ppermute | solution.py:22
  85.8 1.5 collective-permute-start.6
  88.0 1.7 collective-permute-start.15
  89.6 18.7 %collective-permute-done.7.refs_5_ = bf16[768,256]{1,0:T(8,128)(2,1)} collective-permute-done((bf16[768,256]{1,0:T(8,128)(2,1)}, bf16[768,256]{1,0:T(8,128)(2,1)}, u32[]{:S(2)}, u32[]{:S(2)}) %collective-permute-start.7) | collective-permute-done | bytes 393248 | tf_op jit(solution)/shard_map/ppermute | solution.py:22
  108.4 2.7 %collective-permute-start.16 = (bf16[768,256]{1,0:T(8,128)(2,1)}, bf16[768,256]{1,0:T(8,128)(2,1)}, u32[]{:S(2)}, u32[]{:S(2)}) collective-permute-start(bf16[768,256]{1,0:T(8,128)(2,1)} %collective-permute-done.7.refs_5_), channel_id=1, source_target_pairs={{0,4},{4,0},{8,12},{12,8},{1,5},{5,1},{9,13},{13,9},{2,6},{6,2},{1... | collective-permute-start | bytes 1179656 | tf_op jit(solution)/shard_map/ppermute | solution.py:22
  111.1 3.5 %terms.3.refs_1_ = bf16[2,2,384,640]{3,2,1,0:T(8,128)(2,1)S(1)} custom-call(bf16[384,768]{1,0:T(8,128)(2,1)} %attend.1.refs_0_, bf16[384,768]{1,0:T(8,128)(2,1)S(1)} %collective-permute-done.6.refs_1_, bf16[768,384]{1,0:T(8,128)(2,1)S(1)} %constant_dynamic-slice_fusion.1.refs_2_, bf16[768,256]{1,0:T(8,128)(2,1)} %constant_dynamic-slice_fusion.refs_3_, ...), custom_call_target="tpu_custom_call" | custom-call | flops 150994944000 | bytes 5111808 | tf_op jit(solution)/shard_map/terms/pallas_call | solution.py:117
  114.6 1.3 collective-permute-start.9
  115.9 2.6 %terms.4.refs_1_ = bf16[2,2,384,384]{3,2,1,0:T(8,128)(2,1)S(1)} custom-call(bf16[384,768]{1,0:T(8,128)(2,1)} %attend.1.refs_0_, bf16[384,768]{1,0:T(8,128)(2,1)S(1)} %collective-permute-done.6.refs_1_, bf16[768,384]{1,0:T(8,128)(2,1)S(1)} %copy-done.9, bf16[768,384]{1,0:T(8,128)(2,1)} %collective-permute-done.8.refs_6_.refs_3_), custom_call_target="tpu_custom_call" | custom-call | flops 90596966400 | bytes 3538944 | tf_op jit(solution)/shard_map/terms/pallas_call | solution.py:117
  118.6 3.2 %collective-permute-start.12 = (bf16[2,2,384,384]{3,2,1,0:T(8,128)(2,1)S(1)}, bf16[2,2,384,384]{3,2,1,0:T(8,128)(2,1)S(1)}, u32[]{:S(2)}, u32[]{:S(2)}) collective-permute-start(bf16[2,2,384,384]{3,2,1,0:T(8,128)(2,1)S(1)} %terms.4.refs_1_), channel_id=1, source_target_pairs={{0,1},{2,3},{5,4},{7,6},{8,9},{10,11},{13,12},{15,14},{16,17},{18,... | collective-permute-start | bytes 3538952 | tf_op jit(solution)/shard_map/ppermute | solution.py:234
  122.2 3.4 %collective-permute-start.10 = (bf16[2,384,640]{2,1,0:T(8,128)(2,1)S(1)}, bf16[2,384,640]{2,1,0:T(8,128)(2,1)S(1)}, u32[]{:S(2)}, u32[]{:S(2)}) collective-permute-start(bf16[2,384,640]{2,1,0:T(8,128)(2,1)S(1)} %get-tuple-element.29), channel_id=1, source_target_pairs={{0,2},{2,0},{5,7},{7,5},{8,10},{10,8},{13,15},{15,13},{16,18},{18,... | collective-permute-start | bytes 2949128 | tf_op jit(solution)/shard_map/ppermute | solution.py:234
  125.7 2.1 %terms.5.refs_1_ = bf16[2,2,384,256]{3,2,1,0:T(8,128)(2,1)S(1)} custom-call(bf16[384,768]{1,0:T(8,128)(2,1)} %attend.1.refs_0_, bf16[384,768]{1,0:T(8,128)(2,1)S(1)} %collective-permute-done.6.refs_1_, bf16[768,256]{1,0:T(8,128)(2,1)} %collective-permute-done.15.refs_2_, bf16[768,256]{1,0:T(8,128)(2,1)} %collective-permute-done.16.refs_3_), custom_call_target="tpu_custom_call" | custom-call | flops 60397977600 | bytes 2752512 | tf_op jit(solution)/shard_map/terms/pallas_call | solution.py:117
  127.7 1.3 collective-permute-start.17
  129.1 14.8 %collective-permute-done.10.refs_1_ = bf16[2,384,640]{2,1,0:T(8,128)(2,1)S(1)} collective-permute-done((bf16[2,384,640]{2,1,0:T(8,128)(2,1)S(1)}, bf16[2,384,640]{2,1,0:T(8,128)(2,1)S(1)}, u32[]{:S(2)}, u32[]{:S(2)}) %collective-permute-start.10) | collective-permute-done | bytes 983072 | tf_op jit(solution)/shard_map/ppermute | solution.py:234
  144.0 2.6 %collective-permute-start.11 = (bf16[384,640]{1,0:T(8,128)(2,1)S(1)}, bf16[384,640]{1,0:T(8,128)(2,1)S(1)}, u32[]{:S(2)}, u32[]{:S(2)}) collective-permute-start(bf16[384,640]{1,0:T(8,128)(2,1)S(1)} %get-tuple-element.31), channel_id=1, source_target_pairs={{0,16},{2,18},{5,21},{7,23},{8,24},{10,26},{13,29},{15,31},{16,0},... | collective-permute-start | bytes 1474568 | tf_op jit(solution)/shard_map/ppermute | solution.py:234
  147.6 12.1 %collective-permute-done.11.refs_3_.refs_2_.refs_4_ = bf16[384,640]{1,0:T(8,128)(2,1)S(1)} collective-permute-done((bf16[384,640]{1,0:T(8,128)(2,1)S(1)}, bf16[384,640]{1,0:T(8,128)(2,1)S(1)}, u32[]{:S(2)}, u32[]{:S(2)}) %collective-permute-start.11) | collective-permute-done | bytes 491552 | tf_op jit(solution)/shard_map/ppermute | solution.py:234
  161.4 1.4 collective-permute-start.14
  164.3 1.3 collective-permute-start.19
  165.7 1.1 copy-done.2
  166.7 1.0 copy-done.4
  167.7 2.1 %gated.1 = bf16[384,1280]{1,0:T(8,128)(2,1)} custom-call(s32[1]{0:T(128)} %bitcast.refs_0_, s32[1]{0:T(128)} %bitcast.1.refs_1_, f32[1,1280]{1,0:T(1,128)S(1)} %reshape.21.refs_2_, f32[384,640]{1,0:T(8,128)S(1)} %get-tuple-element.30.refs_3_, bf16[384,640]{1,0:T(8,128)(2,1)S(1)} %collective-permute-done.11.refs_3_.refs_2_.refs_4_, f32[384,384]{1,0:T(8,128)S(1)} %copy-done.2, ...), custom_call_target="tpu_custom_call" | custom-call | bytes 3937280 | tf_op jit(solution)/shard_map/gated/pallas_call | solution.py:117
  (47 shorter events, 7.0 us)
Async XLA Ops:
  0.0 9.7 %copy-start = (bf16[768,1280]{1,0:T(8,128)(2,1)S(1)}, bf16[768,1280]{1,0:T(8,128)(2,1)}, u32[]{:S(2)}) copy-start(bf16[768,1280]{1,0:T(8,128)(2,1)} %param.10) | copy-start | bytes 5898244
  0.0 58.9 %copy-start.5 = (bf16[384,6,128]{2,0,1:T(8,128)(2,1)S(1)}, bf16[384,6,128]{2,0,1:T(8,128)(2,1)}, u32[]{:S(2)}) copy-start(bf16[384,6,128]{2,0,1:T(8,128)(2,1)} %param.6) | copy-start | bytes 1769476
  0.0 19.6 %collective-permute-start = (bf16[384,6,128]{2,0,1:T(8,128)(2,1)}, bf16[384,6,128]{2,0,1:T(8,128)(2,1)}, u32[]{:S(2)}, u32[]{:S(2)}) collective-permute-start(bf16[384,6,128]{2,0,1:T(8,128)(2,1)} %param.7), channel_id=1, source_target_pairs={{0,4},{4,8},{8,12},{12,0},{1,5},{5,9},{9,13},{13,1},{2,6},{6,10},{... | collective-permute-start | bytes 1769480 | tf_op jit(solution)/shard_map/ppermute | solution.py:17
  3.0 29.3 %collective-permute-start.1 = (bf16[384,6,128]{2,0,1:T(8,128)(2,1)}, bf16[384,6,128]{2,0,1:T(8,128)(2,1)}, u32[]{:S(2)}, u32[]{:S(2)}) collective-permute-start(bf16[384,6,128]{2,0,1:T(8,128)(2,1)} %param.7), channel_id=1, source_target_pairs={{0,12},{4,0},{8,4},{12,8},{1,13},{5,1},{9,5},{13,9},{2,14},{6,2},{... | collective-permute-start | bytes 1769480 | tf_op jit(solution)/shard_map/ppermute | solution.py:17
  5.1 39.8 %collective-permute-start.2 = (bf16[384,6,128]{2,0,1:T(8,128)(2,1)}, bf16[384,6,128]{2,0,1:T(8,128)(2,1)}, u32[]{:S(2)}, u32[]{:S(2)}) collective-permute-start(bf16[384,6,128]{2,0,1:T(8,128)(2,1)} %param.8), channel_id=1, source_target_pairs={{0,4},{4,8},{8,12},{12,0},{1,5},{5,9},{9,13},{13,1},{2,6},{6,10},{... | collective-permute-start | bytes 1769480 | tf_op jit(solution)/shard_map/ppermute | solution.py:17
  5.1 50.9 %collective-permute-start.3 = (bf16[384,6,128]{2,0,1:T(8,128)(2,1)}, bf16[384,6,128]{2,0,1:T(8,128)(2,1)}, u32[]{:S(2)}, u32[]{:S(2)}) collective-permute-start(bf16[384,6,128]{2,0,1:T(8,128)(2,1)} %param.8), channel_id=1, source_target_pairs={{0,12},{4,0},{8,4},{12,8},{1,13},{5,1},{9,5},{13,9},{2,14},{6,2},{... | collective-permute-start | bytes 1769480 | tf_op jit(solution)/shard_map/ppermute | solution.py:17
  9.7 49.2 %copy-start.6 = (bf16[384,6,128]{2,0,1:T(8,128)(2,1)S(1)}, bf16[384,6,128]{2,0,1:T(8,128)(2,1)}, u32[]{:S(2)}) copy-start(bf16[384,6,128]{2,0,1:T(8,128)(2,1)} %param.7) | copy-start | bytes 1769476
  9.7 49.2 %copy-start.7 = (bf16[384,6,128]{2,0,1:T(8,128)(2,1)S(1)}, bf16[384,6,128]{2,0,1:T(8,128)(2,1)}, u32[]{:S(2)}) copy-start(bf16[384,6,128]{2,0,1:T(8,128)(2,1)} %param.8) | copy-start | bytes 1769476
  56.1 25.5 %collective-permute-start.5 = (bf16[768,384]{1,0:T(8,128)(2,1)S(1)}, bf16[768,384]{1,0:T(8,128)(2,1)S(1)}, u32[]{:S(2)}, u32[]{:S(2)}) collective-permute-start(bf16[768,384]{1,0:T(8,128)(2,1)S(1)} %constant_dynamic-slice_fusion.1.refs_2_), channel_id=1, source_target_pairs={{0,4},{4,0},{8,12},{12,8},{1,5},{5,1},{9,13},{13,9},{2,6},{6,2},{1... | collective-permute-start | bytes 1769480 | tf_op jit(solution)/shard_map/ppermute | solution.py:22
  57.2 28.7 %collective-permute-start.4 = (bf16[768,384]{1,0:T(8,128)(2,1)S(1)}, bf16[768,384]{1,0:T(8,128)(2,1)}, u32[]{:S(2)}, u32[]{:S(2)}) collective-permute-start(bf16[768,384]{1,0:T(8,128)(2,1)S(1)} %constant_dynamic-slice_fusion.1.refs_2_), channel_id=1, source_target_pairs={{0,8},{4,12},{8,0},{12,4},{1,9},{5,13},{9,1},{13,5},{2,10},{6,14},... | collective-permute-start | bytes 1769480 | tf_op jit(solution)/shard_map/ppermute | solution.py:22
  81.5 0.8 copy-start.8
  85.8 25.2 %collective-permute-start.8 = (bf16[768,384]{1,0:T(8,128)(2,1)}, bf16[768,384]{1,0:T(8,128)(2,1)}, u32[]{:S(2)}, u32[]{:S(2)}) collective-permute-start(bf16[768,384]{1,0:T(8,128)(2,1)} %collective-permute-done.4.refs_4_), channel_id=1, source_target_pairs={{0,4},{4,0},{8,12},{12,8},{1,5},{5,1},{9,13},{13,9},{2,6},{6,2},{1... | collective-permute-start | bytes 1769480 | tf_op jit(solution)/shard_map/ppermute | solution.py:22
  85.8 25.2 %collective-permute-start.6 = (bf16[384,768]{1,0:T(8,128)(2,1)}, bf16[384,768]{1,0:T(8,128)(2,1)S(1)}, u32[]{:S(2)}, u32[]{:S(2)}) collective-permute-start(bf16[384,768]{1,0:T(8,128)(2,1)} %attend.1.refs_0_), channel_id=1, source_target_pairs={{0,16},{16,0},{1,17},{17,1},{2,18},{18,2},{3,19},{19,3},{4,20},{20... | collective-permute-start | bytes 1769480 | tf_op jit(solution)/shard_map/ppermute | solution.py:22
  87.4 21.0 %collective-permute-start.7 = (bf16[768,256]{1,0:T(8,128)(2,1)}, bf16[768,256]{1,0:T(8,128)(2,1)}, u32[]{:S(2)}, u32[]{:S(2)}) collective-permute-start(bf16[768,256]{1,0:T(8,128)(2,1)} %constant_dynamic-slice_fusion.refs_3_), channel_id=1, source_target_pairs={{0,8},{4,12},{8,0},{12,4},{1,9},{5,13},{9,1},{13,5},{2,10},{6,14},... | collective-permute-start | bytes 1179656 | tf_op jit(solution)/shard_map/ppermute | solution.py:22
  88.0 37.7 %collective-permute-start.15 = (bf16[768,256]{1,0:T(8,128)(2,1)}, bf16[768,256]{1,0:T(8,128)(2,1)}, u32[]{:S(2)}, u32[]{:S(2)}) collective-permute-start(bf16[768,256]{1,0:T(8,128)(2,1)} %constant_dynamic-slice_fusion.refs_3_), channel_id=1, source_target_pairs={{0,4},{4,0},{8,12},{12,8},{1,5},{5,1},{9,13},{13,9},{2,6},{6,2},{1... | collective-permute-start | bytes 1179656 | tf_op jit(solution)/shard_map/ppermute | solution.py:22
  108.4 17.3 %collective-permute-start.16 = (bf16[768,256]{1,0:T(8,128)(2,1)}, bf16[768,256]{1,0:T(8,128)(2,1)}, u32[]{:S(2)}, u32[]{:S(2)}) collective-permute-start(bf16[768,256]{1,0:T(8,128)(2,1)} %collective-permute-done.7.refs_5_), channel_id=1, source_target_pairs={{0,4},{4,0},{8,12},{12,8},{1,5},{5,1},{9,13},{13,9},{2,6},{6,2},{1... | collective-permute-start | bytes 1179656 | tf_op jit(solution)/shard_map/ppermute | solution.py:22
  111.1 4.8 %copy-start.9 = (bf16[768,384]{1,0:T(8,128)(2,1)S(1)}, bf16[768,384]{1,0:T(8,128)(2,1)}, u32[]{:S(2)}) copy-start(bf16[768,384]{1,0:T(8,128)(2,1)} %copy-done.8) | copy-start | bytes 1769476
  114.6 7.2 %collective-permute-start.9 = (bf16[2,2,384,640]{3,2,1,0:T(8,128)(2,1)S(1)}, bf16[2,2,384,640]{3,2,1,0:T(8,128)(2,1)S(1)}, u32[]{:S(2)}, u32[]{:S(2)}) collective-permute-start(bf16[2,2,384,640]{3,2,1,0:T(8,128)(2,1)S(1)} %terms.3.refs_1_), channel_id=1, source_target_pairs={{1,0},{3,2},{4,5},{6,7},{9,8},{11,10},{12,13},{14,15},{17,16},{19,... | collective-permute-start | bytes 5898248 | tf_op jit(solution)/shard_map/ppermute | solution.py:234
  118.6 28.0 %collective-permute-start.12 = (bf16[2,2,384,384]{3,2,1,0:T(8,128)(2,1)S(1)}, bf16[2,2,384,384]{3,2,1,0:T(8,128)(2,1)S(1)}, u32[]{:S(2)}, u32[]{:S(2)}) collective-permute-start(bf16[2,2,384,384]{3,2,1,0:T(8,128)(2,1)S(1)} %terms.4.refs_1_), channel_id=1, source_target_pairs={{0,1},{2,3},{5,4},{7,6},{8,9},{10,11},{13,12},{15,14},{16,17},{18,... | collective-permute-start | bytes 3538952 | tf_op jit(solution)/shard_map/ppermute | solution.py:234
  122.2 21.6 %collective-permute-start.10 = (bf16[2,384,640]{2,1,0:T(8,128)(2,1)S(1)}, bf16[2,384,640]{2,1,0:T(8,128)(2,1)S(1)}, u32[]{:S(2)}, u32[]{:S(2)}) collective-permute-start(bf16[2,384,640]{2,1,0:T(8,128)(2,1)S(1)} %get-tuple-element.29), channel_id=1, source_target_pairs={{0,2},{2,0},{5,7},{7,5},{8,10},{10,8},{13,15},{15,13},{16,18},{18,... | collective-permute-start | bytes 2949128 | tf_op jit(solution)/shard_map/ppermute | solution.py:234
  127.7 19.8 %collective-permute-start.17 = (bf16[2,2,384,256]{3,2,1,0:T(8,128)(2,1)S(1)}, bf16[2,2,384,256]{3,2,1,0:T(8,128)(2,1)S(1)}, u32[]{:S(2)}, u32[]{:S(2)}) collective-permute-start(bf16[2,2,384,256]{3,2,1,0:T(8,128)(2,1)S(1)} %terms.5.refs_1_), channel_id=1, source_target_pairs={{0,1},{2,3},{5,4},{7,6},{8,9},{10,11},{13,12},{15,14},{16,17},{18,... | collective-permute-start | bytes 2359304 | tf_op jit(solution)/shard_map/ppermute | solution.py:234
  144.0 15.7 %collective-permute-start.11 = (bf16[384,640]{1,0:T(8,128)(2,1)S(1)}, bf16[384,640]{1,0:T(8,128)(2,1)S(1)}, u32[]{:S(2)}, u32[]{:S(2)}) collective-permute-start(bf16[384,640]{1,0:T(8,128)(2,1)S(1)} %get-tuple-element.31), channel_id=1, source_target_pairs={{0,16},{2,18},{5,21},{7,23},{8,24},{10,26},{13,29},{15,31},{16,0},... | collective-permute-start | bytes 1474568 | tf_op jit(solution)/shard_map/ppermute | solution.py:234
  146.9 13.7 %collective-permute-start.13 = (bf16[2,384,384]{2,1,0:T(8,128)(2,1)S(1)}, bf16[2,384,384]{2,1,0:T(8,128)(2,1)S(1)}, u32[]{:S(2)}, u32[]{:S(2)}) collective-permute-start(bf16[2,384,384]{2,1,0:T(8,128)(2,1)S(1)} %get-tuple-element.34), channel_id=1, source_target_pairs={{1,3},{3,1},{4,6},{6,4},{9,11},{11,9},{12,14},{14,12},{17,19},{19,... | collective-permute-start | bytes 1769480 | tf_op jit(solution)/shard_map/ppermute | solution.py:234
  159.9 5.8 %copy-start.10 = (f32[1280]{0:T(1024)S(1)}, f32[1280]{0:T(1024)}, u32[]{:S(2)}) copy-start(f32[1280]{0:T(1024)} %param.11) | copy-start | bytes 15364
  159.9 2.9 %collective-permute-start.18 = (bf16[2,384,256]{2,1,0:T(8,128)(2,1)S(1)}, bf16[2,384,256]{2,1,0:T(8,128)(2,1)S(1)}, u32[]{:S(2)}, u32[]{:S(2)}) collective-permute-start(bf16[2,384,256]{2,1,0:T(8,128)(2,1)S(1)} %get-tuple-element.38), channel_id=1, source_target_pairs={{1,3},{3,1},{4,6},{6,4},{9,11},{11,9},{12,14},{14,12},{17,19},{19,... | collective-permute-start | bytes 1179656 | tf_op jit(solution)/shard_map/ppermute | solution.py:234
  161.4 2.1 %copy-start.1 = (f32[384,384]{1,0:T(8,128)}, f32[384,384]{1,0:T(8,128)S(1)}, u32[]{:S(2)}) copy-start(f32[384,384]{1,0:T(8,128)S(1)} %get-tuple-element.35.refs_5_) | copy-start | bytes 1769476
  161.4 4.2 %collective-permute-start.14 = (bf16[384,384]{1,0:T(8,128)(2,1)}, bf16[384,384]{1,0:T(8,128)(2,1)}, u32[]{:S(2)}, u32[]{:S(2)}) collective-permute-start(bf16[384,384]{1,0:T(8,128)(2,1)} %get-tuple-element.36.refs_3_), channel_id=1, source_target_pairs={{1,17},{3,19},{4,20},{6,22},{9,25},{11,27},{12,28},{14,30},{17,1},... | collective-permute-start | bytes 884744 | tf_op jit(solution)/shard_map/ppermute | solution.py:234
  163.6 0.7 copy-start.3
  164.3 1.4 collective-permute-start.19
  165.7 1.1 copy-start.2
  166.7 1.0 copy-start.4

commit v3 on v2

v3 whole, which is shorter than its diff:
```python
import functools
import math

import jax
import jax.numpy as jnp
from jax import lax
from jax.experimental import pallas as pl
from jax.experimental.pallas import tpu as pltpu
from jax.sharding import PartitionSpec as P

TILE = 128
CUT = 256


def passed_along(array, axis, by):
    count = lax.axis_size(axis)
    return lax.ppermute(array, axis, [(i, (i + by) % count) for i in range(count)])


def swapped(array, axis, mask):
    count = lax.axis_size(axis)
    return lax.ppermute(array, axis, [(i, i ^ mask) for i in range(count)])


def attend_kernel(reach, score_scale, keep_ref, queries_ref, *refs):
    key_refs, value_refs, out_ref = refs[: 2 * reach + 1], refs[2 * reach + 1 : -1], refs[-1]
    tiles = queries_ref.shape[1] // TILE
    scale = score_scale * math.log2(math.e)
    for tile in range(tiles):
        query_tile = queries_ref[0, tile * TILE : (tile + 1) * TILE]
        scores = []
        for slab, key_ref in enumerate(key_refs):
            raw = lax.dot_general(
                query_tile, key_ref[0], (((1,), (1,)), ((), ())), preferred_element_type=jnp.float32
            )
            keep = keep_ref[tile : tile + 1, slab * tiles * TILE : (slab + 1) * tiles * TILE]
            scores.append(jnp.where(keep > 0, raw, -jnp.inf))
        peak = scores[0].max(axis=1, keepdims=True)
        for block in scores[1:]:
            peak = jnp.maximum(peak, block.max(axis=1, keepdims=True))
        total, out = 0.0, 0.0
        for block, value_ref in zip(scores, value_refs):
            weights = jnp.exp2((block - peak) * scale)
            total = total + weights.sum(axis=1, keepdims=True)
            out = out + jnp.dot(
                weights.astype(jnp.bfloat16), value_ref[0], preferred_element_type=jnp.float32
            )
        out_ref[tile * TILE : (tile + 1) * TILE] = (out / total).astype(out_ref.dtype)


def attend(queries, key_slabs, value_slabs, keep_tiles):
    rows, head_count, depth = queries.shape
    by_head = [rows_of.transpose(1, 0, 2) for rows_of in (queries, *key_slabs, *value_slabs)]
    keep = jnp.repeat(keep_tiles.astype(jnp.float32), TILE, axis=1)
    block = pl.BlockSpec((1, rows, depth), lambda head: (head, 0, 0))
    return pl.pallas_call(
        functools.partial(attend_kernel, len(key_slabs) // 2, 1.0 / math.sqrt(depth)),
        grid=(head_count,),
        out_shape=jax.ShapeDtypeStruct((rows, head_count * depth), jnp.bfloat16),
        in_specs=[pl.BlockSpec(keep.shape, lambda head: (0, 0))] + [block] * len(by_head),
        out_specs=pl.BlockSpec((rows, depth), lambda head: (0, head)),
        compiler_params=pltpu.CompilerParams(vmem_limit_bytes=16 * 2**20),
        cost_estimate=pl.CostEstimate(flops=2 * 10**10, bytes_accessed=10**7, transcendentals=0),
        name="attend",
    )(keep, *by_head)


def halo(key_rows, value_rows):
    reach_slabs = min(2, (lax.axis_size("tm") - 1) // 2)
    lower_list = []
    upper_list = []
    for distance in range(1, reach_slabs + 1):
        lower_list.append([passed_along(rows, "tm", distance) for rows in (key_rows, value_rows)])
        upper_list.append([passed_along(rows, "tm", -distance) for rows in (key_rows, value_rows)])
    return lower_list[::-1], upper_list


def diagonal(array):
    pairs = [(4 * g + h, 4 * (g ^ 1) + (h ^ 2)) for g in range(2) for h in range(4)]
    return lax.ppermute(array, ("groups", "head"), pairs)


def all_slabs(lower, own, upper):
    ordered = lower + [own] + upper
    return [[slab[which] for slab in ordered] for which in (0, 1)]


def any_mesh(queries, key_rows, value_rows, keep_tiles, out_weight, gate_scale):
    lower, upper = halo(key_rows, value_rows)
    key_slabs, value_slabs = all_slabs(lower, (key_rows, value_rows), upper)
    attended = attend(queries, key_slabs, value_slabs, keep_tiles)
    partial_value = jnp.dot(
        attended,
        lax.all_gather(out_weight, "tm", axis=1, tiled=True),
        preferred_element_type=jnp.float32,
    )
    summed = lax.psum_scatter(
        partial_value.astype(jnp.bfloat16), "head", scatter_dimension=1, tiled=True
    ).astype(jnp.float32)
    return (gate_scale[None, :] * summed).astype(jnp.bfloat16)


def after(array, *others):
    return lax.optimization_barrier((array, *others))[0]


def f32(array):
    return array.astype(jnp.float32)


SMEM = pl.BlockSpec(memory_space=pltpu.SMEM)
WHOLE = pl.BlockSpec(memory_space=pltpu.VMEM)
LATER = pl.BlockSpec(memory_space=pl.ANY)


def local_call(kernel, outs, flags, arrays, earlier, name, flops=0, left=(), scratch=()):
    def body(*refs):
        count = len(flags) + len(arrays) + len(left)
        kernel(*refs[:count], *refs[count + len(earlier) :])

    moved = sum(array.size * array.dtype.itemsize for array in (*arrays, *left, *outs))
    return pl.pallas_call(
        body,
        out_shape=outs,
        in_specs=[SMEM] * len(flags)
        + [WHOLE] * len(arrays)
        + [LATER] * (len(left) + len(earlier)),
        out_specs=[WHOLE] * len(outs),
        scratch_shapes=scratch,
        compiler_params=pltpu.CompilerParams(vmem_limit_bytes=16 * 2**20),
        cost_estimate=pl.CostEstimate(flops=flops, bytes_accessed=moved, transcendentals=0),
        name=name,
    )(*[jnp.int32(flag).reshape(1) for flag in flags], *arrays, *left, *earlier)


def terms(rows_of, blocks, role, first, cost, earlier=()):
    rows, depth = rows_of[0][0].shape
    width = blocks[0].shape[2]
    flat = [array for core in rows_of for array in core]

    def kernel(role_ref, first_ref, *refs):
        rows_refs, block_refs = refs[:4], refs[4:8]
        near_ref, far_ref, near_given_ref, far_given_ref, held_rows, weight, landed = refs[8:]
        out_refs = ((near_ref, far_ref), (near_given_ref, far_given_ref))

        def write(odd, second):
            copies = [
                pltpu.make_async_copy(
                    rows_ref,
                    held_rows.at[pl.ds(index % 2 * rows, rows), pl.ds(index // 2 * depth, depth)],
                    landed.at[index],
                )
                for index, rows_ref in enumerate(rows_refs)
            ] + [
                pltpu.make_async_copy(
                    block_refs[odd + 2 * (slot ^ second)].at[core],
                    weight.at[slot, pl.ds(core * depth, depth)],
                    landed.at[4 + 2 * slot + core],
                )
                for slot in (0, 1)
                for core in (0, 1)
            ]
            for copy in copies[6:] + copies[:6]:
                copy.start()
            for copy in copies[6:] + copies[:4]:
                copy.wait()
            for slot in (1, 0):
                if slot == 0:
                    for copy in copies[4:6]:
                        copy.wait()
                total = jnp.dot(
                    held_rows[...], weight[slot], preferred_element_type=jnp.float32
                )
                for video, out_ref in enumerate(out_refs[slot]):
                    out_ref[...] = total[video * rows : (video + 1) * rows].astype(out_ref.dtype)

        for odd in (0, 1):
            for second in (0, 1):
                chosen = (role_ref[0] == odd) & (first_ref[0] == 1 - second)
                pl.when(chosen)(functools.partial(write, odd, second))

    kinds = (jnp.float32, jnp.bfloat16, jnp.bfloat16, jnp.bfloat16)
    outs = [jax.ShapeDtypeStruct((rows, width), kind) for kind in kinds]
    scratch = [
        pltpu.VMEM((2 * rows, 2 * depth), jnp.bfloat16),
        pltpu.VMEM((2, 2 * depth, width), jnp.bfloat16),
        pltpu.SemaphoreType.DMA((8,)),
    ]
    left = (*flat, *blocks)
    return local_call(
        kernel, outs, (role, first), (), earlier, "terms", cost, left=left, scratch=scratch
    )


def held(arrays, earlier, cost=0):
    return pl.pallas_call(
        lambda *refs: None,
        out_shape=[jax.ShapeDtypeStruct(array.shape, array.dtype) for array in arrays],
        in_specs=[LATER] * (len(arrays) + len(earlier)),
        out_specs=[LATER] * len(arrays),
        input_output_aliases={index: index for index in range(len(arrays))},
        cost_estimate=pl.CostEstimate(flops=cost, bytes_accessed=0, transcendentals=0),
        name="held",
    )(*arrays, *earlier)


def gated(gate_scale, parts, video, earlier=()):
    rows = parts[0][0][0].shape[0]
    width = sum(near[0].shape[1] for near, _ in parts)

    def kernel(video_ref, gate_ref, *refs):
        out_ref = refs[-1]

        def write(place):
            part_refs = list(refs[:-1])
            column = 0
            for part in parts:
                for side, half in enumerate(part):
                    total = f32(part_refs.pop(0)[...])
                    for _ in half[1:]:
                        total = total + f32(part_refs.pop(0)[...])
                    start = (side ^ place) * width + column
                    columns = slice(start, start + total.shape[1])
                    out_ref[:, columns] = (gate_ref[:, columns] * total).astype(out_ref.dtype)
                column += part[0][0].shape[1]

        for place in (0, 1):
            pl.when(video_ref[0] == place)(functools.partial(write, place))

    arrays = [array for part in parts for half in part for array in half]
    out = jax.ShapeDtypeStruct((rows, 2 * width), jnp.bfloat16)
    arrays = (gate_scale.reshape(1, -1), *arrays)
    return local_call(kernel, [out], (video,), arrays, earlier, "gated")[0]


def square_mesh(queries, key_rows, value_rows, keep_tiles, out_weight, gate_scale):
    video = lax.axis_index("groups")
    slab = lax.axis_index("tm")
    head = lax.axis_index("head")
    width = out_weight.shape[1] // 2
    cut = width - CUT
    role = (slab ^ head) & 1
    first = slab // 2 == head // 2

    def passed(array, slab_mask, head_mask, odd):
        pairs = [
            (4 * t + h, 4 * (t ^ slab_mask) + (h ^ head_mask))
            for t in range(4)
            for h in range(4)
            if (t ^ h) & 1 == odd
        ]
        return lax.ppermute(array, ("tm", "head"), pairs)

    lower, upper = halo(key_rows, value_rows)
    half = lax.dynamic_slice_in_dim(out_weight, video * width, width, 1)
    both = jnp.stack([half, passed(half, 0, 1, 1)])
    early, late = lax.optimization_barrier((both[..., :cut], both[..., cut:], lower, upper))[:2]
    block_0 = [early, late]
    block_2 = [passed(early, 2, 0, 0)]
    block_1 = [passed(early, 1, 0, 0)]

    key_slabs, value_slabs = all_slabs(lower, (key_rows, value_rows), upper)
    mine = attend(queries, key_slabs, value_slabs, keep_tiles)
    mine, late, block_2[0], block_1[0] = lax.optimization_barrier(
        (mine, late, block_2[0], block_1[0])
    )
    other = swapped(mine, "groups", 1)
    rows_of = (mine, other), (swapped(mine, "head", 1), swapped(other, "head", 1))
    block_2 += held([passed(late, 2, 0, 0)], [], 100 * 2**33)
    late = held([late], [block_2[1]])[0]
    block_0[1] = late
    block_1.append(passed(late, 1, 0, 0))
    block_3 = [passed(block, 1, 0, 0) for block in block_2]
    parts = list(zip(block_0, block_1, block_2, block_3))

    cost = 100 * 2**33
    summed = []
    for part in parts:
        near, far, near_given, far_given = terms(rows_of, part, role, first, cost)
        across = swapped(near_given, "head", 2)
        summed.append(((near, across), (swapped(far, "groups", 1), diagonal(far_given))))
    return gated(gate_scale, summed, video)


def solution(mesh):
    placed = (
        P(("groups", "tm"), "head", None),
        P(("groups", "tm"), "head", None),
        P(("groups", "tm"), "head", None),
        P(("groups", "tm"), None),
        P("head", "tm"),
        P(("groups", "head")),
    )
    sizes = (mesh.shape["groups"], mesh.shape["tm"], mesh.shape["head"])
    return jax.shard_map(
        square_mesh if sizes == (2, 4, 4) else any_mesh,
        mesh=mesh,
        in_specs=placed,
        out_specs=P(("groups", "tm"), "head"),
        check_vma=False,
    )
```

time: 170 us -> 155 us (0.912)
  the two profiles are of different devices: /device:TPU:0 before, /device:TPU:1 now
where the time goes in v3:
time: 155 us
  waiting for transfers between devices  80 us (52%)
  starting transfers between devices  45.1 us (29%)
  Pallas kernels  23.1 us (15%)
  local copies, waits for them, and re-layouts  6.29 us (4%)
    ppermute x4, waiting for transfers between devices, passed_along(): lax.ppermute(array, axis, [(i, (i + by) % count) for i in range(count)])  48 us
    ppermute x7, starting transfers between devices, swapped(): return lax.ppermute(array, axis, [(i, i ^ mask) for i in range(count)])  27 us
    ppermute x7, waiting for transfers between devices, passed(): return lax.ppermute(array, ('tm', 'head'), pairs)  25.8 us
    pallas_call x3, Pallas kernels, local_call(): pl.pallas_call(body, out_shape=outs, in_specs=[SMEM] * len(flags) + [WHOL...  13.1 us
    pallas_call x1, Pallas kernels, attend(): pl.pallas_call(functools.partial(attend_kernel, len(key_slabs) // 2, 1.0...  9.98 us
    ppermute x7, starting transfers between devices, passed(): return lax.ppermute(array, ('tm', 'head'), pairs)  8.72 us
    ppermute x4, starting transfers between devices, passed_along(): lax.ppermute(array, axis, [(i, (i + by) % count) for i in range(count)])  6.8 us
    ppermute x7, waiting for transfers between devices, swapped(): return lax.ppermute(array, axis, [(i, i ^ mask) for i in range(count)])  6.18 us
  transfers between devices with their start and end apart: 20, of which 9 were waited for; matrix products, arithmetic and copies ran while one was open for 0% of the time, Pallas kernels for 13%

profile of v3, /device:TPU:1, one launch (start us, length us, event | category | flops | bytes accessed | tf_op | source)
XLA Modules:
  0.0 154.8 jit_solution(3268629683779401182)
XLA Ops:
  0.0 1.5 copy-done
  1.6 2.0 %collective-permute-start.4 = (bf16[768,640]{1,0:T(8,128)(2,1)S(1)}, bf16[768,640]{1,0:T(8,128)(2,1)S(1)}, u32[]{:S(2)}, u32[]{:S(2)}) collective-permute-start(bf16[768,640]{1,0:T(8,128)(2,1)S(1)} %constant_dynamic-slice_fusion), channel_id=1, source_target_pairs={{1,0},{3,2},{4,5},{6,7},{9,8},{11,10},{12,13},{14,15},{17,16},{19,... | collective-permute-start | bytes 2949128 | tf_op jit(solution)/shard_map/ppermute | solution.py:252
  3.7 1.4 collective-permute-start
  5.1 2.1 %collective-permute-start.1 = (bf16[384,6,128]{2,0,1:T(8,128)(2,1)S(1)}, bf16[384,6,128]{2,0,1:T(8,128)(2,1)S(1)}, u32[]{:S(2)}, u32[]{:S(2)}) collective-permute-start(bf16[384,6,128]{2,0,1:T(8,128)(2,1)S(1)} %copy-done.12), channel_id=1, source_target_pairs={{0,12},{4,0},{8,4},{12,8},{1,13},{5,1},{9,5},{13,9},{2,14},{6,2},{... | collective-permute-start | bytes 1769480 | tf_op jit(solution)/shard_map/ppermute | solution.py:17
  7.8 2.7 %collective-permute-start.3 = (bf16[384,6,128]{2,0,1:T(8,128)(2,1)}, bf16[384,6,128]{2,0,1:T(8,128)(2,1)S(1)}, u32[]{:S(2)}, u32[]{:S(2)}) collective-permute-start(bf16[384,6,128]{2,0,1:T(8,128)(2,1)} %param.8), channel_id=1, source_target_pairs={{0,12},{4,0},{8,4},{12,8},{1,13},{5,1},{9,5},{13,9},{2,14},{6,2},{... | collective-permute-start | bytes 1769480 | tf_op jit(solution)/shard_map/ppermute | solution.py:17
  10.9 8.7 %collective-permute-done = bf16[384,6,128]{2,0,1:T(8,128)(2,1)S(1)} collective-permute-done((bf16[384,6,128]{2,0,1:T(8,128)(2,1)S(1)}, bf16[384,6,128]{2,0,1:T(8,128)(2,1)S(1)}, u32[]{:S(2)}, u32[]{:S(2)}) %collective-permute-start) | collective-permute-done | bytes 589856 | tf_op jit(solution)/shard_map/ppermute | solution.py:17
  19.7 15.2 %collective-permute-done.1 = bf16[384,6,128]{2,0,1:T(8,128)(2,1)S(1)} collective-permute-done((bf16[384,6,128]{2,0,1:T(8,128)(2,1)S(1)}, bf16[384,6,128]{2,0,1:T(8,128)(2,1)S(1)}, u32[]{:S(2)}, u32[]{:S(2)}) %collective-permute-start.1) | collective-permute-done | bytes 589856 | tf_op jit(solution)/shard_map/ppermute | solution.py:17
  34.9 10.1 %collective-permute-done.2 = bf16[384,6,128]{2,0,1:T(8,128)(2,1)S(1)} collective-permute-done((bf16[384,6,128]{2,0,1:T(8,128)(2,1)}, bf16[384,6,128]{2,0,1:T(8,128)(2,1)S(1)}, u32[]{:S(2)}, u32[]{:S(2)}) %collective-permute-start.2) | collective-permute-done | bytes 589856 | tf_op jit(solution)/shard_map/ppermute | solution.py:17
  45.0 13.9 %collective-permute-done.3 = bf16[384,6,128]{2,0,1:T(8,128)(2,1)S(1)} collective-permute-done((bf16[384,6,128]{2,0,1:T(8,128)(2,1)}, bf16[384,6,128]{2,0,1:T(8,128)(2,1)S(1)}, u32[]{:S(2)}, u32[]{:S(2)}) %collective-permute-start.3) | collective-permute-done | bytes 589856 | tf_op jit(solution)/shard_map/ppermute | solution.py:17
  59.6 1.3 collective-permute-start.6
  60.9 10.0 %attend.1.refs_2_ = bf16[384,768]{1,0:T(8,128)(2,1)} custom-call(f32[3,1152]{1,0:T(4,128)S(1)} %bitcast.18, bf16[6,384,128]{2,1,0:T(8,128)(2,1)S(1)} %bitcast.19, bf16[6,384,128]{2,1,0:T(8,128)(2,1)S(1)} %bitcast.21, bf16[6,384,128]{2,1,0:T(8,128)(2,1)S(1)} %bitcast.20, bf16[6,384,128]{2,1,0:T(8,128)(2,1)S(1)} %bitcast.22, ...), custom_call_target="tpu_custom_call" | custom-call | flops 20000000000 | bytes 10000000 | tf_op jit(solution)/shard_map/attend/pallas_call | solution.py:56
  70.9 6.0 %collective-permute-done.6.refs_7_ = bf16[2,768,384]{2,1,0:T(8,128)(2,1)S(1)} collective-permute-done((bf16[2,768,384]{2,1,0:T(8,128)(2,1)S(1)}, bf16[2,768,384]{2,1,0:T(8,128)(2,1)S(1)}, u32[]{:S(2)}, u32[]{:S(2)}) %collective-permute-start.6) | collective-permute-done | bytes 1179680 | tf_op jit(solution)/shard_map/ppermute | solution.py:252
  77.0 1.0 copy-done.9
  78.7 2.0 %collective-permute-start.7 = (bf16[384,768]{1,0:T(8,128)(2,1)}, bf16[384,768]{1,0:T(8,128)(2,1)}, u32[]{:S(2)}, u32[]{:S(2)}) collective-permute-start(bf16[384,768]{1,0:T(8,128)(2,1)} %attend.1.refs_2_), channel_id=1, source_target_pairs={{0,16},{16,0},{1,17},{17,1},{2,18},{18,2},{3,19},{19,3},{4,20},{20... | collective-permute-start | bytes 1769480 | tf_op jit(solution)/shard_map/ppermute | solution.py:22
  80.7 15.2 %collective-permute-start.8 = (bf16[384,768]{1,0:T(8,128)(2,1)}, bf16[384,768]{1,0:T(8,128)(2,1)}, u32[]{:S(2)}, u32[]{:S(2)}) collective-permute-start(bf16[384,768]{1,0:T(8,128)(2,1)} %attend.1.refs_2_), channel_id=1, source_target_pairs={{0,1},{1,0},{2,3},{3,2},{4,5},{5,4},{6,7},{7,6},{8,9},{9,8},{10,11... | collective-permute-start | bytes 1769480 | tf_op jit(solution)/shard_map/ppermute | solution.py:22
  96.0 1.3 collective-permute-start.10
  97.3 6.9 %collective-permute-start.9 = (bf16[384,768]{1,0:T(8,128)(2,1)}, bf16[384,768]{1,0:T(8,128)(2,1)}, u32[]{:S(2)}, u32[]{:S(2)}) collective-permute-start(bf16[384,768]{1,0:T(8,128)(2,1)} %collective-permute-done.7.refs_3_), channel_id=1, source_target_pairs={{0,1},{1,0},{2,3},{3,2},{4,5},{5,4},{6,7},{7,6},{8,9},{9,8},{10,11... | collective-permute-start | bytes 1769480 | tf_op jit(solution)/shard_map/ppermute | solution.py:22
  105.0 1.4 collective-permute-start.16
  106.5 1.3 collective-permute-start.15
  107.8 13.8 %collective-permute-done.10.refs_9_ = bf16[2,768,384]{2,1,0:T(8,128)(2,1)} collective-permute-done((bf16[2,768,384]{2,1,0:T(8,128)(2,1)}, bf16[2,768,384]{2,1,0:T(8,128)(2,1)}, u32[]{:S(2)}, u32[]{:S(2)}) %collective-permute-start.10) | collective-permute-done | bytes 1179680 | tf_op jit(solution)/shard_map/ppermute | solution.py:252
  121.6 1.3 copy-done.8
  122.8 1.3 copy-done.10
  124.1 5.9 %terms.2 = (f32[384,384]{1,0:T(8,128)S(1)}, bf16[384,384]{1,0:T(8,128)(2,1)}, bf16[384,384]{1,0:T(8,128)(2,1)}, bf16[384,384]{1,0:T(8,128)(2,1)}) custom-call(s32[1]{0:T(128)} %bitcast.1.refs_0_, s32[1]{0:T(128)} %bitcast.2.refs_1_, bf16[384,768]{1,0:T(8,128)(2,1)} %attend.1.refs_2_, bf16[384,768]{1,0:T(8,128)(2,1)} %collective-permute-done.7.refs_3_, ...), custom_call_target="tpu_custom_call" | custom-call | flops 858993459200 | bytes 8552448 | tf_op jit(solution)/shard_map/terms/pallas_call | solution.py:122
  130.0 1.2 collective-permute-start.11
  131.4 1.3 collective-permute-start.13
  132.7 6.0 %collective-permute-done.15.refs_7_ = bf16[2,768,256]{2,1,0:T(8,128)(2,1)} collective-permute-done((bf16[2,768,256]{2,1,0:T(8,128)(2,1)}, bf16[2,768,256]{2,1,0:T(8,128)(2,1)}, u32[]{:S(2)}, u32[]{:S(2)}) %collective-permute-start.15) | collective-permute-done | bytes 786464 | tf_op jit(solution)/shard_map/ppermute | solution.py:252
  138.7 4.8 %terms.3 = (f32[384,256]{1,0:T(8,128)S(1)}, bf16[384,256]{1,0:T(8,128)(2,1)S(1)}, bf16[384,256]{1,0:T(8,128)(2,1)S(1)}, bf16[384,256]{1,0:T(8,128)(2,1)S(1)}) custom-call(s32[1]{0:T(128)} %bitcast.1.refs_0_, s32[1]{0:T(128)} %bitcast.2.refs_1_, bf16[384,768]{1,0:T(8,128)(2,1)} %attend.1.refs_2_, bf16[384,768]{1,0:T(8,128)(2,1)} %collective-permute-done.7.refs_3_, ...), custom_call_target="tpu_custom_call" | custom-call | flops 858993459200 | bytes 6488064 | tf_op jit(solution)/shard_map/terms/pallas_call | solution.py:122
  143.6 1.3 collective-permute-start.17
  145.1 1.2 collective-permute-start.19
  146.3 2.6 %collective-permute-done.17.refs_7_ = bf16[384,256]{1,0:T(8,128)(2,1)S(1)} collective-permute-done((bf16[384,256]{1,0:T(8,128)(2,1)S(1)}, bf16[384,256]{1,0:T(8,128)(2,1)S(1)}, u32[]{:S(2)}, u32[]{:S(2)}) %collective-permute-start.17) | collective-permute-done | bytes 196640 | tf_op jit(solution)/shard_map/ppermute | solution.py:22
  149.0 3.5 %collective-permute-done.18.refs_8_ = bf16[384,256]{1,0:T(8,128)(2,1)S(1)} collective-permute-done((bf16[384,256]{1,0:T(8,128)(2,1)S(1)}, bf16[384,256]{1,0:T(8,128)(2,1)S(1)}, u32[]{:S(2)}, u32[]{:S(2)}) %collective-permute-start.18) | collective-permute-done | bytes 196640 | tf_op jit(solution)/shard_map/ppermute | solution.py:22
  152.5 2.4 %gated.1 = bf16[384,1280]{1,0:T(8,128)(2,1)} custom-call(s32[1]{0:T(128)} %bitcast.refs_0_, f32[1,1280]{1,0:T(1,128)S(1)} %reshape.20.refs_1_, f32[384,384]{1,0:T(8,128)S(1)} %get-tuple-element.24.refs_2_, bf16[384,384]{1,0:T(8,128)(2,1)} %collective-permute-done.11.refs_3_, bf16[384,384]{1,0:T(8,128)(2,1)} %collective-permute-done.12.refs_4_, ...), custom_call_target="tpu_custom_call" | custom-call | bytes 3445760 | tf_op jit(solution)/shard_map/gated/pallas_call | solution.py:122
  (52 shorter events, 3.9 us)
Async XLA Ops:
  0.0 1.5 copy-start
  0.0 3.7 %copy-start.12 = (bf16[384,6,128]{2,0,1:T(8,128)(2,1)S(1)}, bf16[384,6,128]{2,0,1:T(8,128)(2,1)}, u32[]{:S(2)}) copy-start(bf16[384,6,128]{2,0,1:T(8,128)(2,1)} %param.7) | copy-start | bytes 1769476
  0.0 10.5 %copy-start.14 = (s32[3,9]{1,0:T(4,128)S(1)}, s32[3,9]{1,0:T(4,128)}, u32[]{:S(2)}) copy-start(s32[3,9]{1,0:T(4,128)} %param.9) | copy-start | bytes 328
  1.6 9.0 %collective-permute-start.4 = (bf16[768,640]{1,0:T(8,128)(2,1)S(1)}, bf16[768,640]{1,0:T(8,128)(2,1)S(1)}, u32[]{:S(2)}, u32[]{:S(2)}) collective-permute-start(bf16[768,640]{1,0:T(8,128)(2,1)S(1)} %constant_dynamic-slice_fusion), channel_id=1, source_target_pairs={{1,0},{3,2},{4,5},{6,7},{9,8},{11,10},{12,13},{14,15},{17,16},{19,... | collective-permute-start | bytes 2949128 | tf_op jit(solution)/shard_map/ppermute | solution.py:252
  3.7 16.0 %collective-permute-start = (bf16[384,6,128]{2,0,1:T(8,128)(2,1)S(1)}, bf16[384,6,128]{2,0,1:T(8,128)(2,1)S(1)}, u32[]{:S(2)}, u32[]{:S(2)}) collective-permute-start(bf16[384,6,128]{2,0,1:T(8,128)(2,1)S(1)} %copy-done.12), channel_id=1, source_target_pairs={{0,4},{4,8},{8,12},{12,0},{1,5},{5,9},{9,13},{13,1},{2,6},{6,10},{... | collective-permute-start | bytes 1769480 | tf_op jit(solution)/shard_map/ppermute | solution.py:17
  5.1 29.8 %collective-permute-start.1 = (bf16[384,6,128]{2,0,1:T(8,128)(2,1)S(1)}, bf16[384,6,128]{2,0,1:T(8,128)(2,1)S(1)}, u32[]{:S(2)}, u32[]{:S(2)}) collective-permute-start(bf16[384,6,128]{2,0,1:T(8,128)(2,1)S(1)} %copy-done.12), channel_id=1, source_target_pairs={{0,12},{4,0},{8,4},{12,8},{1,13},{5,1},{9,5},{13,9},{2,14},{6,2},{... | collective-permute-start | bytes 1769480 | tf_op jit(solution)/shard_map/ppermute | solution.py:17
  7.2 37.8 %collective-permute-start.2 = (bf16[384,6,128]{2,0,1:T(8,128)(2,1)}, bf16[384,6,128]{2,0,1:T(8,128)(2,1)S(1)}, u32[]{:S(2)}, u32[]{:S(2)}) collective-permute-start(bf16[384,6,128]{2,0,1:T(8,128)(2,1)} %param.8), channel_id=1, source_target_pairs={{0,4},{4,8},{8,12},{12,0},{1,5},{5,9},{9,13},{13,1},{2,6},{6,10},{... | collective-permute-start | bytes 1769480 | tf_op jit(solution)/shard_map/ppermute | solution.py:17
  7.8 51.1 %collective-permute-start.3 = (bf16[384,6,128]{2,0,1:T(8,128)(2,1)}, bf16[384,6,128]{2,0,1:T(8,128)(2,1)S(1)}, u32[]{:S(2)}, u32[]{:S(2)}) collective-permute-start(bf16[384,6,128]{2,0,1:T(8,128)(2,1)} %param.8), channel_id=1, source_target_pairs={{0,12},{4,0},{8,4},{12,8},{1,13},{5,1},{9,5},{13,9},{2,14},{6,2},{... | collective-permute-start | bytes 1769480 | tf_op jit(solution)/shard_map/ppermute | solution.py:17
  10.8 66.2 %copy-start.1 = (bf16[2,768,256]{2,1,0:T(8,128)(2,1)}, bf16[2,768,256]{2,1,0:T(8,128)(2,1)S(1)}, u32[]{:S(2)}) copy-start(bf16[2,768,256]{2,1,0:T(8,128)(2,1)S(1)} %pad_maximum_fusion.refs_0_) | copy-start | bytes 2359300
  10.8 50.2 %copy-start.11 = (bf16[384,6,128]{2,0,1:T(8,128)(2,1)S(1)}, bf16[384,6,128]{2,0,1:T(8,128)(2,1)}, u32[]{:S(2)}) copy-start(bf16[384,6,128]{2,0,1:T(8,128)(2,1)} %param.6) | copy-start | bytes 1769476
  10.9 60.0 %copy-start.3 = (bf16[2,768,384]{2,1,0:T(8,128)(2,1)}, bf16[2,768,384]{2,1,0:T(8,128)(2,1)S(1)}, u32[]{:S(2)}) copy-start(bf16[2,768,384]{2,1,0:T(8,128)(2,1)S(1)} %fusion.refs_6_) | copy-start | bytes 3538948
  58.9 12.0 %collective-permute-start.5 = (bf16[2,768,384]{2,1,0:T(8,128)(2,1)S(1)}, bf16[2,768,384]{2,1,0:T(8,128)(2,1)S(1)}, u32[]{:S(2)}, u32[]{:S(2)}) collective-permute-start(bf16[2,768,384]{2,1,0:T(8,128)(2,1)S(1)} %fusion.refs_6_), channel_id=1, source_target_pairs={{0,8},{2,10},{5,13},{7,15},{8,0},{10,2},{13,5},{15,7},{16,24},{18,... | collective-permute-start | bytes 3538952 | tf_op jit(solution)/shard_map/ppermute | solution.py:252
  59.6 17.3 %collective-permute-start.6 = (bf16[2,768,384]{2,1,0:T(8,128)(2,1)S(1)}, bf16[2,768,384]{2,1,0:T(8,128)(2,1)S(1)}, u32[]{:S(2)}, u32[]{:S(2)}) collective-permute-start(bf16[2,768,384]{2,1,0:T(8,128)(2,1)S(1)} %fusion.refs_6_), channel_id=1, source_target_pairs={{0,4},{2,6},{5,1},{7,3},{8,12},{10,14},{13,9},{15,11},{16,20},{18,... | collective-permute-start | bytes 3538952 | tf_op jit(solution)/shard_map/ppermute | solution.py:252
  70.9 7.8 %copy-start.7 = (bf16[2,768,384]{2,1,0:T(8,128)(2,1)}, bf16[2,768,384]{2,1,0:T(8,128)(2,1)S(1)}, u32[]{:S(2)}) copy-start(bf16[2,768,384]{2,1,0:T(8,128)(2,1)S(1)} %collective-permute-done.5.refs_8_) | copy-start | bytes 3538948
  78.0 26.2 %collective-permute-start.14 = (bf16[2,768,256]{2,1,0:T(8,128)(2,1)S(1)}, bf16[2,768,256]{2,1,0:T(8,128)(2,1)S(1)}, u32[]{:S(2)}, u32[]{:S(2)}) collective-permute-start(bf16[2,768,256]{2,1,0:T(8,128)(2,1)S(1)} %pad_maximum_fusion.refs_0_), channel_id=1, source_target_pairs={{0,8},{2,10},{5,13},{7,15},{8,0},{10,2},{13,5},{15,7},{16,24},{18,... | collective-permute-start | bytes 2359304 | tf_op jit(solution)/shard_map/ppermute | solution.py:252
  78.7 18.6 %collective-permute-start.7 = (bf16[384,768]{1,0:T(8,128)(2,1)}, bf16[384,768]{1,0:T(8,128)(2,1)}, u32[]{:S(2)}, u32[]{:S(2)}) collective-permute-start(bf16[384,768]{1,0:T(8,128)(2,1)} %attend.1.refs_2_), channel_id=1, source_target_pairs={{0,16},{16,0},{1,17},{17,1},{2,18},{18,2},{3,19},{19,3},{4,20},{20... | collective-permute-start | bytes 1769480 | tf_op jit(solution)/shard_map/ppermute | solution.py:22
  80.7 27.0 %collective-permute-start.8 = (bf16[384,768]{1,0:T(8,128)(2,1)}, bf16[384,768]{1,0:T(8,128)(2,1)}, u32[]{:S(2)}, u32[]{:S(2)}) collective-permute-start(bf16[384,768]{1,0:T(8,128)(2,1)} %attend.1.refs_2_), channel_id=1, source_target_pairs={{0,1},{1,0},{2,3},{3,2},{4,5},{5,4},{6,7},{7,6},{8,9},{9,8},{10,11... | collective-permute-start | bytes 1769480 | tf_op jit(solution)/shard_map/ppermute | solution.py:22
  96.0 25.6 %collective-permute-start.10 = (bf16[2,768,384]{2,1,0:T(8,128)(2,1)}, bf16[2,768,384]{2,1,0:T(8,128)(2,1)}, u32[]{:S(2)}, u32[]{:S(2)}) collective-permute-start(bf16[2,768,384]{2,1,0:T(8,128)(2,1)} %copy-done.7), channel_id=1, source_target_pairs={{0,4},{2,6},{5,1},{7,3},{8,12},{10,14},{13,9},{15,11},{16,20},{18,... | collective-permute-start | bytes 3538952 | tf_op jit(solution)/shard_map/ppermute | solution.py:252
  97.3 10.5 %collective-permute-start.9 = (bf16[384,768]{1,0:T(8,128)(2,1)}, bf16[384,768]{1,0:T(8,128)(2,1)}, u32[]{:S(2)}, u32[]{:S(2)}) collective-permute-start(bf16[384,768]{1,0:T(8,128)(2,1)} %collective-permute-done.7.refs_3_), channel_id=1, source_target_pairs={{0,1},{1,0},{2,3},{3,2},{4,5},{5,4},{6,7},{7,6},{8,9},{9,8},{10,11... | collective-permute-start | bytes 1769480 | tf_op jit(solution)/shard_map/ppermute | solution.py:22
  105.0 16.5 %copy-start.4 = (bf16[2,768,384]{2,1,0:T(8,128)(2,1)S(1)}, bf16[2,768,384]{2,1,0:T(8,128)(2,1)}, u32[]{:S(2)}) copy-start(bf16[2,768,384]{2,1,0:T(8,128)(2,1)} %copy-done.3) | copy-start | bytes 3538948
  105.0 33.7 %collective-permute-start.16 = (bf16[2,768,256]{2,1,0:T(8,128)(2,1)}, bf16[2,768,256]{2,1,0:T(8,128)(2,1)}, u32[]{:S(2)}, u32[]{:S(2)}) collective-permute-start(bf16[2,768,256]{2,1,0:T(8,128)(2,1)} %held.2.refs_1_.refs_8_), channel_id=1, source_target_pairs={{0,4},{2,6},{5,1},{7,3},{8,12},{10,14},{13,9},{15,11},{16,20},{18,... | collective-permute-start | bytes 2359304 | tf_op jit(solution)/shard_map/ppermute | solution.py:252
  106.5 32.2 %collective-permute-start.15 = (bf16[2,768,256]{2,1,0:T(8,128)(2,1)}, bf16[2,768,256]{2,1,0:T(8,128)(2,1)}, u32[]{:S(2)}, u32[]{:S(2)}) collective-permute-start(bf16[2,768,256]{2,1,0:T(8,128)(2,1)} %held.3.refs_6_), channel_id=1, source_target_pairs={{0,4},{2,6},{5,1},{7,3},{8,12},{10,14},{13,9},{15,11},{16,20},{18,... | collective-permute-start | bytes 2359304 | tf_op jit(solution)/shard_map/ppermute | solution.py:252
  121.6 1.3 copy-start.8
  124.1 14.6 %copy-start.2 = (bf16[2,768,256]{2,1,0:T(8,128)(2,1)S(1)}, bf16[2,768,256]{2,1,0:T(8,128)(2,1)}, u32[]{:S(2)}) copy-start(bf16[2,768,256]{2,1,0:T(8,128)(2,1)} %held.3.refs_6_) | copy-start | bytes 2359300
  124.1 14.6 %copy-start.6 = (bf16[2,768,256]{2,1,0:T(8,128)(2,1)S(1)}, bf16[2,768,256]{2,1,0:T(8,128)(2,1)}, u32[]{:S(2)}) copy-start(bf16[2,768,256]{2,1,0:T(8,128)(2,1)} %held.2.refs_1_.refs_8_) | copy-start | bytes 2359300
  130.0 15.1 %collective-permute-start.11 = (bf16[384,384]{1,0:T(8,128)(2,1)}, bf16[384,384]{1,0:T(8,128)(2,1)}, u32[]{:S(2)}, u32[]{:S(2)}) collective-permute-start(bf16[384,384]{1,0:T(8,128)(2,1)} %get-tuple-element.25), channel_id=1, source_target_pairs={{0,2},{1,3},{2,0},{3,1},{4,6},{5,7},{6,4},{7,5},{8,10},{9,11},{10,... | collective-permute-start | bytes 884744 | tf_op jit(solution)/shard_map/ppermute | solution.py:22
  131.1 15.2 %collective-permute-start.12 = (bf16[384,384]{1,0:T(8,128)(2,1)}, bf16[384,384]{1,0:T(8,128)(2,1)}, u32[]{:S(2)}, u32[]{:S(2)}) collective-permute-start(bf16[384,384]{1,0:T(8,128)(2,1)} %get-tuple-element.26), channel_id=1, source_target_pairs={{0,16},{16,0},{1,17},{17,1},{2,18},{18,2},{3,19},{19,3},{4,20},{20... | collective-permute-start | bytes 884744 | tf_op jit(solution)/shard_map/ppermute | solution.py:22
  131.4 14.9 %collective-permute-start.13 = (bf16[384,384]{1,0:T(8,128)(2,1)}, bf16[384,384]{1,0:T(8,128)(2,1)}, u32[]{:S(2)}, u32[]{:S(2)}) collective-permute-start(bf16[384,384]{1,0:T(8,128)(2,1)} %get-tuple-element.27), channel_id=1, source_target_pairs={{0,18},{1,19},{2,16},{3,17},{16,2},{17,3},{18,0},{19,1},{4,22},{5,... | collective-permute-start | bytes 884744 | tf_op jit(solution)/shard_map/ppermute | solution.py:80
  138.7 7.6 %copy-start.13 = (f32[1280]{0:T(1024)S(1)}, f32[1280]{0:T(1024)}, u32[]{:S(2)}) copy-start(f32[1280]{0:T(1024)} %param.11) | copy-start | bytes 15364
  143.6 5.4 %collective-permute-start.17 = (bf16[384,256]{1,0:T(8,128)(2,1)S(1)}, bf16[384,256]{1,0:T(8,128)(2,1)S(1)}, u32[]{:S(2)}, u32[]{:S(2)}) collective-permute-start(bf16[384,256]{1,0:T(8,128)(2,1)S(1)} %get-tuple-element.30), channel_id=1, source_target_pairs={{0,2},{1,3},{2,0},{3,1},{4,6},{5,7},{6,4},{7,5},{8,10},{9,11},{10,... | collective-permute-start | bytes 589832 | tf_op jit(solution)/shard_map/ppermute | solution.py:22
  144.9 7.6 %collective-permute-start.18 = (bf16[384,256]{1,0:T(8,128)(2,1)S(1)}, bf16[384,256]{1,0:T(8,128)(2,1)S(1)}, u32[]{:S(2)}, u32[]{:S(2)}) collective-permute-start(bf16[384,256]{1,0:T(8,128)(2,1)S(1)} %get-tuple-element.31), channel_id=1, source_target_pairs={{0,16},{16,0},{1,17},{17,1},{2,18},{18,2},{3,19},{19,3},{4,20},{20... | collective-permute-start | bytes 589832 | tf_op jit(solution)/shard_map/ppermute | solution.py:22
  145.1 7.4 %collective-permute-start.19 = (bf16[384,256]{1,0:T(8,128)(2,1)S(1)}, bf16[384,256]{1,0:T(8,128)(2,1)S(1)}, u32[]{:S(2)}, u32[]{:S(2)}) collective-permute-start(bf16[384,256]{1,0:T(8,128)(2,1)S(1)} %get-tuple-element.32), channel_id=1, source_target_pairs={{0,18},{1,19},{2,16},{3,17},{16,2},{17,3},{18,0},{19,1},{4,22},{5,... | collective-permute-start | bytes 589832 | tf_op jit(solution)/shard_map/ppermute | solution.py:80
  (3 other events, 3.2 us)

commit v4 on v3

--- a/solution.py
+++ b/solution.py
@@ -143,41 +143,43 @@
         near_ref, far_ref, near_given_ref, far_given_ref, held_rows, weight, landed = refs[8:]
         out_refs = ((near_ref, far_ref), (near_given_ref, far_given_ref))
 
-        def write(odd, second):
-            copies = [
+        def weight_copies(slot, index):
+            return [
                 pltpu.make_async_copy(
-                    rows_ref,
-                    held_rows.at[pl.ds(index % 2 * rows, rows), pl.ds(index // 2 * depth, depth)],
-                    landed.at[index],
-                )
-                for index, rows_ref in enumerate(rows_refs)
-            ] + [
-                pltpu.make_async_copy(
-                    block_refs[odd + 2 * (slot ^ second)].at[core],
+                    block_refs[index].at[core],
                     weight.at[slot, pl.ds(core * depth, depth)],
                     landed.at[4 + 2 * slot + core],
                 )
-                for slot in (0, 1)
                 for core in (0, 1)
             ]
-            for copy in copies[6:] + copies[:6]:
-                copy.start()
-            for copy in copies[6:] + copies[:4]:
-                copy.wait()
+
+        def start_weights(odd, second):
             for slot in (1, 0):
-                if slot == 0:
-                    for copy in copies[4:6]:
-                        copy.wait()
-                total = jnp.dot(
-                    held_rows[...], weight[slot], preferred_element_type=jnp.float32
-                )
-                for video, out_ref in enumerate(out_refs[slot]):
-                    out_ref[...] = total[video * rows : (video + 1) * rows].astype(out_ref.dtype)
+                for copy in weight_copies(slot, odd + 2 * (slot ^ second)):
+                    copy.start()
 
         for odd in (0, 1):
             for second in (0, 1):
                 chosen = (role_ref[0] == odd) & (first_ref[0] == 1 - second)
-                pl.when(chosen)(functools.partial(write, odd, second))
+                pl.when(chosen)(functools.partial(start_weights, odd, second))
+        rows_copies = [
+            pltpu.make_async_copy(
+                rows_ref,
+                held_rows.at[pl.ds(index % 2 * rows, rows), pl.ds(index // 2 * depth, depth)],
+                landed.at[index],
+            )
+            for index, rows_ref in enumerate(rows_refs)
+        ]
+        for copy in rows_copies:
+            copy.start()
+        for copy in rows_copies:
+            copy.wait()
+        for slot in (1, 0):
+            for copy in weight_copies(slot, 0):
+                copy.wait()
+            total = jnp.dot(held_rows[...], weight[slot], preferred_element_type=jnp.float32)
+            for video, out_ref in enumerate(out_refs[slot]):
+                out_ref[...] = total[video * rows : (video + 1) * rows].astype(out_ref.dtype)
 
     kinds = (jnp.float32, jnp.bfloat16, jnp.bfloat16, jnp.bfloat16)
     outs = [jax.ShapeDtypeStruct((rows, width), kind) for kind in kinds]
@@ -209,23 +211,17 @@
     width = sum(near[0].shape[1] for near, _ in parts)
 
     def kernel(video_ref, gate_ref, *refs):
-        out_ref = refs[-1]
-
-        def write(place):
-            part_refs = list(refs[:-1])
-            column = 0
-            for part in parts:
-                for side, half in enumerate(part):
-                    total = f32(part_refs.pop(0)[...])
-                    for _ in half[1:]:
-                        total = total + f32(part_refs.pop(0)[...])
-                    start = (side ^ place) * width + column
-                    columns = slice(start, start + total.shape[1])
-                    out_ref[:, columns] = (gate_ref[:, columns] * total).astype(out_ref.dtype)
-                column += part[0][0].shape[1]
-
-        for place in (0, 1):
-            pl.when(video_ref[0] == place)(functools.partial(write, place))
+        part_refs, out_ref = list(refs[:-1]), refs[-1]
+        starts = video_ref[0] * width, (1 - video_ref[0]) * width
+        column = 0
+        for part in parts:
+            for start, half in zip(starts, part):
+                total = f32(part_refs.pop(0)[...])
+                for _ in half[1:]:
+                    total = total + f32(part_refs.pop(0)[...])
+                columns = pl.ds(pl.multiple_of(start + column, TILE), total.shape[1])
+                out_ref[:, columns] = (gate_ref[:, columns] * total).astype(out_ref.dtype)
+            column += part[0][0].shape[1]
 
     arrays = [array for part in parts for half in part for array in half]
     out = jax.ShapeDtypeStruct((rows, 2 * width), jnp.bfloat16)
@@ -254,31 +250,32 @@
     lower, upper = halo(key_rows, value_rows)
     half = lax.dynamic_slice_in_dim(out_weight, video * width, width, 1)
     both = jnp.stack([half, passed(half, 0, 1, 1)])
-    early, late = lax.optimization_barrier((both[..., :cut], both[..., cut:], lower, upper))[:2]
+    early, late = lax.optimization_barrier((both[..., :cut], both[..., cut:], lower[-1][0], upper[0][0]))[:2]
     block_0 = [early, late]
     block_2 = [passed(early, 2, 0, 0)]
     block_1 = [passed(early, 1, 0, 0)]
 
     key_slabs, value_slabs = all_slabs(lower, (key_rows, value_rows), upper)
     mine = attend(queries, key_slabs, value_slabs, keep_tiles)
-    mine, late, block_2[0], block_1[0] = lax.optimization_barrier(
-        (mine, late, block_2[0], block_1[0])
-    )
+    mine, block_2[0], block_1[0] = lax.optimization_barrier((mine, block_2[0], block_1[0]))
     other = swapped(mine, "groups", 1)
     rows_of = (mine, other), (swapped(mine, "head", 1), swapped(other, "head", 1))
     block_2 += held([passed(late, 2, 0, 0)], [], 100 * 2**33)
-    late = held([late], [block_2[1]])[0]
-    block_0[1] = late
-    block_1.append(passed(late, 1, 0, 0))
+    block_1.append(passed(after(late, block_2[0]), 1, 0, 0))
     block_3 = [passed(block, 1, 0, 0) for block in block_2]
+    block_3[0] = held([block_3[0]], [], 100 * 2**33)[0]
     parts = list(zip(block_0, block_1, block_2, block_3))
 
     cost = 100 * 2**33
     summed = []
+    given = []
     for part in parts:
-        near, far, near_given, far_given = terms(rows_of, part, role, first, cost)
-        across = swapped(near_given, "head", 2)
-        summed.append(((near, across), (swapped(far, "groups", 1), diagonal(far_given))))
+        near, far, near_given, far_given = terms(rows_of, part, role, first, cost, given)
+        given = [near_given]
+        arrived = [swapped(near_given, "head", 2), swapped(far, "groups", 1), diagonal(far_given)]
+        if not summed:
+            arrived = held(arrived, [], 100 * 2**33)
+        summed.append(((near, arrived[0]), arrived[1:]))
     return gated(gate_scale, summed, video)
 
 

time: 155 us -> 150 us (0.968)
  waiting for transfers between devices: 80 us -> 58.9 us
  starting transfers between devices: 45.1 us -> 54.1 us
  other arithmetic: 0.2 us -> 3.2 us
  local copies, waits for them, and re-layouts: 6.29 us -> 9.08 us
    ppermute x7, waiting for transfers between devices: 25.8 us -> 12.9 us  [passed(): return lax.ppermute(array, ('tm', 'head'), pairs)]
    ppermute x7, starting transfers between devices: 27 us -> 34.9 us  [swapped(): return lax.ppermute(array, axis, [(i, i ^ mask) for i in range(count)])]
    ppermute x4, waiting for transfers between devices: 48 us -> 40.6 us  [passed_along(): lax.ppermute(array, axis, [(i, (i + by) % count) for i in range(count)])]
    another operation x2, other arithmetic: 0.19 us -> 3.2 us  [square_mesh(): both = jnp.stack([half, passed(half, 0, 1, 1)])]
    ppermute x7, waiting for transfers between devices: 6.18 us -> 3.92 us  [swapped(): return lax.ppermute(array, axis, [(i, i ^ mask) for i in range(count)])]
    unnamed x32, local copies, waits for them, and re-layouts: 6.11 us -> 7.95 us
    ppermute x7, starting transfers between devices: 8.72 us -> 10.4 us  [passed(): return lax.ppermute(array, ('tm', 'head'), pairs)]
  transfers between devices with their start and end apart: 20 -> 20, of which waited for: 9 -> 10; matrix products, arithmetic and copies ran while one was open for 0% -> 2% of each run, Pallas kernels for 13% -> 14%
where the time goes in v4:
time: 150 us
  waiting for transfers between devices  58.9 us (39%)
  starting transfers between devices  54.1 us (36%)
  Pallas kernels  24.1 us (16%)
  local copies, waits for them, and re-layouts  9.08 us (6%)
  other arithmetic  3.2 us (2%)
    ppermute x4, waiting for transfers between devices, passed_along(): lax.ppermute(array, axis, [(i, (i + by) % count) for i in range(count)])  40.6 us
    ppermute x7, starting transfers between devices, swapped(): return lax.ppermute(array, axis, [(i, i ^ mask) for i in range(count)])  34.9 us
    pallas_call x3, Pallas kernels, local_call(): pl.pallas_call(body, out_shape=outs, in_specs=[SMEM] * len(flags) + [WHOL...  13.9 us
    ppermute x7, waiting for transfers between devices, passed(): return lax.ppermute(array, ('tm', 'head'), pairs)  12.9 us
    ppermute x7, starting transfers between devices, passed(): return lax.ppermute(array, ('tm', 'head'), pairs)  10.4 us
    pallas_call x1, Pallas kernels, attend(): pl.pallas_call(functools.partial(attend_kernel, len(key_slabs) // 2, 1.0...  10.2 us
    unnamed x32, local copies, waits for them, and re-layouts  7.95 us
    ppermute x4, starting transfers between devices, passed_along(): lax.ppermute(array, axis, [(i, (i + by) % count) for i in range(count)])  6.53 us
  transfers between devices with their start and end apart: 20, of which 10 were waited for; matrix products, arithmetic and copies ran while one was open for 2% of the time, Pallas kernels for 14%

profile of v4, /device:TPU:1, one launch (start us, length us, event | category | flops | bytes accessed | tf_op | source)
XLA Modules:
  0.0 149.6 jit_solution(7505304196358215028)
XLA Ops:
  0.0 1.5 %copy-done = bf16[768,1280]{1,0:T(8,128)(2,1)S(1)} copy-done((bf16[768,1280]{1,0:T(8,128)(2,1)S(1)}, bf16[768,1280]{1,0:T(8,128)(2,1)}, u32[]{:S(2)}) %copy-start) | copy-done | bytes 1966104
  2.6 2.9 %collective-permute-start.4 = (bf16[768,640]{1,0:T(8,128)(2,1)}, bf16[768,640]{1,0:T(8,128)(2,1)}, u32[]{:S(2)}, u32[]{:S(2)}) collective-permute-start(bf16[768,640]{1,0:T(8,128)(2,1)} %constant_dynamic-slice_fusion), channel_id=1, source_target_pairs={{1,0},{3,2},{4,5},{6,7},{9,8},{11,10},{12,13},{14,15},{17,16},{19,... | collective-permute-start | bytes 2949128 | tf_op jit(solution)/shard_map/ppermute | solution.py:248
  6.1 2.7 %collective-permute-start.1 = (bf16[384,6,128]{2,0,1:T(8,128)(2,1)S(1)}, bf16[384,6,128]{2,0,1:T(8,128)(2,1)}, u32[]{:S(2)}, u32[]{:S(2)}) collective-permute-start(bf16[384,6,128]{2,0,1:T(8,128)(2,1)S(1)} %copy-done.10), channel_id=1, source_target_pairs={{0,12},{4,0},{8,4},{12,8},{1,13},{5,1},{9,5},{13,9},{2,14},{6,2},{... | collective-permute-start | bytes 1769480 | tf_op jit(solution)/shard_map/ppermute | solution.py:17
  9.5 2.5 %collective-permute-start.3 = (bf16[384,6,128]{2,0,1:T(8,128)(2,1)}, bf16[384,6,128]{2,0,1:T(8,128)(2,1)}, u32[]{:S(2)}, u32[]{:S(2)}) collective-permute-start(bf16[384,6,128]{2,0,1:T(8,128)(2,1)} %param.8), channel_id=1, source_target_pairs={{0,12},{4,0},{8,4},{12,8},{1,13},{5,1},{9,5},{13,9},{2,14},{6,2},{... | collective-permute-start | bytes 1769480 | tf_op jit(solution)/shard_map/ppermute | solution.py:17
  12.2 1.9 %pad_maximum_fusion.refs_6_ = bf16[2,768,256]{2,1,0:T(8,128)(2,1)} fusion(bf16[1,768,640]{2,1,0:T(8,128)(2,1)} %bitcast.11, bf16[1,768,640]{2,1,0:T(8,128)(2,1)S(1)} %fusion.1), kind=kLoop, calls=%fused_computation.3 | loop fusion | flops 1572864 | bytes 2752512 | tf_op jit(solution)/shard_map/stack | solution.py:252
  14.2 1.3 fusion.refs_6_
  15.5 5.6 %collective-permute-done = bf16[384,6,128]{2,0,1:T(8,128)(2,1)S(1)} collective-permute-done((bf16[384,6,128]{2,0,1:T(8,128)(2,1)S(1)}, bf16[384,6,128]{2,0,1:T(8,128)(2,1)S(1)}, u32[]{:S(2)}, u32[]{:S(2)}) %collective-permute-start) | collective-permute-done | bytes 589856 | tf_op jit(solution)/shard_map/ppermute | solution.py:17
  21.9 14.9 %collective-permute-done.1 = bf16[384,6,128]{2,0,1:T(8,128)(2,1)} collective-permute-done((bf16[384,6,128]{2,0,1:T(8,128)(2,1)S(1)}, bf16[384,6,128]{2,0,1:T(8,128)(2,1)}, u32[]{:S(2)}, u32[]{:S(2)}) %collective-permute-start.1) | collective-permute-done | bytes 589856 | tf_op jit(solution)/shard_map/ppermute | solution.py:17
  36.8 1.7 %collective-permute-start.5 = (bf16[2,768,384]{2,1,0:T(8,128)(2,1)S(1)}, bf16[2,768,384]{2,1,0:T(8,128)(2,1)}, u32[]{:S(2)}, u32[]{:S(2)}) collective-permute-start(bf16[2,768,384]{2,1,0:T(8,128)(2,1)S(1)} %fusion.refs_6_), channel_id=1, source_target_pairs={{0,8},{2,10},{5,13},{7,15},{8,0},{10,2},{13,5},{15,7},{16,24},{18,... | collective-permute-start | bytes 3538952 | tf_op jit(solution)/shard_map/ppermute | solution.py:248
  38.5 1.3 collective-permute-start.6
  40.5 6.0 %collective-permute-done.2 = bf16[384,6,128]{2,0,1:T(8,128)(2,1)} collective-permute-done((bf16[384,6,128]{2,0,1:T(8,128)(2,1)}, bf16[384,6,128]{2,0,1:T(8,128)(2,1)}, u32[]{:S(2)}, u32[]{:S(2)}) %collective-permute-start.2) | collective-permute-done | bytes 589856 | tf_op jit(solution)/shard_map/ppermute | solution.py:17
  46.5 14.1 %collective-permute-done.3 = bf16[384,6,128]{2,0,1:T(8,128)(2,1)} collective-permute-done((bf16[384,6,128]{2,0,1:T(8,128)(2,1)}, bf16[384,6,128]{2,0,1:T(8,128)(2,1)}, u32[]{:S(2)}, u32[]{:S(2)}) %collective-permute-start.3) | collective-permute-done | bytes 589856 | tf_op jit(solution)/shard_map/ppermute | solution.py:17
  61.7 10.2 %attend.1.refs_2_ = bf16[384,768]{1,0:T(8,128)(2,1)} custom-call(f32[3,1152]{1,0:T(4,128)S(1)} %bitcast.18, bf16[6,384,128]{2,1,0:T(8,128)(2,1)S(1)} %bitcast.19, bf16[6,384,128]{2,1,0:T(8,128)(2,1)S(1)} %bitcast.21, bf16[6,384,128]{2,1,0:T(8,128)(2,1)S(1)} %bitcast.20, bf16[6,384,128]{2,1,0:T(8,128)(2,1)} %bitcast.6.refs_2_, ...), custom_call_target="tpu_custom_call" | custom-call | flops 20000000000 | bytes 10000000 | tf_op jit(solution)/shard_map/attend/pallas_call | solution.py:56
  71.9 1.6 %collective-permute-done.6.refs_7_ = bf16[2,768,384]{2,1,0:T(8,128)(2,1)S(1)} collective-permute-done((bf16[2,768,384]{2,1,0:T(8,128)(2,1)S(1)}, bf16[2,768,384]{2,1,0:T(8,128)(2,1)S(1)}, u32[]{:S(2)}, u32[]{:S(2)}) %collective-permute-start.6) | collective-permute-done | bytes 1179680 | tf_op jit(solution)/shard_map/ppermute | solution.py:248
  74.5 2.0 %collective-permute-start.7 = (bf16[384,768]{1,0:T(8,128)(2,1)}, bf16[384,768]{1,0:T(8,128)(2,1)}, u32[]{:S(2)}, u32[]{:S(2)}) collective-permute-start(bf16[384,768]{1,0:T(8,128)(2,1)} %attend.1.refs_2_), channel_id=1, source_target_pairs={{0,16},{16,0},{1,17},{17,1},{2,18},{18,2},{3,19},{19,3},{4,20},{20... | collective-permute-start | bytes 1769480 | tf_op jit(solution)/shard_map/ppermute | solution.py:22
  76.5 1.3 collective-permute-start.10
  78.7 1.3 collective-permute-start.16
  80.0 26.3 %collective-permute-start.8 = (bf16[384,768]{1,0:T(8,128)(2,1)}, bf16[384,768]{1,0:T(8,128)(2,1)}, u32[]{:S(2)}, u32[]{:S(2)}) collective-permute-start(bf16[384,768]{1,0:T(8,128)(2,1)} %attend.1.refs_2_), channel_id=1, source_target_pairs={{0,1},{1,0},{2,3},{3,2},{4,5},{5,4},{6,7},{7,6},{8,9},{9,8},{10,11... | collective-permute-start | bytes 1769480 | tf_op jit(solution)/shard_map/ppermute | solution.py:22
  106.3 1.3 collective-permute-start.14
  108.5 6.6 %collective-permute-done.10.refs_0_ = bf16[2,768,384]{2,1,0:T(8,128)(2,1)} collective-permute-done((bf16[2,768,384]{2,1,0:T(8,128)(2,1)}, bf16[2,768,384]{2,1,0:T(8,128)(2,1)}, u32[]{:S(2)}, u32[]{:S(2)}) %collective-permute-start.10) | collective-permute-done | bytes 1179680 | tf_op jit(solution)/shard_map/ppermute | solution.py:248
  115.2 1.3 copy-done.2
  116.4 1.3 copy-done.6
  117.7 5.7 %terms.2 = (f32[384,384]{1,0:T(8,128)S(1)}, bf16[384,384]{1,0:T(8,128)(2,1)}, bf16[384,384]{1,0:T(8,128)(2,1)}, bf16[384,384]{1,0:T(8,128)(2,1)}) custom-call(s32[1]{0:T(128)} %bitcast.1.refs_0_, s32[1]{0:T(128)} %bitcast.2.refs_1_, bf16[384,768]{1,0:T(8,128)(2,1)} %attend.1.refs_2_, bf16[384,768]{1,0:T(8,128)(2,1)} %collective-permute-done.7.refs_3_, ...), custom_call_target="tpu_custom_call" | custom-call | flops 858993459200 | bytes 8552448 | tf_op jit(solution)/shard_map/terms/pallas_call | solution.py:122
  123.5 2.8 %collective-permute-start.12 = (bf16[384,384]{1,0:T(8,128)(2,1)}, bf16[384,384]{1,0:T(8,128)(2,1)}, u32[]{:S(2)}, u32[]{:S(2)}) collective-permute-start(bf16[384,384]{1,0:T(8,128)(2,1)} %get-tuple-element.28), channel_id=1, source_target_pairs={{0,16},{16,0},{1,17},{17,1},{2,18},{18,2},{3,19},{19,3},{4,20},{20... | collective-permute-start | bytes 884744 | tf_op jit(solution)/shard_map/ppermute | solution.py:22
  126.3 1.1 collective-permute-start.13
  127.4 4.6 %collective-permute-done.14.refs_7_ = bf16[2,768,256]{2,1,0:T(8,128)(2,1)} collective-permute-done((bf16[2,768,256]{2,1,0:T(8,128)(2,1)}, bf16[2,768,256]{2,1,0:T(8,128)(2,1)}, u32[]{:S(2)}, u32[]{:S(2)}) %collective-permute-start.14) | collective-permute-done | bytes 786464 | tf_op jit(solution)/shard_map/ppermute | solution.py:248
  132.0 5.6 %terms.3 = (f32[384,256]{1,0:T(8,128)S(1)}, bf16[384,256]{1,0:T(8,128)(2,1)}, bf16[384,256]{1,0:T(8,128)(2,1)}, bf16[384,256]{1,0:T(8,128)(2,1)}) custom-call(s32[1]{0:T(128)} %bitcast.1.refs_0_, s32[1]{0:T(128)} %bitcast.2.refs_1_, bf16[384,768]{1,0:T(8,128)(2,1)} %attend.1.refs_2_, bf16[384,768]{1,0:T(8,128)(2,1)} %collective-permute-done.7.refs_3_, ...), custom_call_target="tpu_custom_call" | custom-call | flops 858993459200 | bytes 6488064 | tf_op jit(solution)/shard_map/terms/pallas_call | solution.py:122
  137.7 2.8 %collective-permute-start.18 = (bf16[384,256]{1,0:T(8,128)(2,1)}, bf16[384,256]{1,0:T(8,128)(2,1)}, u32[]{:S(2)}, u32[]{:S(2)}) collective-permute-start(bf16[384,256]{1,0:T(8,128)(2,1)} %get-tuple-element.37), channel_id=1, source_target_pairs={{0,16},{16,0},{1,17},{17,1},{2,18},{18,2},{3,19},{19,3},{4,20},{20... | collective-permute-start | bytes 589832 | tf_op jit(solution)/shard_map/ppermute | solution.py:22
  140.5 1.1 collective-permute-start.19
  142.5 3.0 %collective-permute-done.18.refs_8_ = bf16[384,256]{1,0:T(8,128)(2,1)} collective-permute-done((bf16[384,256]{1,0:T(8,128)(2,1)}, bf16[384,256]{1,0:T(8,128)(2,1)}, u32[]{:S(2)}, u32[]{:S(2)}) %collective-permute-start.18) | collective-permute-done | bytes 196640 | tf_op jit(solution)/shard_map/ppermute | solution.py:22
  145.5 1.5 %collective-permute-done.19.refs_9_ = bf16[384,256]{1,0:T(8,128)(2,1)} collective-permute-done((bf16[384,256]{1,0:T(8,128)(2,1)}, bf16[384,256]{1,0:T(8,128)(2,1)}, u32[]{:S(2)}, u32[]{:S(2)}) %collective-permute-start.19) | collective-permute-done | bytes 196640 | tf_op jit(solution)/shard_map/ppermute | solution.py:80
  147.0 2.6 %gated.1 = bf16[384,1280]{1,0:T(8,128)(2,1)} custom-call(s32[1]{0:T(128)} %bitcast.refs_0_, f32[1,1280]{1,0:T(1,128)S(1)} %reshape.20.refs_1_, f32[384,384]{1,0:T(8,128)S(1)} %copy-done.4, bf16[384,384]{1,0:T(8,128)(2,1)} %get-tuple-element.30.refs_3_, bf16[384,384]{1,0:T(8,128)(2,1)} %get-tuple-element.31.refs_4_, ...), custom_call_target="tpu_custom_call" | custom-call | bytes 3445760 | tf_op jit(solution)/shard_map/gated/pallas_call | solution.py:122
  (53 shorter events, 9.2 us)
Async XLA Ops:
  0.0 1.5 %copy-start = (bf16[768,1280]{1,0:T(8,128)(2,1)S(1)}, bf16[768,1280]{1,0:T(8,128)(2,1)}, u32[]{:S(2)}) copy-start(bf16[768,1280]{1,0:T(8,128)(2,1)} %param.10) | copy-start | bytes 5898244
  0.0 5.5 %copy-start.10 = (bf16[384,6,128]{2,0,1:T(8,128)(2,1)S(1)}, bf16[384,6,128]{2,0,1:T(8,128)(2,1)}, u32[]{:S(2)}) copy-start(bf16[384,6,128]{2,0,1:T(8,128)(2,1)} %param.7) | copy-start | bytes 1769476
  0.0 12.0 %copy-start.13 = (f32[1280]{0:T(1024)S(1)}, f32[1280]{0:T(1024)}, u32[]{:S(2)}) copy-start(f32[1280]{0:T(1024)} %param.11) | copy-start | bytes 15364
  0.0 12.0 %copy-start.14 = (s32[3,9]{1,0:T(4,128)S(1)}, s32[3,9]{1,0:T(4,128)}, u32[]{:S(2)}) copy-start(s32[3,9]{1,0:T(4,128)} %param.9) | copy-start | bytes 328
  2.6 9.7 %collective-permute-start.4 = (bf16[768,640]{1,0:T(8,128)(2,1)}, bf16[768,640]{1,0:T(8,128)(2,1)}, u32[]{:S(2)}, u32[]{:S(2)}) collective-permute-start(bf16[768,640]{1,0:T(8,128)(2,1)} %constant_dynamic-slice_fusion), channel_id=1, source_target_pairs={{1,0},{3,2},{4,5},{6,7},{9,8},{11,10},{12,13},{14,15},{17,16},{19,... | collective-permute-start | bytes 2949128 | tf_op jit(solution)/shard_map/ppermute | solution.py:248
  5.5 15.6 %collective-permute-start = (bf16[384,6,128]{2,0,1:T(8,128)(2,1)S(1)}, bf16[384,6,128]{2,0,1:T(8,128)(2,1)S(1)}, u32[]{:S(2)}, u32[]{:S(2)}) collective-permute-start(bf16[384,6,128]{2,0,1:T(8,128)(2,1)S(1)} %copy-done.10), channel_id=1, source_target_pairs={{0,4},{4,8},{8,12},{12,0},{1,5},{5,9},{9,13},{13,1},{2,6},{6,10},{... | collective-permute-start | bytes 1769480 | tf_op jit(solution)/shard_map/ppermute | solution.py:17
  6.1 30.7 %collective-permute-start.1 = (bf16[384,6,128]{2,0,1:T(8,128)(2,1)S(1)}, bf16[384,6,128]{2,0,1:T(8,128)(2,1)}, u32[]{:S(2)}, u32[]{:S(2)}) collective-permute-start(bf16[384,6,128]{2,0,1:T(8,128)(2,1)S(1)} %copy-done.10), channel_id=1, source_target_pairs={{0,12},{4,0},{8,4},{12,8},{1,13},{5,1},{9,5},{13,9},{2,14},{6,2},{... | collective-permute-start | bytes 1769480 | tf_op jit(solution)/shard_map/ppermute | solution.py:17
  8.8 37.8 %collective-permute-start.2 = (bf16[384,6,128]{2,0,1:T(8,128)(2,1)}, bf16[384,6,128]{2,0,1:T(8,128)(2,1)}, u32[]{:S(2)}, u32[]{:S(2)}) collective-permute-start(bf16[384,6,128]{2,0,1:T(8,128)(2,1)} %param.8), channel_id=1, source_target_pairs={{0,4},{4,8},{8,12},{12,0},{1,5},{5,9},{9,13},{13,1},{2,6},{6,10},{... | collective-permute-start | bytes 1769480 | tf_op jit(solution)/shard_map/ppermute | solution.py:17
  9.5 51.1 %collective-permute-start.3 = (bf16[384,6,128]{2,0,1:T(8,128)(2,1)}, bf16[384,6,128]{2,0,1:T(8,128)(2,1)}, u32[]{:S(2)}, u32[]{:S(2)}) collective-permute-start(bf16[384,6,128]{2,0,1:T(8,128)(2,1)} %param.8), channel_id=1, source_target_pairs={{0,12},{4,0},{8,4},{12,8},{1,13},{5,1},{9,5},{13,9},{2,14},{6,2},{... | collective-permute-start | bytes 1769480 | tf_op jit(solution)/shard_map/ppermute | solution.py:17
  14.2 46.4 %copy-start.9 = (bf16[384,6,128]{2,0,1:T(8,128)(2,1)S(1)}, bf16[384,6,128]{2,0,1:T(8,128)(2,1)}, u32[]{:S(2)}) copy-start(bf16[384,6,128]{2,0,1:T(8,128)(2,1)} %param.6) | copy-start | bytes 1769476
  15.4 56.4 %copy-start.1 = (bf16[2,768,384]{2,1,0:T(8,128)(2,1)}, bf16[2,768,384]{2,1,0:T(8,128)(2,1)S(1)}, u32[]{:S(2)}) copy-start(bf16[2,768,384]{2,1,0:T(8,128)(2,1)S(1)} %fusion.refs_6_) | copy-start | bytes 3538948
  36.8 35.1 %collective-permute-start.5 = (bf16[2,768,384]{2,1,0:T(8,128)(2,1)S(1)}, bf16[2,768,384]{2,1,0:T(8,128)(2,1)}, u32[]{:S(2)}, u32[]{:S(2)}) collective-permute-start(bf16[2,768,384]{2,1,0:T(8,128)(2,1)S(1)} %fusion.refs_6_), channel_id=1, source_target_pairs={{0,8},{2,10},{5,13},{7,15},{8,0},{10,2},{13,5},{15,7},{16,24},{18,... | collective-permute-start | bytes 3538952 | tf_op jit(solution)/shard_map/ppermute | solution.py:248
  38.5 35.0 %collective-permute-start.6 = (bf16[2,768,384]{2,1,0:T(8,128)(2,1)S(1)}, bf16[2,768,384]{2,1,0:T(8,128)(2,1)S(1)}, u32[]{:S(2)}, u32[]{:S(2)}) collective-permute-start(bf16[2,768,384]{2,1,0:T(8,128)(2,1)S(1)} %fusion.refs_6_), channel_id=1, source_target_pairs={{0,4},{2,6},{5,1},{7,3},{8,12},{10,14},{13,9},{15,11},{16,20},{18,... | collective-permute-start | bytes 3538952 | tf_op jit(solution)/shard_map/ppermute | solution.py:248
  39.8 38.1 %collective-permute-start.15 = (bf16[2,768,256]{2,1,0:T(8,128)(2,1)}, bf16[2,768,256]{2,1,0:T(8,128)(2,1)S(1)}, u32[]{:S(2)}, u32[]{:S(2)}) collective-permute-start(bf16[2,768,256]{2,1,0:T(8,128)(2,1)} %pad_maximum_fusion.refs_6_), channel_id=1, source_target_pairs={{0,8},{2,10},{5,13},{7,15},{8,0},{10,2},{13,5},{15,7},{16,24},{18,... | collective-permute-start | bytes 2359304 | tf_op jit(solution)/shard_map/ppermute | solution.py:248
  60.6 1.1 copy-start.12
  74.5 33.0 %collective-permute-start.7 = (bf16[384,768]{1,0:T(8,128)(2,1)}, bf16[384,768]{1,0:T(8,128)(2,1)}, u32[]{:S(2)}, u32[]{:S(2)}) collective-permute-start(bf16[384,768]{1,0:T(8,128)(2,1)} %attend.1.refs_2_), channel_id=1, source_target_pairs={{0,16},{16,0},{1,17},{17,1},{2,18},{18,2},{3,19},{19,3},{4,20},{20... | collective-permute-start | bytes 1769480 | tf_op jit(solution)/shard_map/ppermute | solution.py:22
  76.5 38.6 %collective-permute-start.10 = (bf16[2,768,384]{2,1,0:T(8,128)(2,1)}, bf16[2,768,384]{2,1,0:T(8,128)(2,1)}, u32[]{:S(2)}, u32[]{:S(2)}) collective-permute-start(bf16[2,768,384]{2,1,0:T(8,128)(2,1)} %collective-permute-done.5.refs_8_), channel_id=1, source_target_pairs={{0,4},{2,6},{5,1},{7,3},{8,12},{10,14},{13,9},{15,11},{16,20},{18,... | collective-permute-start | bytes 3538952 | tf_op jit(solution)/shard_map/ppermute | solution.py:248
  78.7 48.7 %collective-permute-start.16 = (bf16[2,768,256]{2,1,0:T(8,128)(2,1)}, bf16[2,768,256]{2,1,0:T(8,128)(2,1)}, u32[]{:S(2)}, u32[]{:S(2)}) collective-permute-start(bf16[2,768,256]{2,1,0:T(8,128)(2,1)} %held.5.refs_8_), channel_id=1, source_target_pairs={{0,4},{2,6},{5,1},{7,3},{8,12},{10,14},{13,9},{15,11},{16,20},{18,... | collective-permute-start | bytes 2359304 | tf_op jit(solution)/shard_map/ppermute | solution.py:248
  80.0 35.1 %collective-permute-start.8 = (bf16[384,768]{1,0:T(8,128)(2,1)}, bf16[384,768]{1,0:T(8,128)(2,1)}, u32[]{:S(2)}, u32[]{:S(2)}) collective-permute-start(bf16[384,768]{1,0:T(8,128)(2,1)} %attend.1.refs_2_), channel_id=1, source_target_pairs={{0,1},{1,0},{2,3},{3,2},{4,5},{5,4},{6,7},{7,6},{8,9},{9,8},{10,11... | collective-permute-start | bytes 1769480 | tf_op jit(solution)/shard_map/ppermute | solution.py:22
  106.3 25.7 %collective-permute-start.14 = (bf16[2,768,256]{2,1,0:T(8,128)(2,1)}, bf16[2,768,256]{2,1,0:T(8,128)(2,1)}, u32[]{:S(2)}, u32[]{:S(2)}) collective-permute-start(bf16[2,768,256]{2,1,0:T(8,128)(2,1)} %pad_maximum_fusion.refs_6_), channel_id=1, source_target_pairs={{0,4},{2,6},{5,1},{7,3},{8,12},{10,14},{13,9},{15,11},{16,20},{18,... | collective-permute-start | bytes 2359304 | tf_op jit(solution)/shard_map/ppermute | solution.py:248
  107.6 7.6 %collective-permute-start.9 = (bf16[384,768]{1,0:T(8,128)(2,1)}, bf16[384,768]{1,0:T(8,128)(2,1)}, u32[]{:S(2)}, u32[]{:S(2)}) collective-permute-start(bf16[384,768]{1,0:T(8,128)(2,1)} %collective-permute-done.7.refs_3_), channel_id=1, source_target_pairs={{0,1},{1,0},{2,3},{3,2},{4,5},{5,4},{6,7},{7,6},{8,9},{9,8},{10,11... | collective-permute-start | bytes 1769480 | tf_op jit(solution)/shard_map/ppermute | solution.py:22
  115.1 1.3 copy-start.2
  116.4 1.3 copy-start.6
  117.7 14.3 %copy-start.8 = (bf16[2,768,256]{2,1,0:T(8,128)(2,1)S(1)}, bf16[2,768,256]{2,1,0:T(8,128)(2,1)}, u32[]{:S(2)}) copy-start(bf16[2,768,256]{2,1,0:T(8,128)(2,1)} %held.5.refs_8_) | copy-start | bytes 2359300
  123.4 14.2 %copy-start.3 = (f32[384,384]{1,0:T(8,128)}, f32[384,384]{1,0:T(8,128)S(1)}, u32[]{:S(2)}) copy-start(f32[384,384]{1,0:T(8,128)S(1)} %get-tuple-element.26.refs_2_) | copy-start | bytes 1769476
  123.4 17.0 %collective-permute-start.11 = (bf16[384,384]{1,0:T(8,128)(2,1)}, bf16[384,384]{1,0:T(8,128)(2,1)}, u32[]{:S(2)}, u32[]{:S(2)}) collective-permute-start(bf16[384,384]{1,0:T(8,128)(2,1)} %get-tuple-element.27.refs_10_), channel_id=1, source_target_pairs={{0,2},{1,3},{2,0},{3,1},{4,6},{5,7},{6,4},{7,5},{8,10},{9,11},{10,... | collective-permute-start | bytes 884744 | tf_op jit(solution)/shard_map/ppermute | solution.py:22
  123.5 18.1 %collective-permute-start.12 = (bf16[384,384]{1,0:T(8,128)(2,1)}, bf16[384,384]{1,0:T(8,128)(2,1)}, u32[]{:S(2)}, u32[]{:S(2)}) collective-permute-start(bf16[384,384]{1,0:T(8,128)(2,1)} %get-tuple-element.28), channel_id=1, source_target_pairs={{0,16},{16,0},{1,17},{17,1},{2,18},{18,2},{3,19},{19,3},{4,20},{20... | collective-permute-start | bytes 884744 | tf_op jit(solution)/shard_map/ppermute | solution.py:22
  126.3 15.3 %collective-permute-start.13 = (bf16[384,384]{1,0:T(8,128)(2,1)}, bf16[384,384]{1,0:T(8,128)(2,1)}, u32[]{:S(2)}, u32[]{:S(2)}) collective-permute-start(bf16[384,384]{1,0:T(8,128)(2,1)} %get-tuple-element.29), channel_id=1, source_target_pairs={{0,18},{1,19},{2,16},{3,17},{16,2},{17,3},{18,0},{19,1},{4,22},{5,... | collective-permute-start | bytes 884744 | tf_op jit(solution)/shard_map/ppermute | solution.py:80
  137.6 4.9 %collective-permute-start.17 = (bf16[384,256]{1,0:T(8,128)(2,1)}, bf16[384,256]{1,0:T(8,128)(2,1)}, u32[]{:S(2)}, u32[]{:S(2)}) collective-permute-start(bf16[384,256]{1,0:T(8,128)(2,1)} %get-tuple-element.36), channel_id=1, source_target_pairs={{0,2},{1,3},{2,0},{3,1},{4,6},{5,7},{6,4},{7,5},{8,10},{9,11},{10,... | collective-permute-start | bytes 589832 | tf_op jit(solution)/shard_map/ppermute | solution.py:22
  137.7 7.8 %collective-permute-start.18 = (bf16[384,256]{1,0:T(8,128)(2,1)}, bf16[384,256]{1,0:T(8,128)(2,1)}, u32[]{:S(2)}, u32[]{:S(2)}) collective-permute-start(bf16[384,256]{1,0:T(8,128)(2,1)} %get-tuple-element.37), channel_id=1, source_target_pairs={{0,16},{16,0},{1,17},{17,1},{2,18},{18,2},{3,19},{19,3},{4,20},{20... | collective-permute-start | bytes 589832 | tf_op jit(solution)/shard_map/ppermute | solution.py:22
  140.5 6.6 %collective-permute-start.19 = (bf16[384,256]{1,0:T(8,128)(2,1)}, bf16[384,256]{1,0:T(8,128)(2,1)}, u32[]{:S(2)}, u32[]{:S(2)}) collective-permute-start(bf16[384,256]{1,0:T(8,128)(2,1)} %get-tuple-element.38), channel_id=1, source_target_pairs={{0,18},{1,19},{2,16},{3,17},{16,2},{17,3},{18,0},{19,1},{4,22},{5,... | collective-permute-start | bytes 589832 | tf_op jit(solution)/shard_map/ppermute | solution.py:80
  141.6 5.5 %copy-start.4 = (f32[384,384]{1,0:T(8,128)S(1)}, f32[384,384]{1,0:T(8,128)}, u32[]{:S(2)}) copy-start(f32[384,384]{1,0:T(8,128)} %copy-done.3) | copy-start | bytes 1769476
  (3 other events, 2.7 us)

commit v5 on v4

--- a/solution.py
+++ b/solution.py
@@ -9,7 +9,7 @@
 from jax.sharding import PartitionSpec as P
 
 TILE = 128
-CUT = 256
+STARTS = 0, 2
 
 
 def passed_along(array, axis, by):
@@ -135,7 +135,9 @@
 
 def terms(rows_of, blocks, role, first, cost, earlier=()):
     rows, depth = rows_of[0][0].shape
-    width = blocks[0].shape[2]
+    width = blocks[0][0].shape[2]
+    starts = [column for _, column in blocks]
+    blocks = [block for block, _ in blocks]
     flat = [array for core in rows_of for array in core]
 
     def kernel(role_ref, first_ref, *refs):
@@ -146,7 +148,7 @@
         def weight_copies(slot, index):
             return [
                 pltpu.make_async_copy(
-                    block_refs[index].at[core],
+                    block_refs[index].at[core, :, pl.ds(starts[index], width)],
                     weight.at[slot, pl.ds(core * depth, depth)],
                     landed.at[4 + 2 * slot + core],
                 )
@@ -234,7 +236,8 @@
     slab = lax.axis_index("tm")
     head = lax.axis_index("head")
     width = out_weight.shape[1] // 2
-    cut = width - CUT
+    starts = [width * place // 5 // TILE * TILE for place in STARTS]
+    spans = list(zip(starts, starts[1:] + [width]))
     role = (slab ^ head) & 1
     first = slab // 2 == head // 2
 
@@ -250,21 +253,25 @@
     lower, upper = halo(key_rows, value_rows)
     half = lax.dynamic_slice_in_dim(out_weight, video * width, width, 1)
     both = jnp.stack([half, passed(half, 0, 1, 1)])
-    early, late = lax.optimization_barrier((both[..., :cut], both[..., cut:], lower[-1][0], upper[0][0]))[:2]
-    block_0 = [early, late]
-    block_2 = [passed(early, 2, 0, 0)]
-    block_1 = [passed(early, 1, 0, 0)]
+    both, *block_0 = lax.optimization_barrier(
+        (both, *[both[..., start:end] for start, end in spans], lower[-1][0], upper[0][0])
+    )[: len(spans) + 1]
+    block_2 = [passed(part, 2, 0, 0) for part in block_0]
+    block_1 = passed(both, 1, 0, 0)
 
     key_slabs, value_slabs = all_slabs(lower, (key_rows, value_rows), upper)
     mine = attend(queries, key_slabs, value_slabs, keep_tiles)
-    mine, block_2[0], block_1[0] = lax.optimization_barrier((mine, block_2[0], block_1[0]))
+    to_core = mine
+    block_2[0], block_1 = lax.optimization_barrier((block_2[0], block_1))
     other = swapped(mine, "groups", 1)
-    rows_of = (mine, other), (swapped(mine, "head", 1), swapped(other, "head", 1))
-    block_2 += held([passed(late, 2, 0, 0)], [], 100 * 2**33)
-    block_1.append(passed(after(late, block_2[0]), 1, 0, 0))
+    rows_of = (mine, other), (swapped(to_core, "head", 1), swapped(other, "head", 1))
+    block_2[1:] = [held([block], [], 100 * 2**33)[0] for block in block_2[1:]]
     block_3 = [passed(block, 1, 0, 0) for block in block_2]
     block_3[0] = held([block_3[0]], [], 100 * 2**33)[0]
-    parts = list(zip(block_0, block_1, block_2, block_3))
+    parts = [
+        [(block_0[i], 0), (block_1, spans[i][0]), (block_2[i], 0), (block_3[i], 0)]
+        for i in range(len(spans))
+    ]
 
     cost = 100 * 2**33
     summed = []
@@ -273,7 +280,7 @@
         near, far, near_given, far_given = terms(rows_of, part, role, first, cost, given)
         given = [near_given]
         arrived = [swapped(near_given, "head", 2), swapped(far, "groups", 1), diagonal(far_given)]
-        if not summed:
+        if len(summed) < len(parts) - 1:
             arrived = held(arrived, [], 100 * 2**33)
         summed.append(((near, arrived[0]), arrived[1:]))
     return gated(gate_scale, summed, video)

time: 150 us -> 147 us (0.980)
  waiting for transfers between devices: 58.9 us -> 89.6 us
  starting transfers between devices: 54.1 us -> 27.7 us
  local copies, waits for them, and re-layouts: 9.08 us -> 2.64 us
    ppermute x7, starting transfers between devices: 34.9 us -> 11.7 us  [swapped(): return lax.ppermute(array, axis, [(i, i ^ mask) for i in range(count)])]
    ppermute x7 -> x6, waiting for transfers between devices: 12.9 us -> 30 us  [passed(): return lax.ppermute(array, ('tm', 'head'), pairs)]
    ppermute x7, waiting for transfers between devices: 3.92 us -> 18.3 us  [swapped(): return lax.ppermute(array, axis, [(i, i ^ mask) for i in range(count)])]
    unnamed x32 -> x14, local copies, waits for them, and re-layouts: 7.95 us -> 2.46 us
    ppermute x2, starting transfers between devices: 2.21 us -> 0.02 us  [diagonal(): return lax.ppermute(array, ('groups', 'head'), pairs)]
    ppermute x2, waiting for transfers between devices: 1.54 us -> 0.01 us  [diagonal(): return lax.ppermute(array, ('groups', 'head'), pairs)]
    ppermute x7 -> x6, starting transfers between devices: 10.4 us -> 9.1 us  [passed(): return lax.ppermute(array, ('tm', 'head'), pairs)]
    another operation x2 -> x3, other arithmetic: 3.2 us -> 2.57 us  [square_mesh(): both = jnp.stack([half, passed(half, 0, 1, 1)])]
  transfers between devices with their start and end apart: 20 -> 19, of which waited for: 10 -> 10; matrix products, arithmetic and copies ran while one was open for 2% -> 2% of each run, Pallas kernels for 14% -> 15%
where the time goes in v5:
time: 147 us
  waiting for transfers between devices  89.6 us (61%)
  starting transfers between devices  27.7 us (19%)
  Pallas kernels  24.4 us (17%)
  local copies, waits for them, and re-layouts  2.64 us (2%)
  other arithmetic  2.58 us (2%)
    ppermute x4, waiting for transfers between devices, passed_along(): lax.ppermute(array, axis, [(i, (i + by) % count) for i in range(count)])  41.3 us
    ppermute x6, waiting for transfers between devices, passed(): return lax.ppermute(array, ('tm', 'head'), pairs)  30 us
    ppermute x7, waiting for transfers between devices, swapped(): return lax.ppermute(array, axis, [(i, i ^ mask) for i in range(count)])  18.3 us
    pallas_call x3, Pallas kernels, local_call(): pl.pallas_call(body, out_shape=outs, in_specs=[SMEM] * len(flags) + [WHOL...  14.3 us
    ppermute x7, starting transfers between devices, swapped(): return lax.ppermute(array, axis, [(i, i ^ mask) for i in range(count)])  11.7 us
    pallas_call x1, Pallas kernels, attend(): pl.pallas_call(functools.partial(attend_kernel, len(key_slabs) // 2, 1.0...  10.1 us
    ppermute x6, starting transfers between devices, passed(): return lax.ppermute(array, ('tm', 'head'), pairs)  9.1 us
    ppermute x4, starting transfers between devices, passed_along(): lax.ppermute(array, axis, [(i, (i + by) % count) for i in range(count)])  6.8 us
  transfers between devices with their start and end apart: 19, of which 10 were waited for; matrix products, arithmetic and copies ran while one was open for 2% of the time, Pallas kernels for 15%

profile of v5, /device:TPU:1, one launch (start us, length us, event | category | flops | bytes accessed | tf_op | source)
XLA Modules:
  0.0 147.1 jit_solution(1444219154455804033)
XLA Ops:
  0.0 1.5 %copy-done = bf16[768,1280]{1,0:T(8,128)(2,1)S(1)} copy-done((bf16[768,1280]{1,0:T(8,128)(2,1)S(1)}, bf16[768,1280]{1,0:T(8,128)(2,1)}, u32[]{:S(2)}) %copy-start) | copy-done | bytes 1966104
  1.6 2.0 %collective-permute-start.7 = (bf16[768,640]{1,0:T(8,128)(2,1)S(1)}, bf16[768,640]{1,0:T(8,128)(2,1)S(1)}, u32[]{:S(2)}, u32[]{:S(2)}) collective-permute-start(bf16[768,640]{1,0:T(8,128)(2,1)S(1)} %constant_dynamic-slice_fusion), channel_id=1, source_target_pairs={{1,0},{3,2},{4,5},{6,7},{9,8},{11,10},{12,13},{14,15},{17,16},{19,... | collective-permute-start | bytes 2949128 | tf_op jit(solution)/shard_map/ppermute | solution.py:251
  3.7 1.4 collective-permute-start
  5.1 2.1 %collective-permute-start.1 = (bf16[384,6,128]{2,0,1:T(8,128)(2,1)}, bf16[384,6,128]{2,0,1:T(8,128)(2,1)S(1)}, u32[]{:S(2)}, u32[]{:S(2)}) collective-permute-start(bf16[384,6,128]{2,0,1:T(8,128)(2,1)} %param.7), channel_id=1, source_target_pairs={{0,12},{4,0},{8,4},{12,8},{1,13},{5,1},{9,5},{13,9},{2,14},{6,2},{... | collective-permute-start | bytes 1769480 | tf_op jit(solution)/shard_map/ppermute | solution.py:17
  7.8 2.7 %collective-permute-start.3 = (bf16[384,6,128]{2,0,1:T(8,128)(2,1)}, bf16[384,6,128]{2,0,1:T(8,128)(2,1)S(1)}, u32[]{:S(2)}, u32[]{:S(2)}) collective-permute-start(bf16[384,6,128]{2,0,1:T(8,128)(2,1)} %param.8), channel_id=1, source_target_pairs={{0,12},{4,0},{8,4},{12,8},{1,13},{5,1},{9,5},{13,9},{2,14},{6,2},{... | collective-permute-start | bytes 1769480 | tf_op jit(solution)/shard_map/ppermute | solution.py:17
  11.8 1.5 %pad_maximum_fusion = bf16[2,768,640]{2,1,0:T(8,128)(2,1)} fusion(bf16[1,768,640]{2,1,0:T(8,128)(2,1)S(1)} %bitcast.26, bf16[1,768,640]{2,1,0:T(8,128)(2,1)S(1)} %fusion.2), kind=kLoop, calls=%fused_computation.2 | loop fusion | flops 983040 | bytes 3932160 | tf_op jit(solution)/shard_map/stack | solution.py:255
  13.3 6.6 %collective-permute-done = bf16[384,6,128]{2,0,1:T(8,128)(2,1)S(1)} collective-permute-done((bf16[384,6,128]{2,0,1:T(8,128)(2,1)}, bf16[384,6,128]{2,0,1:T(8,128)(2,1)S(1)}, u32[]{:S(2)}, u32[]{:S(2)}) %collective-permute-start) | collective-permute-done | bytes 589856 | tf_op jit(solution)/shard_map/ppermute | solution.py:17
  19.9 15.2 %collective-permute-done.1 = bf16[384,6,128]{2,0,1:T(8,128)(2,1)S(1)} collective-permute-done((bf16[384,6,128]{2,0,1:T(8,128)(2,1)}, bf16[384,6,128]{2,0,1:T(8,128)(2,1)S(1)}, u32[]{:S(2)}, u32[]{:S(2)}) %collective-permute-start.1) | collective-permute-done | bytes 589856 | tf_op jit(solution)/shard_map/ppermute | solution.py:17
  35.1 1.6 %collective-permute-start.8 = (bf16[2,768,256]{2,1,0:T(8,128)(2,1)}, bf16[2,768,256]{2,1,0:T(8,128)(2,1)}, u32[]{:S(2)}, u32[]{:S(2)}) collective-permute-start(bf16[2,768,256]{2,1,0:T(8,128)(2,1)} %fusion.1.refs_6_), channel_id=1, source_target_pairs={{0,8},{2,10},{5,13},{7,15},{8,0},{10,2},{13,5},{15,7},{16,24},{18,... | collective-permute-start | bytes 2359304 | tf_op jit(solution)/shard_map/ppermute | solution.py:251
  36.7 1.3 collective-permute-start.9
  38.0 1.7 %collective-permute-start.14 = (bf16[2,768,384]{2,1,0:T(8,128)(2,1)S(1)}, bf16[2,768,384]{2,1,0:T(8,128)(2,1)}, u32[]{:S(2)}, u32[]{:S(2)}) collective-permute-start(bf16[2,768,384]{2,1,0:T(8,128)(2,1)S(1)} %fusion.refs_6_), channel_id=1, source_target_pairs={{0,8},{2,10},{5,13},{7,15},{8,0},{10,2},{13,5},{15,7},{16,24},{18,... | collective-permute-start | bytes 3538952 | tf_op jit(solution)/shard_map/ppermute | solution.py:251
  39.6 5.6 %collective-permute-done.2 = bf16[384,6,128]{2,0,1:T(8,128)(2,1)S(1)} collective-permute-done((bf16[384,6,128]{2,0,1:T(8,128)(2,1)}, bf16[384,6,128]{2,0,1:T(8,128)(2,1)S(1)}, u32[]{:S(2)}, u32[]{:S(2)}) %collective-permute-start.2) | collective-permute-done | bytes 589856 | tf_op jit(solution)/shard_map/ppermute | solution.py:17
  45.2 13.9 %collective-permute-done.3 = bf16[384,6,128]{2,0,1:T(8,128)(2,1)S(1)} collective-permute-done((bf16[384,6,128]{2,0,1:T(8,128)(2,1)}, bf16[384,6,128]{2,0,1:T(8,128)(2,1)S(1)}, u32[]{:S(2)}, u32[]{:S(2)}) %collective-permute-start.3) | collective-permute-done | bytes 589856 | tf_op jit(solution)/shard_map/ppermute | solution.py:17
  59.1 10.1 %attend.1.refs_2_ = bf16[384,768]{1,0:T(8,128)(2,1)} custom-call(f32[3,1152]{1,0:T(4,128)S(1)} %bitcast.18, bf16[6,384,128]{2,1,0:T(8,128)(2,1)S(1)} %bitcast.19, bf16[6,384,128]{2,1,0:T(8,128)(2,1)S(1)} %bitcast.20, bf16[6,384,128]{2,1,0:T(8,128)(2,1)} %bitcast.5.refs_1_, bf16[6,384,128]{2,1,0:T(8,128)(2,1)S(1)} %bitcast.21, ...), custom_call_target="tpu_custom_call" | custom-call | flops 20000000000 | bytes 10000000 | tf_op jit(solution)/shard_map/attend/pallas_call | solution.py:56
  69.2 1.3 collective-permute-start.4
  70.5 2.0 %collective-permute-start.5 = (bf16[384,768]{1,0:T(8,128)(2,1)}, bf16[384,768]{1,0:T(8,128)(2,1)}, u32[]{:S(2)}, u32[]{:S(2)}) collective-permute-start(bf16[384,768]{1,0:T(8,128)(2,1)} %attend.1.refs_2_), channel_id=1, source_target_pairs={{0,1},{1,0},{2,3},{3,2},{4,5},{5,4},{6,7},{7,6},{8,9},{9,8},{10,11... | collective-permute-start | bytes 1769480 | tf_op jit(solution)/shard_map/ppermute | solution.py:22
  72.5 10.6 %collective-permute-done.4.refs_3_ = bf16[384,768]{1,0:T(8,128)(2,1)} collective-permute-done((bf16[384,768]{1,0:T(8,128)(2,1)}, bf16[384,768]{1,0:T(8,128)(2,1)}, u32[]{:S(2)}, u32[]{:S(2)}) %collective-permute-start.4) | collective-permute-done | bytes 589856 | tf_op jit(solution)/shard_map/ppermute | solution.py:22
  83.1 2.2 %collective-permute-start.6 = (bf16[384,768]{1,0:T(8,128)(2,1)}, bf16[384,768]{1,0:T(8,128)(2,1)}, u32[]{:S(2)}, u32[]{:S(2)}) collective-permute-start(bf16[384,768]{1,0:T(8,128)(2,1)} %collective-permute-done.4.refs_3_), channel_id=1, source_target_pairs={{0,1},{1,0},{2,3},{3,2},{4,5},{5,4},{6,7},{7,6},{8,9},{9,8},{10,11... | collective-permute-start | bytes 1769480 | tf_op jit(solution)/shard_map/ppermute | solution.py:22
  85.3 15.8 %collective-permute-done.9.refs_7_ = bf16[2,768,640]{2,1,0:T(8,128)(2,1)} collective-permute-done((bf16[2,768,640]{2,1,0:T(8,128)(2,1)}, bf16[2,768,640]{2,1,0:T(8,128)(2,1)}, u32[]{:S(2)}, u32[]{:S(2)}) %collective-permute-start.9) | collective-permute-done | bytes 1966112 | tf_op jit(solution)/shard_map/ppermute | solution.py:251
  101.1 1.3 collective-permute-start.10
  102.4 1.3 collective-permute-start.15
  103.7 10.4 %collective-permute-done.10.refs_0_ = bf16[2,768,256]{2,1,0:T(8,128)(2,1)} collective-permute-done((bf16[2,768,256]{2,1,0:T(8,128)(2,1)}, bf16[2,768,256]{2,1,0:T(8,128)(2,1)}, u32[]{:S(2)}, u32[]{:S(2)}) %collective-permute-start.10) | collective-permute-done | bytes 786464 | tf_op jit(solution)/shard_map/ppermute | solution.py:251
  114.2 5.7 %terms.2 = (f32[384,256]{1,0:T(8,128)S(1)}, bf16[384,256]{1,0:T(8,128)(2,1)}, bf16[384,256]{1,0:T(8,128)(2,1)}, bf16[384,256]{1,0:T(8,128)(2,1)}) custom-call(s32[1]{0:T(128)} %bitcast.1.refs_0_, s32[1]{0:T(128)} %bitcast.2.refs_1_, bf16[384,768]{1,0:T(8,128)(2,1)} %attend.1.refs_2_, bf16[384,768]{1,0:T(8,128)(2,1)} %collective-permute-done.4.refs_3_, ...), custom_call_target="tpu_custom_call" | custom-call | flops 858993459200 | bytes 7667712 | tf_op jit(solution)/shard_map/terms/pallas_call | solution.py:122
  119.8 1.9 %collective-permute-start.11 = (bf16[384,256]{1,0:T(8,128)(2,1)}, bf16[384,256]{1,0:T(8,128)(2,1)}, u32[]{:S(2)}, u32[]{:S(2)}) collective-permute-start(bf16[384,256]{1,0:T(8,128)(2,1)} %get-tuple-element.26.refs_10_), channel_id=1, source_target_pairs={{0,2},{1,3},{2,0},{3,1},{4,6},{5,7},{6,4},{7,5},{8,10},{9,11},{10,... | collective-permute-start | bytes 589832 | tf_op jit(solution)/shard_map/ppermute | solution.py:22
  121.8 1.2 collective-permute-start.12
  123.0 3.7 %collective-permute-done.15.refs_9_ = bf16[2,768,384]{2,1,0:T(8,128)(2,1)} collective-permute-done((bf16[2,768,384]{2,1,0:T(8,128)(2,1)}, bf16[2,768,384]{2,1,0:T(8,128)(2,1)}, u32[]{:S(2)}, u32[]{:S(2)}) %collective-permute-start.15) | collective-permute-done | bytes 1179680 | tf_op jit(solution)/shard_map/ppermute | solution.py:251
  126.8 6.0 %terms.3 = (f32[384,384]{1,0:T(8,128)S(1)}, bf16[384,384]{1,0:T(8,128)(2,1)}, bf16[384,384]{1,0:T(8,128)(2,1)}, bf16[384,384]{1,0:T(8,128)(2,1)}) custom-call(s32[1]{0:T(128)} %bitcast.1.refs_0_, s32[1]{0:T(128)} %bitcast.2.refs_1_, bf16[384,768]{1,0:T(8,128)(2,1)} %attend.1.refs_2_, bf16[384,768]{1,0:T(8,128)(2,1)} %collective-permute-done.4.refs_3_, ...), custom_call_target="tpu_custom_call" | custom-call | flops 858993459200 | bytes 9338880 | tf_op jit(solution)/shard_map/terms/pallas_call | solution.py:122
  133.6 1.9 %collective-permute-start.16 = (bf16[384,384]{1,0:T(8,128)(2,1)}, bf16[384,384]{1,0:T(8,128)(2,1)}, u32[]{:S(2)}, u32[]{:S(2)}) collective-permute-start(bf16[384,384]{1,0:T(8,128)(2,1)} %get-tuple-element.34), channel_id=1, source_target_pairs={{0,2},{1,3},{2,0},{3,1},{4,6},{5,7},{6,4},{7,5},{8,10},{9,11},{10,... | collective-permute-start | bytes 884744 | tf_op jit(solution)/shard_map/ppermute | solution.py:22
  135.5 1.2 collective-permute-start.17
  136.7 3.1 %collective-permute-done.16.refs_7_ = bf16[384,384]{1,0:T(8,128)(2,1)} collective-permute-done((bf16[384,384]{1,0:T(8,128)(2,1)}, bf16[384,384]{1,0:T(8,128)(2,1)}, u32[]{:S(2)}, u32[]{:S(2)}) %collective-permute-start.16) | collective-permute-done | bytes 294944 | tf_op jit(solution)/shard_map/ppermute | solution.py:22
  139.9 4.6 %collective-permute-done.17.refs_8_ = bf16[384,384]{1,0:T(8,128)(2,1)} collective-permute-done((bf16[384,384]{1,0:T(8,128)(2,1)}, bf16[384,384]{1,0:T(8,128)(2,1)}, u32[]{:S(2)}, u32[]{:S(2)}) %collective-permute-start.17) | collective-permute-done | bytes 294944 | tf_op jit(solution)/shard_map/ppermute | solution.py:22
  144.5 2.6 %gated.1 = bf16[384,1280]{1,0:T(8,128)(2,1)} custom-call(s32[1]{0:T(128)} %bitcast.refs_0_, f32[1,1280]{1,0:T(1,128)S(1)} %reshape.20.refs_1_, f32[384,256]{1,0:T(8,128)S(1)} %get-tuple-element.25.refs_2_, bf16[384,256]{1,0:T(8,128)(2,1)} %get-tuple-element.29.refs_3_, bf16[384,256]{1,0:T(8,128)(2,1)} %get-tuple-element.30.refs_4_, ...), custom_call_target="tpu_custom_call" | custom-call | bytes 3445760 | tf_op jit(solution)/shard_map/gated/pallas_call | solution.py:122
  (34 shorter events, 2.8 us)
Async XLA Ops:
  0.0 1.5 %copy-start = (bf16[768,1280]{1,0:T(8,128)(2,1)S(1)}, bf16[768,1280]{1,0:T(8,128)(2,1)}, u32[]{:S(2)}) copy-start(bf16[768,1280]{1,0:T(8,128)(2,1)} %param.10) | copy-start | bytes 5898244
  0.0 10.5 %copy-start.5 = (s32[3,9]{1,0:T(4,128)S(1)}, s32[3,9]{1,0:T(4,128)}, u32[]{:S(2)}) copy-start(s32[3,9]{1,0:T(4,128)} %param.9) | copy-start | bytes 328
  1.6 9.0 %collective-permute-start.7 = (bf16[768,640]{1,0:T(8,128)(2,1)S(1)}, bf16[768,640]{1,0:T(8,128)(2,1)S(1)}, u32[]{:S(2)}, u32[]{:S(2)}) collective-permute-start(bf16[768,640]{1,0:T(8,128)(2,1)S(1)} %constant_dynamic-slice_fusion), channel_id=1, source_target_pairs={{1,0},{3,2},{4,5},{6,7},{9,8},{11,10},{12,13},{14,15},{17,16},{19,... | collective-permute-start | bytes 2949128 | tf_op jit(solution)/shard_map/ppermute | solution.py:251
  3.7 16.2 %collective-permute-start = (bf16[384,6,128]{2,0,1:T(8,128)(2,1)}, bf16[384,6,128]{2,0,1:T(8,128)(2,1)S(1)}, u32[]{:S(2)}, u32[]{:S(2)}) collective-permute-start(bf16[384,6,128]{2,0,1:T(8,128)(2,1)} %param.7), channel_id=1, source_target_pairs={{0,4},{4,8},{8,12},{12,0},{1,5},{5,9},{9,13},{13,1},{2,6},{6,10},{... | collective-permute-start | bytes 1769480 | tf_op jit(solution)/shard_map/ppermute | solution.py:17
  5.1 30.0 %collective-permute-start.1 = (bf16[384,6,128]{2,0,1:T(8,128)(2,1)}, bf16[384,6,128]{2,0,1:T(8,128)(2,1)S(1)}, u32[]{:S(2)}, u32[]{:S(2)}) collective-permute-start(bf16[384,6,128]{2,0,1:T(8,128)(2,1)} %param.7), channel_id=1, source_target_pairs={{0,12},{4,0},{8,4},{12,8},{1,13},{5,1},{9,5},{13,9},{2,14},{6,2},{... | collective-permute-start | bytes 1769480 | tf_op jit(solution)/shard_map/ppermute | solution.py:17
  7.2 38.0 %collective-permute-start.2 = (bf16[384,6,128]{2,0,1:T(8,128)(2,1)}, bf16[384,6,128]{2,0,1:T(8,128)(2,1)S(1)}, u32[]{:S(2)}, u32[]{:S(2)}) collective-permute-start(bf16[384,6,128]{2,0,1:T(8,128)(2,1)} %param.8), channel_id=1, source_target_pairs={{0,4},{4,8},{8,12},{12,0},{1,5},{5,9},{9,13},{13,1},{2,6},{6,10},{... | collective-permute-start | bytes 1769480 | tf_op jit(solution)/shard_map/ppermute | solution.py:17
  7.8 51.3 %collective-permute-start.3 = (bf16[384,6,128]{2,0,1:T(8,128)(2,1)}, bf16[384,6,128]{2,0,1:T(8,128)(2,1)S(1)}, u32[]{:S(2)}, u32[]{:S(2)}) collective-permute-start(bf16[384,6,128]{2,0,1:T(8,128)(2,1)} %param.8), channel_id=1, source_target_pairs={{0,12},{4,0},{8,4},{12,8},{1,13},{5,1},{9,5},{13,9},{2,14},{6,2},{... | collective-permute-start | bytes 1769480 | tf_op jit(solution)/shard_map/ppermute | solution.py:17
  11.8 47.3 %copy-start.3 = (bf16[384,6,128]{2,0,1:T(8,128)(2,1)S(1)}, bf16[384,6,128]{2,0,1:T(8,128)(2,1)}, u32[]{:S(2)}) copy-start(bf16[384,6,128]{2,0,1:T(8,128)(2,1)} %param.6) | copy-start | bytes 1769476
  35.1 50.2 %collective-permute-start.8 = (bf16[2,768,256]{2,1,0:T(8,128)(2,1)}, bf16[2,768,256]{2,1,0:T(8,128)(2,1)}, u32[]{:S(2)}, u32[]{:S(2)}) collective-permute-start(bf16[2,768,256]{2,1,0:T(8,128)(2,1)} %fusion.1.refs_6_), channel_id=1, source_target_pairs={{0,8},{2,10},{5,13},{7,15},{8,0},{10,2},{13,5},{15,7},{16,24},{18,... | collective-permute-start | bytes 2359304 | tf_op jit(solution)/shard_map/ppermute | solution.py:251
  36.7 64.4 %collective-permute-start.9 = (bf16[2,768,640]{2,1,0:T(8,128)(2,1)}, bf16[2,768,640]{2,1,0:T(8,128)(2,1)}, u32[]{:S(2)}, u32[]{:S(2)}) collective-permute-start(bf16[2,768,640]{2,1,0:T(8,128)(2,1)} %pad_maximum_fusion), channel_id=1, source_target_pairs={{0,4},{2,6},{5,1},{7,3},{8,12},{10,14},{13,9},{15,11},{16,20},{18,... | collective-permute-start | bytes 5898248 | tf_op jit(solution)/shard_map/ppermute | solution.py:251
  38.0 64.4 %collective-permute-start.14 = (bf16[2,768,384]{2,1,0:T(8,128)(2,1)S(1)}, bf16[2,768,384]{2,1,0:T(8,128)(2,1)}, u32[]{:S(2)}, u32[]{:S(2)}) collective-permute-start(bf16[2,768,384]{2,1,0:T(8,128)(2,1)S(1)} %fusion.refs_6_), channel_id=1, source_target_pairs={{0,8},{2,10},{5,13},{7,15},{8,0},{10,2},{13,5},{15,7},{16,24},{18,... | collective-permute-start | bytes 3538952 | tf_op jit(solution)/shard_map/ppermute | solution.py:251
  59.1 11.4 %copy-start.4 = (f32[1280]{0:T(1024)S(1)}, f32[1280]{0:T(1024)}, u32[]{:S(2)}) copy-start(f32[1280]{0:T(1024)} %param.11) | copy-start | bytes 15364
  69.2 13.9 %collective-permute-start.4 = (bf16[384,768]{1,0:T(8,128)(2,1)}, bf16[384,768]{1,0:T(8,128)(2,1)}, u32[]{:S(2)}, u32[]{:S(2)}) collective-permute-start(bf16[384,768]{1,0:T(8,128)(2,1)} %attend.1.refs_2_), channel_id=1, source_target_pairs={{0,16},{16,0},{1,17},{17,1},{2,18},{18,2},{3,19},{19,3},{4,20},{20... | collective-permute-start | bytes 1769480 | tf_op jit(solution)/shard_map/ppermute | solution.py:22
  70.5 43.6 %collective-permute-start.5 = (bf16[384,768]{1,0:T(8,128)(2,1)}, bf16[384,768]{1,0:T(8,128)(2,1)}, u32[]{:S(2)}, u32[]{:S(2)}) collective-permute-start(bf16[384,768]{1,0:T(8,128)(2,1)} %attend.1.refs_2_), channel_id=1, source_target_pairs={{0,1},{1,0},{2,3},{3,2},{4,5},{5,4},{6,7},{7,6},{8,9},{9,8},{10,11... | collective-permute-start | bytes 1769480 | tf_op jit(solution)/shard_map/ppermute | solution.py:22
  83.1 31.0 %collective-permute-start.6 = (bf16[384,768]{1,0:T(8,128)(2,1)}, bf16[384,768]{1,0:T(8,128)(2,1)}, u32[]{:S(2)}, u32[]{:S(2)}) collective-permute-start(bf16[384,768]{1,0:T(8,128)(2,1)} %collective-permute-done.4.refs_3_), channel_id=1, source_target_pairs={{0,1},{1,0},{2,3},{3,2},{4,5},{5,4},{6,7},{7,6},{8,9},{9,8},{10,11... | collective-permute-start | bytes 1769480 | tf_op jit(solution)/shard_map/ppermute | solution.py:22
  101.1 13.0 %collective-permute-start.10 = (bf16[2,768,256]{2,1,0:T(8,128)(2,1)}, bf16[2,768,256]{2,1,0:T(8,128)(2,1)}, u32[]{:S(2)}, u32[]{:S(2)}) collective-permute-start(bf16[2,768,256]{2,1,0:T(8,128)(2,1)} %collective-permute-done.8.refs_8_), channel_id=1, source_target_pairs={{0,4},{2,6},{5,1},{7,3},{8,12},{10,14},{13,9},{15,11},{16,20},{18,... | collective-permute-start | bytes 2359304 | tf_op jit(solution)/shard_map/ppermute | solution.py:251
  102.4 24.4 %collective-permute-start.15 = (bf16[2,768,384]{2,1,0:T(8,128)(2,1)}, bf16[2,768,384]{2,1,0:T(8,128)(2,1)}, u32[]{:S(2)}, u32[]{:S(2)}) collective-permute-start(bf16[2,768,384]{2,1,0:T(8,128)(2,1)} %held.5.refs_8_), channel_id=1, source_target_pairs={{0,4},{2,6},{5,1},{7,3},{8,12},{10,14},{13,9},{15,11},{16,20},{18,... | collective-permute-start | bytes 3538952 | tf_op jit(solution)/shard_map/ppermute | solution.py:251
  119.8 16.9 %collective-permute-start.11 = (bf16[384,256]{1,0:T(8,128)(2,1)}, bf16[384,256]{1,0:T(8,128)(2,1)}, u32[]{:S(2)}, u32[]{:S(2)}) collective-permute-start(bf16[384,256]{1,0:T(8,128)(2,1)} %get-tuple-element.26.refs_10_), channel_id=1, source_target_pairs={{0,2},{1,3},{2,0},{3,1},{4,6},{5,7},{6,4},{7,5},{8,10},{9,11},{10,... | collective-permute-start | bytes 589832 | tf_op jit(solution)/shard_map/ppermute | solution.py:22
  121.8 14.9 %collective-permute-start.12 = (bf16[384,256]{1,0:T(8,128)(2,1)}, bf16[384,256]{1,0:T(8,128)(2,1)}, u32[]{:S(2)}, u32[]{:S(2)}) collective-permute-start(bf16[384,256]{1,0:T(8,128)(2,1)} %get-tuple-element.27), channel_id=1, source_target_pairs={{0,16},{16,0},{1,17},{17,1},{2,18},{18,2},{3,19},{19,3},{4,20},{20... | collective-permute-start | bytes 589832 | tf_op jit(solution)/shard_map/ppermute | solution.py:22
  123.0 13.7 %collective-permute-start.13 = (bf16[384,256]{1,0:T(8,128)(2,1)}, bf16[384,256]{1,0:T(8,128)(2,1)}, u32[]{:S(2)}, u32[]{:S(2)}) collective-permute-start(bf16[384,256]{1,0:T(8,128)(2,1)} %get-tuple-element.28), channel_id=1, source_target_pairs={{0,18},{1,19},{2,16},{3,17},{16,2},{17,3},{18,0},{19,1},{4,22},{5,... | collective-permute-start | bytes 589832 | tf_op jit(solution)/shard_map/ppermute | solution.py:80
  132.8 0.8 copy-start.1
  133.6 6.3 %collective-permute-start.16 = (bf16[384,384]{1,0:T(8,128)(2,1)}, bf16[384,384]{1,0:T(8,128)(2,1)}, u32[]{:S(2)}, u32[]{:S(2)}) collective-permute-start(bf16[384,384]{1,0:T(8,128)(2,1)} %get-tuple-element.34), channel_id=1, source_target_pairs={{0,2},{1,3},{2,0},{3,1},{4,6},{5,7},{6,4},{7,5},{8,10},{9,11},{10,... | collective-permute-start | bytes 884744 | tf_op jit(solution)/shard_map/ppermute | solution.py:22
  135.5 9.0 %collective-permute-start.17 = (bf16[384,384]{1,0:T(8,128)(2,1)}, bf16[384,384]{1,0:T(8,128)(2,1)}, u32[]{:S(2)}, u32[]{:S(2)}) collective-permute-start(bf16[384,384]{1,0:T(8,128)(2,1)} %get-tuple-element.35), channel_id=1, source_target_pairs={{0,16},{16,0},{1,17},{17,1},{2,18},{18,2},{3,19},{19,3},{4,20},{20... | collective-permute-start | bytes 884744 | tf_op jit(solution)/shard_map/ppermute | solution.py:22
  136.7 7.8 %collective-permute-start.18 = (bf16[384,384]{1,0:T(8,128)(2,1)}, bf16[384,384]{1,0:T(8,128)(2,1)}, u32[]{:S(2)}, u32[]{:S(2)}) collective-permute-start(bf16[384,384]{1,0:T(8,128)(2,1)} %get-tuple-element.36), channel_id=1, source_target_pairs={{0,18},{1,19},{2,16},{3,17},{16,2},{17,3},{18,0},{19,1},{4,22},{5,... | collective-permute-start | bytes 884744 | tf_op jit(solution)/shard_map/ppermute | solution.py:80
  136.7 7.8 %copy-start.2 = (f32[384,384]{1,0:T(8,128)S(1)}, f32[384,384]{1,0:T(8,128)}, u32[]{:S(2)}) copy-start(f32[384,384]{1,0:T(8,128)} %copy-done.1) | copy-start | bytes 1769476

commit v6 on v5

--- a/solution.py
+++ b/solution.py
@@ -196,6 +196,107 @@
     )
 
 
+def early_terms(rows_of, blocks, role, cost):
+    rows, depth = rows_of[0][0].shape
+    width = blocks[0][0].shape[2]
+    starts = [column for _, column in blocks]
+    flat = [array for core in rows_of for array in core]
+
+    def kernel(role_ref, *refs):
+        rows_refs, block_refs, out_ref = refs[:4], refs[4:6], refs[6]
+        held_rows, weight, landed = refs[7:]
+        copies = row_copies(rows_refs, held_rows, landed)
+        for odd in (0, 1):
+            for copy in weight_copies(block_refs[odd], starts[odd], weight, landed):
+                pl.when(role_ref[0] == odd)(copy.start)
+        for copy in copies:
+            copy.start()
+        for copy in copies + weight_copies(block_refs[0], starts[0], weight, landed):
+            copy.wait()
+        total = jnp.dot(held_rows[...], weight[...], preferred_element_type=jnp.float32)
+        for video in (0, 1):
+            out_ref[video] = total[video * rows : (video + 1) * rows]
+
+    out = jax.ShapeDtypeStruct((2, rows, width), jnp.float32)
+    left = (*flat, *[block for block, _ in blocks])
+    scratch = term_scratch(rows, depth, width)
+    return local_call(
+        kernel, [out], (role,), (), (), "early_terms", cost, left=left, scratch=scratch
+    )[0]
+
+
+def late_terms(rows_of, blocks, role, first, early, cost, earlier=()):
+    rows, depth = rows_of[0][0].shape
+    width = blocks[0][0].shape[2]
+    starts = [column for _, column in blocks]
+    flat = [array for core in rows_of for array in core]
+
+    def kernel(role_ref, first_ref, early_ref, *refs):
+        rows_refs, block_refs = refs[:4], refs[4:6]
+        near_ref, far_ref, near_given_ref, far_given_ref, held_rows, weight, landed = refs[6:]
+        copies = row_copies(rows_refs, held_rows, landed)
+        for odd in (0, 1):
+            for copy in weight_copies(block_refs[odd], starts[odd], weight, landed):
+                pl.when(role_ref[0] == odd)(copy.start)
+        for copy in copies:
+            copy.start()
+        for copy in copies + weight_copies(block_refs[0], starts[0], weight, landed):
+            copy.wait()
+        total = jnp.dot(held_rows[...], weight[...], preferred_element_type=jnp.float32)
+        kept_refs, given_refs = (near_ref, far_ref), (near_given_ref, far_given_ref)
+        for stays, late_refs, early_refs in (
+            (1, given_refs, kept_refs),
+            (0, kept_refs, given_refs),
+        ):
+
+            @pl.when(first_ref[0] == stays)
+            def _():
+                for video in (0, 1):
+                    late = total[video * rows : (video + 1) * rows]
+                    late_refs[video][...] = late.astype(late_refs[video].dtype)
+                    early_refs[video][...] = early_ref[video].astype(early_refs[video].dtype)
+
+    kinds = (jnp.float32, jnp.bfloat16, jnp.bfloat16, jnp.bfloat16)
+    outs = [jax.ShapeDtypeStruct((rows, width), kind) for kind in kinds]
+    left = (*flat, *[block for block, _ in blocks])
+    scratch = term_scratch(rows, depth, width)
+    return local_call(
+        kernel, outs, (role, first), (early,), earlier, "late_terms", cost, left=left, scratch=scratch
+    )
+
+
+def row_copies(rows_refs, held_rows, landed):
+    rows, depth = rows_refs[0].shape
+    return [
+        pltpu.make_async_copy(
+            rows_ref,
+            held_rows.at[pl.ds(index % 2 * rows, rows), pl.ds(index // 2 * depth, depth)],
+            landed.at[index],
+        )
+        for index, rows_ref in enumerate(rows_refs)
+    ]
+
+
+def weight_copies(block_ref, start, weight, landed):
+    depth, width = weight.shape[0] // 2, weight.shape[1]
+    return [
+        pltpu.make_async_copy(
+            block_ref.at[core, :, pl.ds(start, width)],
+            weight.at[pl.ds(core * depth, depth)],
+            landed.at[4 + core],
+        )
+        for core in (0, 1)
+    ]
+
+
+def term_scratch(rows, depth, width):
+    return [
+        pltpu.VMEM((2 * rows, 2 * depth), jnp.bfloat16),
+        pltpu.VMEM((2 * depth, width), jnp.bfloat16),
+        pltpu.SemaphoreType.DMA((6,)),
+    ]
+
+
 def held(arrays, earlier, cost=0):
     return pl.pallas_call(
         lambda *refs: None,
@@ -261,10 +362,10 @@
 
     key_slabs, value_slabs = all_slabs(lower, (key_rows, value_rows), upper)
     mine = attend(queries, key_slabs, value_slabs, keep_tiles)
-    to_core = mine
-    block_2[0], block_1 = lax.optimization_barrier((block_2[0], block_1))
+    to_core, block_1 = lax.optimization_barrier((mine, block_1))
     other = swapped(mine, "groups", 1)
-    rows_of = (mine, other), (swapped(to_core, "head", 1), swapped(other, "head", 1))
+    mine_core = held([swapped(to_core, "head", 1)], [], 100 * 2**33)[0]
+    rows_of = (mine, other), (mine_core, swapped(after(other, mine_core), "head", 1))
     block_2[1:] = [held([block], [], 100 * 2**33)[0] for block in block_2[1:]]
     block_3 = [passed(block, 1, 0, 0) for block in block_2]
     block_3[0] = held([block_3[0]], [], 100 * 2**33)[0]
@@ -275,10 +376,16 @@
 
     cost = 100 * 2**33
     summed = []
-    given = []
+    early = early_terms(rows_of, parts[-1][:2], role, 0)
+    given = [early]
     for part in parts:
-        near, far, near_given, far_given = terms(rows_of, part, role, first, cost, given)
-        given = [near_given]
+        if len(summed) < len(parts) - 1:
+            near, far, near_given, far_given = terms(rows_of, part, role, first, cost, given)
+            given = [near_given]
+        else:
+            near, far, near_given, far_given = late_terms(
+                rows_of, part[2:], role, first, early, cost, given
+            )
         arrived = [swapped(near_given, "head", 2), swapped(far, "groups", 1), diagonal(far_given)]
         if len(summed) < len(parts) - 1:
             arrived = held(arrived, [], 100 * 2**33)

time: 147 us -> 146 us (level)
  waiting for transfers between devices: 89.6 us -> 84.4 us
  local copies, waits for them, and re-layouts: 2.64 us -> 7.51 us
  starting transfers between devices: 27.7 us -> 24.5 us
  Pallas kernels: 24.4 us -> 26.4 us
    ppermute x7, waiting for transfers between devices: 18.3 us -> 13.1 us  [swapped(): return lax.ppermute(array, axis, [(i, i ^ mask) for i in range(count)])]
    unnamed x14 -> x24, local copies, waits for them, and re-layouts: 2.46 us -> 7.33 us
    ppermute x7, starting transfers between devices: 11.7 us -> 8.49 us  [swapped(): return lax.ppermute(array, axis, [(i, i ^ mask) for i in range(count)])]
    pallas_call x3 -> x4, Pallas kernels: 14.3 us -> 16.2 us  [local_call(): pl.pallas_call(body, out_shape=outs, in_specs=[SMEM] * len(flags) + [WHOL...]
    ppermute x4, waiting for transfers between devices: 41.3 us -> 39.6 us  [passed_along(): lax.ppermute(array, axis, [(i, (i + by) % count) for i in range(count)])]
    ppermute x6, waiting for transfers between devices: 30 us -> 31.6 us  [passed(): return lax.ppermute(array, ('tm', 'head'), pairs)]
  transfers between devices with their start and end apart: 19 -> 19, of which waited for: 10 -> 10; matrix products, arithmetic and copies ran while one was open for 2% -> 2% of each run, Pallas kernels for 15% -> 16%
where the time goes in v6:
time: 146 us
  waiting for transfers between devices  84.4 us (58%)
  Pallas kernels  26.4 us (18%)
  starting transfers between devices  24.5 us (17%)
  local copies, waits for them, and re-layouts  7.51 us (5%)
  other arithmetic  2.59 us (2%)
    ppermute x4, waiting for transfers between devices, passed_along(): lax.ppermute(array, axis, [(i, (i + by) % count) for i in range(count)])  39.6 us
    ppermute x6, waiting for transfers between devices, passed(): return lax.ppermute(array, ('tm', 'head'), pairs)  31.6 us
    pallas_call x4, Pallas kernels, local_call(): pl.pallas_call(body, out_shape=outs, in_specs=[SMEM] * len(flags) + [WHOL...  16.2 us
    ppermute x7, waiting for transfers between devices, swapped(): return lax.ppermute(array, axis, [(i, i ^ mask) for i in range(count)])  13.1 us
    pallas_call x1, Pallas kernels, attend(): pl.pallas_call(functools.partial(attend_kernel, len(key_slabs) // 2, 1.0...  10.2 us
    ppermute x6, starting transfers between devices, passed(): return lax.ppermute(array, ('tm', 'head'), pairs)  9.14 us
    ppermute x7, starting transfers between devices, swapped(): return lax.ppermute(array, axis, [(i, i ^ mask) for i in range(count)])  8.49 us
    unnamed x24, local copies, waits for them, and re-layouts  7.33 us
  transfers between devices with their start and end apart: 19, of which 10 were waited for; matrix products, arithmetic and copies ran while one was open for 2% of the time, Pallas kernels for 16%

profile of v6, /device:TPU:1, one launch (start us, length us, event | category | flops | bytes accessed | tf_op | source)
XLA Modules:
  0.0 145.5 jit_solution(12423837937627670760)
XLA Ops:
  0.0 1.5 %copy-done = bf16[768,1280]{1,0:T(8,128)(2,1)S(1)} copy-done((bf16[768,1280]{1,0:T(8,128)(2,1)S(1)}, bf16[768,1280]{1,0:T(8,128)(2,1)}, u32[]{:S(2)}) %copy-start) | copy-done | bytes 1966104
  1.6 2.0 %collective-permute-start.5 = (bf16[768,640]{1,0:T(8,128)(2,1)S(1)}, bf16[768,640]{1,0:T(8,128)(2,1)S(1)}, u32[]{:S(2)}, u32[]{:S(2)}) collective-permute-start(bf16[768,640]{1,0:T(8,128)(2,1)S(1)} %constant_dynamic-slice_fusion), channel_id=1, source_target_pairs={{1,0},{3,2},{4,5},{6,7},{9,8},{11,10},{12,13},{14,15},{17,16},{19,... | collective-permute-start | bytes 2949128 | tf_op jit(solution)/shard_map/ppermute | solution.py:352
  3.7 1.4 collective-permute-start
  5.1 2.1 %collective-permute-start.1 = (bf16[384,6,128]{2,0,1:T(8,128)(2,1)}, bf16[384,6,128]{2,0,1:T(8,128)(2,1)S(1)}, u32[]{:S(2)}, u32[]{:S(2)}) collective-permute-start(bf16[384,6,128]{2,0,1:T(8,128)(2,1)} %param.7), channel_id=1, source_target_pairs={{0,12},{4,0},{8,4},{12,8},{1,13},{5,1},{9,5},{13,9},{2,14},{6,2},{... | collective-permute-start | bytes 1769480 | tf_op jit(solution)/shard_map/ppermute | solution.py:17
  7.8 2.7 %collective-permute-start.3 = (bf16[384,6,128]{2,0,1:T(8,128)(2,1)}, bf16[384,6,128]{2,0,1:T(8,128)(2,1)}, u32[]{:S(2)}, u32[]{:S(2)}) collective-permute-start(bf16[384,6,128]{2,0,1:T(8,128)(2,1)} %param.8), channel_id=1, source_target_pairs={{0,12},{4,0},{8,4},{12,8},{1,13},{5,1},{9,5},{13,9},{2,14},{6,2},{... | collective-permute-start | bytes 1769480 | tf_op jit(solution)/shard_map/ppermute | solution.py:17
  11.7 1.5 %pad_maximum_fusion = bf16[2,768,640]{2,1,0:T(8,128)(2,1)} fusion(bf16[1,768,640]{2,1,0:T(8,128)(2,1)S(1)} %bitcast.24, bf16[1,768,640]{2,1,0:T(8,128)(2,1)S(1)} %fusion.2), kind=kLoop, calls=%fused_computation.2 | loop fusion | flops 983040 | bytes 3932160 | tf_op jit(solution)/shard_map/stack | solution.py:356
  13.2 6.7 %collective-permute-done = bf16[384,6,128]{2,0,1:T(8,128)(2,1)S(1)} collective-permute-done((bf16[384,6,128]{2,0,1:T(8,128)(2,1)}, bf16[384,6,128]{2,0,1:T(8,128)(2,1)S(1)}, u32[]{:S(2)}, u32[]{:S(2)}) %collective-permute-start) | collective-permute-done | bytes 589856 | tf_op jit(solution)/shard_map/ppermute | solution.py:17
  20.7 14.4 %collective-permute-done.1 = bf16[384,6,128]{2,0,1:T(8,128)(2,1)S(1)} collective-permute-done((bf16[384,6,128]{2,0,1:T(8,128)(2,1)}, bf16[384,6,128]{2,0,1:T(8,128)(2,1)S(1)}, u32[]{:S(2)}, u32[]{:S(2)}) %collective-permute-start.1) | collective-permute-done | bytes 589856 | tf_op jit(solution)/shard_map/ppermute | solution.py:17
  36.0 1.3 collective-permute-start.6
  37.4 1.6 %collective-permute-start.9 = (bf16[2,768,256]{2,1,0:T(8,128)(2,1)}, bf16[2,768,256]{2,1,0:T(8,128)(2,1)}, u32[]{:S(2)}, u32[]{:S(2)}) collective-permute-start(bf16[2,768,256]{2,1,0:T(8,128)(2,1)} %fusion.1.refs_6_), channel_id=1, source_target_pairs={{0,8},{2,10},{5,13},{7,15},{8,0},{10,2},{13,5},{15,7},{16,24},{18,... | collective-permute-start | bytes 2359304 | tf_op jit(solution)/shard_map/ppermute | solution.py:352
  39.0 1.7 %collective-permute-start.14 = (bf16[2,768,384]{2,1,0:T(8,128)(2,1)S(1)}, bf16[2,768,384]{2,1,0:T(8,128)(2,1)}, u32[]{:S(2)}, u32[]{:S(2)}) collective-permute-start(bf16[2,768,384]{2,1,0:T(8,128)(2,1)S(1)} %fusion.refs_5_), channel_id=1, source_target_pairs={{0,8},{2,10},{5,13},{7,15},{8,0},{10,2},{13,5},{15,7},{16,24},{18,... | collective-permute-start | bytes 3538952 | tf_op jit(solution)/shard_map/ppermute | solution.py:352
  40.7 4.6 %collective-permute-done.2 = bf16[384,6,128]{2,0,1:T(8,128)(2,1)} collective-permute-done((bf16[384,6,128]{2,0,1:T(8,128)(2,1)}, bf16[384,6,128]{2,0,1:T(8,128)(2,1)}, u32[]{:S(2)}, u32[]{:S(2)}) %collective-permute-start.2) | collective-permute-done | bytes 589856 | tf_op jit(solution)/shard_map/ppermute | solution.py:17
  45.3 13.9 %collective-permute-done.3 = bf16[384,6,128]{2,0,1:T(8,128)(2,1)} collective-permute-done((bf16[384,6,128]{2,0,1:T(8,128)(2,1)}, bf16[384,6,128]{2,0,1:T(8,128)(2,1)}, u32[]{:S(2)}, u32[]{:S(2)}) %collective-permute-start.3) | collective-permute-done | bytes 589856 | tf_op jit(solution)/shard_map/ppermute | solution.py:17
  59.2 1.1 copy-done.4
  60.3 1.1 copy-done.6
  61.3 1.1 copy-done.8
  62.4 10.2 %attend.1.refs_1_.refs_2_.refs_3_ = bf16[384,768]{1,0:T(8,128)(2,1)} custom-call(f32[3,1152]{1,0:T(4,128)S(1)} %bitcast.18, bf16[6,384,128]{2,1,0:T(8,128)(2,1)S(1)} %bitcast.19, bf16[6,384,128]{2,1,0:T(8,128)(2,1)S(1)} %bitcast.20, bf16[6,384,128]{2,1,0:T(8,128)(2,1)} %bitcast.5.refs_1_, bf16[6,384,128]{2,1,0:T(8,128)(2,1)S(1)} %bitcast.21, ...), custom_call_target="tpu_custom_call" | custom-call | flops 20000000000 | bytes 10000000 | tf_op jit(solution)/shard_map/attend/pallas_call | solution.py:56
  72.6 1.3 collective-permute-start.4
  73.9 1.3 collective-permute-start.10
  75.2 25.9 %collective-permute-done.6.refs_6_.refs_7_ = bf16[2,768,640]{2,1,0:T(8,128)(2,1)} collective-permute-done((bf16[2,768,640]{2,1,0:T(8,128)(2,1)}, bf16[2,768,640]{2,1,0:T(8,128)(2,1)}, u32[]{:S(2)}, u32[]{:S(2)}) %collective-permute-start.6) | collective-permute-done | bytes 1966112 | tf_op jit(solution)/shard_map/ppermute | solution.py:352
  101.1 1.3 collective-permute-start.15
  104.4 5.1 %collective-permute-done.10.refs_0_ = bf16[2,768,256]{2,1,0:T(8,128)(2,1)} collective-permute-done((bf16[2,768,256]{2,1,0:T(8,128)(2,1)}, bf16[2,768,256]{2,1,0:T(8,128)(2,1)}, u32[]{:S(2)}, u32[]{:S(2)}) %collective-permute-start.10) | collective-permute-done | bytes 786464 | tf_op jit(solution)/shard_map/ppermute | solution.py:352
  109.5 3.5 %early_terms.1.refs_10_.refs_2_ = f32[2,384,384]{2,1,0:T(8,128)S(1)} custom-call(s32[1]{0:T(128)} %bitcast.1.refs_0_, bf16[384,768]{1,0:T(8,128)(2,1)} %attend.1.refs_1_.refs_2_.refs_3_, bf16[384,768]{1,0:T(8,128)(2,1)} %collective-permute-done.4.refs_2_.refs_3_.refs_4_, bf16[384,768]{1,0:T(8,128)(2,1)} %held.4.refs_3_.refs_4_.refs_5_, ...), custom_call_target="tpu_custom_call" | custom-call | bytes 6684672 | tf_op jit(solution)/shard_map/early_terms/pallas_call | solution.py:122
  113.0 5.7 %terms.1 = (f32[384,256]{1,0:T(8,128)S(1)}, bf16[384,256]{1,0:T(8,128)(2,1)}, bf16[384,256]{1,0:T(8,128)(2,1)}, bf16[384,256]{1,0:T(8,128)(2,1)}) custom-call(s32[1]{0:T(128)} %bitcast.1.refs_0_, s32[1]{0:T(128)} %bitcast.2.refs_1_, bf16[384,768]{1,0:T(8,128)(2,1)} %attend.1.refs_1_.refs_2_.refs_3_, ...), custom_call_target="tpu_custom_call" | custom-call | flops 858993459200 | bytes 7667712 | tf_op jit(solution)/shard_map/terms/pallas_call | solution.py:122
  118.7 1.9 %collective-permute-start.11 = (bf16[384,256]{1,0:T(8,128)(2,1)}, bf16[384,256]{1,0:T(8,128)(2,1)}, u32[]{:S(2)}, u32[]{:S(2)}) collective-permute-start(bf16[384,256]{1,0:T(8,128)(2,1)} %get-tuple-element.29.refs_9_), channel_id=1, source_target_pairs={{0,2},{1,3},{2,0},{3,1},{4,6},{5,7},{6,4},{7,5},{8,10},{9,11},{10,... | collective-permute-start | bytes 589832 | tf_op jit(solution)/shard_map/ppermute | solution.py:22
  120.6 1.2 collective-permute-start.12
  122.5 4.5 %late_terms.1 = (f32[384,384]{1,0:T(8,128)S(1)}, bf16[384,384]{1,0:T(8,128)(2,1)}, bf16[384,384]{1,0:T(8,128)(2,1)}, bf16[384,384]{1,0:T(8,128)(2,1)}) custom-call(s32[1]{0:T(128)} %bitcast.1.refs_0_, s32[1]{0:T(128)} %bitcast.2.refs_1_, f32[2,384,384]{2,1,0:T(8,128)S(1)} %early_terms.1.refs_10_.refs_2_, bf16[384,768]{1,0:T(8,128)(2,1)} %attend.1.refs_1_.refs_2_.refs_3_, ...), custom_call_target="tpu_custom_call" | custom-call | flops 858993459200 | bytes 7372800 | tf_op jit(solution)/shard_map/late_terms/pallas_call | solution.py:122
  127.8 1.6 %collective-permute-start.16 = (bf16[384,384]{1,0:T(8,128)(2,1)}, bf16[384,384]{1,0:T(8,128)(2,1)}, u32[]{:S(2)}, u32[]{:S(2)}) collective-permute-start(bf16[384,384]{1,0:T(8,128)(2,1)} %get-tuple-element.36), channel_id=1, source_target_pairs={{0,2},{1,3},{2,0},{3,1},{4,6},{5,7},{6,4},{7,5},{8,10},{9,11},{10,... | collective-permute-start | bytes 884744 | tf_op jit(solution)/shard_map/ppermute | solution.py:22
  129.3 1.5 %collective-permute-start.17 = (bf16[384,384]{1,0:T(8,128)(2,1)}, bf16[384,384]{1,0:T(8,128)(2,1)}, u32[]{:S(2)}, u32[]{:S(2)}) collective-permute-start(bf16[384,384]{1,0:T(8,128)(2,1)} %get-tuple-element.37), channel_id=1, source_target_pairs={{0,16},{16,0},{1,17},{17,1},{2,18},{18,2},{3,19},{19,3},{4,20},{20... | collective-permute-start | bytes 884744 | tf_op jit(solution)/shard_map/ppermute | solution.py:22
  130.9 6.4 %collective-permute-done.16.refs_7_ = bf16[384,384]{1,0:T(8,128)(2,1)} collective-permute-done((bf16[384,384]{1,0:T(8,128)(2,1)}, bf16[384,384]{1,0:T(8,128)(2,1)}, u32[]{:S(2)}, u32[]{:S(2)}) %collective-permute-start.16) | collective-permute-done | bytes 294944 | tf_op jit(solution)/shard_map/ppermute | solution.py:22
  137.3 5.6 %collective-permute-done.17.refs_8_ = bf16[384,384]{1,0:T(8,128)(2,1)} collective-permute-done((bf16[384,384]{1,0:T(8,128)(2,1)}, bf16[384,384]{1,0:T(8,128)(2,1)}, u32[]{:S(2)}, u32[]{:S(2)}) %collective-permute-start.17) | collective-permute-done | bytes 294944 | tf_op jit(solution)/shard_map/ppermute | solution.py:22
  142.9 2.6 %gated.1 = bf16[384,1280]{1,0:T(8,128)(2,1)} custom-call(s32[1]{0:T(128)} %bitcast.refs_0_, f32[1,1280]{1,0:T(1,128)S(1)} %reshape.21.refs_1_, f32[384,256]{1,0:T(8,128)S(1)} %get-tuple-element.28.refs_2_, bf16[384,256]{1,0:T(8,128)(2,1)} %get-tuple-element.32.refs_3_, bf16[384,256]{1,0:T(8,128)(2,1)} %get-tuple-element.33.refs_4_, ...), custom_call_target="tpu_custom_call" | custom-call | bytes 3445760 | tf_op jit(solution)/shard_map/gated/pallas_call | solution.py:122
  (46 shorter events, 7.0 us)
Async XLA Ops:
  0.0 1.5 %copy-start = (bf16[768,1280]{1,0:T(8,128)(2,1)S(1)}, bf16[768,1280]{1,0:T(8,128)(2,1)}, u32[]{:S(2)}) copy-start(bf16[768,1280]{1,0:T(8,128)(2,1)} %param.10) | copy-start | bytes 5898244
  0.0 10.5 %copy-start.10 = (s32[3,9]{1,0:T(4,128)S(1)}, s32[3,9]{1,0:T(4,128)}, u32[]{:S(2)}) copy-start(s32[3,9]{1,0:T(4,128)} %param.9) | copy-start | bytes 328
  1.6 8.9 %collective-permute-start.5 = (bf16[768,640]{1,0:T(8,128)(2,1)S(1)}, bf16[768,640]{1,0:T(8,128)(2,1)S(1)}, u32[]{:S(2)}, u32[]{:S(2)}) collective-permute-start(bf16[768,640]{1,0:T(8,128)(2,1)S(1)} %constant_dynamic-slice_fusion), channel_id=1, source_target_pairs={{1,0},{3,2},{4,5},{6,7},{9,8},{11,10},{12,13},{14,15},{17,16},{19,... | collective-permute-start | bytes 2949128 | tf_op jit(solution)/shard_map/ppermute | solution.py:352
  3.7 16.2 %collective-permute-start = (bf16[384,6,128]{2,0,1:T(8,128)(2,1)}, bf16[384,6,128]{2,0,1:T(8,128)(2,1)S(1)}, u32[]{:S(2)}, u32[]{:S(2)}) collective-permute-start(bf16[384,6,128]{2,0,1:T(8,128)(2,1)} %param.7), channel_id=1, source_target_pairs={{0,4},{4,8},{8,12},{12,0},{1,5},{5,9},{9,13},{13,1},{2,6},{6,10},{... | collective-permute-start | bytes 1769480 | tf_op jit(solution)/shard_map/ppermute | solution.py:17
  5.1 30.0 %collective-permute-start.1 = (bf16[384,6,128]{2,0,1:T(8,128)(2,1)}, bf16[384,6,128]{2,0,1:T(8,128)(2,1)S(1)}, u32[]{:S(2)}, u32[]{:S(2)}) collective-permute-start(bf16[384,6,128]{2,0,1:T(8,128)(2,1)} %param.7), channel_id=1, source_target_pairs={{0,12},{4,0},{8,4},{12,8},{1,13},{5,1},{9,5},{13,9},{2,14},{6,2},{... | collective-permute-start | bytes 1769480 | tf_op jit(solution)/shard_map/ppermute | solution.py:17
  7.2 38.1 %collective-permute-start.2 = (bf16[384,6,128]{2,0,1:T(8,128)(2,1)}, bf16[384,6,128]{2,0,1:T(8,128)(2,1)}, u32[]{:S(2)}, u32[]{:S(2)}) collective-permute-start(bf16[384,6,128]{2,0,1:T(8,128)(2,1)} %param.8), channel_id=1, source_target_pairs={{0,4},{4,8},{8,12},{12,0},{1,5},{5,9},{9,13},{13,1},{2,6},{6,10},{... | collective-permute-start | bytes 1769480 | tf_op jit(solution)/shard_map/ppermute | solution.py:17
  7.8 51.4 %collective-permute-start.3 = (bf16[384,6,128]{2,0,1:T(8,128)(2,1)}, bf16[384,6,128]{2,0,1:T(8,128)(2,1)}, u32[]{:S(2)}, u32[]{:S(2)}) collective-permute-start(bf16[384,6,128]{2,0,1:T(8,128)(2,1)} %param.8), channel_id=1, source_target_pairs={{0,12},{4,0},{8,4},{12,8},{1,13},{5,1},{9,5},{13,9},{2,14},{6,2},{... | collective-permute-start | bytes 1769480 | tf_op jit(solution)/shard_map/ppermute | solution.py:17
  11.7 25.7 %copy-start.9 = (f32[1280]{0:T(1024)S(1)}, f32[1280]{0:T(1024)}, u32[]{:S(2)}) copy-start(f32[1280]{0:T(1024)} %param.11) | copy-start | bytes 15364
  19.9 0.8 copy-start.5
  35.1 0.9 copy-start.7
  36.0 65.1 %collective-permute-start.6 = (bf16[2,768,640]{2,1,0:T(8,128)(2,1)}, bf16[2,768,640]{2,1,0:T(8,128)(2,1)}, u32[]{:S(2)}, u32[]{:S(2)}) collective-permute-start(bf16[2,768,640]{2,1,0:T(8,128)(2,1)} %pad_maximum_fusion), channel_id=1, source_target_pairs={{0,4},{2,6},{5,1},{7,3},{8,12},{10,14},{13,9},{15,11},{16,20},{18,... | collective-permute-start | bytes 5898248 | tf_op jit(solution)/shard_map/ppermute | solution.py:352
  37.4 36.5 %collective-permute-start.9 = (bf16[2,768,256]{2,1,0:T(8,128)(2,1)}, bf16[2,768,256]{2,1,0:T(8,128)(2,1)}, u32[]{:S(2)}, u32[]{:S(2)}) collective-permute-start(bf16[2,768,256]{2,1,0:T(8,128)(2,1)} %fusion.1.refs_6_), channel_id=1, source_target_pairs={{0,8},{2,10},{5,13},{7,15},{8,0},{10,2},{13,5},{15,7},{16,24},{18,... | collective-permute-start | bytes 2359304 | tf_op jit(solution)/shard_map/ppermute | solution.py:352
  39.0 62.1 %collective-permute-start.14 = (bf16[2,768,384]{2,1,0:T(8,128)(2,1)S(1)}, bf16[2,768,384]{2,1,0:T(8,128)(2,1)}, u32[]{:S(2)}, u32[]{:S(2)}) collective-permute-start(bf16[2,768,384]{2,1,0:T(8,128)(2,1)S(1)} %fusion.refs_5_), channel_id=1, source_target_pairs={{0,8},{2,10},{5,13},{7,15},{8,0},{10,2},{13,5},{15,7},{16,24},{18,... | collective-permute-start | bytes 3538952 | tf_op jit(solution)/shard_map/ppermute | solution.py:352
  59.2 1.1 copy-start.4
  60.3 1.1 copy-start.6
  61.3 1.1 copy-start.8
  72.6 30.9 %collective-permute-start.4 = (bf16[384,768]{1,0:T(8,128)(2,1)}, bf16[384,768]{1,0:T(8,128)(2,1)}, u32[]{:S(2)}, u32[]{:S(2)}) collective-permute-start(bf16[384,768]{1,0:T(8,128)(2,1)} %attend.1.refs_1_.refs_2_.refs_3_), channel_id=1, source_target_pairs={{0,16},{16,0},{1,17},{17,1},{2,18},{18,2},{3,19},{19,3},{4,20},{20... | collective-permute-start | bytes 1769480 | tf_op jit(solution)/shard_map/ppermute | solution.py:22
  73.9 35.6 %collective-permute-start.10 = (bf16[2,768,256]{2,1,0:T(8,128)(2,1)}, bf16[2,768,256]{2,1,0:T(8,128)(2,1)}, u32[]{:S(2)}, u32[]{:S(2)}) collective-permute-start(bf16[2,768,256]{2,1,0:T(8,128)(2,1)} %collective-permute-done.9.refs_8_), channel_id=1, source_target_pairs={{0,4},{2,6},{5,1},{7,3},{8,12},{10,14},{13,9},{15,11},{16,20},{18,... | collective-permute-start | bytes 2359304 | tf_op jit(solution)/shard_map/ppermute | solution.py:352
  101.1 2.3 %collective-permute-start.7 = (bf16[384,768]{1,0:T(8,128)(2,1)}, bf16[384,768]{1,0:T(8,128)(2,1)}, u32[]{:S(2)}, u32[]{:S(2)}) collective-permute-start(bf16[384,768]{1,0:T(8,128)(2,1)} %attend.1.refs_1_.refs_2_.refs_3_), channel_id=1, source_target_pairs={{0,1},{1,0},{2,3},{3,2},{4,5},{5,4},{6,7},{7,6},{8,9},{9,8},{10,11... | collective-permute-start | bytes 1769480 | tf_op jit(solution)/shard_map/ppermute | solution.py:22
  101.1 21.4 %collective-permute-start.15 = (bf16[2,768,384]{2,1,0:T(8,128)(2,1)}, bf16[2,768,384]{2,1,0:T(8,128)(2,1)}, u32[]{:S(2)}, u32[]{:S(2)}) collective-permute-start(bf16[2,768,384]{2,1,0:T(8,128)(2,1)} %held.7.refs_7_), channel_id=1, source_target_pairs={{0,4},{2,6},{5,1},{7,3},{8,12},{10,14},{13,9},{15,11},{16,20},{18,... | collective-permute-start | bytes 3538952 | tf_op jit(solution)/shard_map/ppermute | solution.py:352
  103.5 6.1 %collective-permute-start.8 = (bf16[384,768]{1,0:T(8,128)(2,1)}, bf16[384,768]{1,0:T(8,128)(2,1)}, u32[]{:S(2)}, u32[]{:S(2)}) collective-permute-start(bf16[384,768]{1,0:T(8,128)(2,1)} %collective-permute-done.4.refs_2_.refs_3_.refs_4_), channel_id=1, source_target_pairs={{0,1},{1,0},{2,3},{3,2},{4,5},{5,4},{6,7},{7,6},{8,9},{9,8},{10,11... | collective-permute-start | bytes 1769480 | tf_op jit(solution)/shard_map/ppermute | solution.py:22
  109.5 3.5 %copy-start.1 = (bf16[2,768,256]{2,1,0:T(8,128)(2,1)S(1)}, bf16[2,768,256]{2,1,0:T(8,128)(2,1)}, u32[]{:S(2)}) copy-start(bf16[2,768,256]{2,1,0:T(8,128)(2,1)} %fusion.1.refs_6_) | copy-start | bytes 2359300
  118.7 12.1 %collective-permute-start.11 = (bf16[384,256]{1,0:T(8,128)(2,1)}, bf16[384,256]{1,0:T(8,128)(2,1)}, u32[]{:S(2)}, u32[]{:S(2)}) collective-permute-start(bf16[384,256]{1,0:T(8,128)(2,1)} %get-tuple-element.29.refs_9_), channel_id=1, source_target_pairs={{0,2},{1,3},{2,0},{3,1},{4,6},{5,7},{6,4},{7,5},{8,10},{9,11},{10,... | collective-permute-start | bytes 589832 | tf_op jit(solution)/shard_map/ppermute | solution.py:22
  120.6 10.2 %collective-permute-start.12 = (bf16[384,256]{1,0:T(8,128)(2,1)}, bf16[384,256]{1,0:T(8,128)(2,1)}, u32[]{:S(2)}, u32[]{:S(2)}) collective-permute-start(bf16[384,256]{1,0:T(8,128)(2,1)} %get-tuple-element.30), channel_id=1, source_target_pairs={{0,16},{16,0},{1,17},{17,1},{2,18},{18,2},{3,19},{19,3},{4,20},{20... | collective-permute-start | bytes 589832 | tf_op jit(solution)/shard_map/ppermute | solution.py:22
  121.9 9.0 %collective-permute-start.13 = (bf16[384,256]{1,0:T(8,128)(2,1)}, bf16[384,256]{1,0:T(8,128)(2,1)}, u32[]{:S(2)}, u32[]{:S(2)}) collective-permute-start(bf16[384,256]{1,0:T(8,128)(2,1)} %get-tuple-element.31), channel_id=1, source_target_pairs={{0,18},{1,19},{2,16},{3,17},{16,2},{17,3},{18,0},{19,1},{4,22},{5,... | collective-permute-start | bytes 589832 | tf_op jit(solution)/shard_map/ppermute | solution.py:80
  126.9 0.8 copy-start.2
  127.8 9.5 %collective-permute-start.16 = (bf16[384,384]{1,0:T(8,128)(2,1)}, bf16[384,384]{1,0:T(8,128)(2,1)}, u32[]{:S(2)}, u32[]{:S(2)}) collective-permute-start(bf16[384,384]{1,0:T(8,128)(2,1)} %get-tuple-element.36), channel_id=1, source_target_pairs={{0,2},{1,3},{2,0},{3,1},{4,6},{5,7},{6,4},{7,5},{8,10},{9,11},{10,... | collective-permute-start | bytes 884744 | tf_op jit(solution)/shard_map/ppermute | solution.py:22
  129.3 13.6 %collective-permute-start.17 = (bf16[384,384]{1,0:T(8,128)(2,1)}, bf16[384,384]{1,0:T(8,128)(2,1)}, u32[]{:S(2)}, u32[]{:S(2)}) collective-permute-start(bf16[384,384]{1,0:T(8,128)(2,1)} %get-tuple-element.37), channel_id=1, source_target_pairs={{0,16},{16,0},{1,17},{17,1},{2,18},{18,2},{3,19},{19,3},{4,20},{20... | collective-permute-start | bytes 884744 | tf_op jit(solution)/shard_map/ppermute | solution.py:22
  130.8 12.1 %collective-permute-start.18 = (bf16[384,384]{1,0:T(8,128)(2,1)}, bf16[384,384]{1,0:T(8,128)(2,1)}, u32[]{:S(2)}, u32[]{:S(2)}) collective-permute-start(bf16[384,384]{1,0:T(8,128)(2,1)} %get-tuple-element.38), channel_id=1, source_target_pairs={{0,18},{1,19},{2,16},{3,17},{16,2},{17,3},{18,0},{19,1},{4,22},{5,... | collective-permute-start | bytes 884744 | tf_op jit(solution)/shard_map/ppermute | solution.py:80
  130.9 12.1 %copy-start.3 = (f32[384,384]{1,0:T(8,128)S(1)}, f32[384,384]{1,0:T(8,128)}, u32[]{:S(2)}) copy-start(f32[384,384]{1,0:T(8,128)} %copy-done.2) | copy-start | bytes 1769476

commit v7 on v6

--- a/solution.py
+++ b/solution.py
@@ -309,27 +309,44 @@
     )(*arrays, *earlier)
 
 
-def gated(gate_scale, parts, video, earlier=()):
-    rows = parts[0][0][0].shape[0]
-    width = sum(near[0].shape[1] for near, _ in parts)
+def gated(gate_scale, parts, video, starts, shape, before=()):
+    rows, width = shape[0], shape[1] // 2
 
     def kernel(video_ref, gate_ref, *refs):
-        part_refs, out_ref = list(refs[:-1]), refs[-1]
-        starts = video_ref[0] * width, (1 - video_ref[0]) * width
-        column = 0
-        for part in parts:
-            for start, half in zip(starts, part):
+        part_refs = list(refs[: sum(len(half) for part in parts for half in part)])
+        out_ref, *held_refs, landed = refs[len(part_refs) + len(before) :]
+        halves = video_ref[0] * width, (1 - video_ref[0]) * width
+        copies = []
+        for part, start in zip(parts, starts):
+            for half_start, half in zip(halves, part):
                 total = f32(part_refs.pop(0)[...])
                 for _ in half[1:]:
                     total = total + f32(part_refs.pop(0)[...])
-                columns = pl.ds(pl.multiple_of(start + column, TILE), total.shape[1])
-                out_ref[:, columns] = (gate_ref[:, columns] * total).astype(out_ref.dtype)
-            column += part[0][0].shape[1]
+                columns = pl.ds(pl.multiple_of(half_start + start, TILE), total.shape[1])
+                held_ref = held_refs[len(copies)]
+                held_ref[...] = (gate_ref[:, columns] * total).astype(held_ref.dtype)
+                copies.append(
+                    pltpu.make_async_copy(held_ref, out_ref.at[:, columns], landed.at[len(copies)])
+                )
+                copies[-1].start()
+        for copy in copies:
+            copy.wait()
 
     arrays = [array for part in parts for half in part for array in half]
-    out = jax.ShapeDtypeStruct((rows, 2 * width), jnp.bfloat16)
-    arrays = (gate_scale.reshape(1, -1), *arrays)
-    return local_call(kernel, [out], (video,), arrays, earlier, "gated")[0]
+    arrays = (jnp.int32(video).reshape(1), gate_scale.reshape(1, -1), *arrays)
+    return pl.pallas_call(
+        kernel,
+        out_shape=jax.ShapeDtypeStruct(shape, jnp.bfloat16),
+        in_specs=[SMEM] + [WHOLE] * (len(arrays) - 1) + [LATER] * len(before),
+        out_specs=LATER,
+        scratch_shapes=[
+            pltpu.VMEM((rows, half[0].shape[1]), jnp.bfloat16) for part in parts for half in part
+        ]
+        + [pltpu.SemaphoreType.DMA((2 * len(parts),))],
+        input_output_aliases={len(arrays): 0} if before else {},
+        compiler_params=pltpu.CompilerParams(vmem_limit_bytes=16 * 2**20),
+        name="gated",
+    )(*arrays, *before)
 
 
 def square_mesh(queries, key_rows, value_rows, keep_tiles, out_weight, gate_scale):
@@ -339,6 +356,7 @@
     width = out_weight.shape[1] // 2
     starts = [width * place // 5 // TILE * TILE for place in STARTS]
     spans = list(zip(starts, starts[1:] + [width]))
+    rows = queries.shape[0]
     role = (slab ^ head) & 1
     first = slab // 2 == head // 2
 
@@ -390,7 +408,10 @@
         if len(summed) < len(parts) - 1:
             arrived = held(arrived, [], 100 * 2**33)
         summed.append(((near, arrived[0]), arrived[1:]))
-    return gated(gate_scale, summed, video)
+    out = ()
+    for part, (start, _) in zip(summed, spans):
+        out = (gated(gate_scale, [part], video, [start], (rows, 2 * width), out),)
+    return out[0]
 
 
 def solution(mesh):

time: 146 us -> 146 us (level)
  waiting for transfers between devices: 84.4 us -> 82.4 us
    pallas_call x0 -> x2, Pallas kernels: none -> 4.04 us  [gated(): pl.pallas_call(kernel, out_shape=jax.ShapeDtypeStruct(shape, jnp.bfloat16...]
    pallas_call x4 -> x3, Pallas kernels: 16.2 us -> 13.6 us  [local_call(): pl.pallas_call(body, out_shape=outs, in_specs=[SMEM] * len(flags) + [WHOL...]
    ppermute x7, waiting for transfers between devices: 13.1 us -> 11.1 us  [swapped(): return lax.ppermute(array, axis, [(i, i ^ mask) for i in range(count)])]
  transfers between devices with their start and end apart: 19 -> 19, of which waited for: 10 -> 10; matrix products, arithmetic and copies ran while one was open for 2% -> 2% of each run, Pallas kernels for 16% -> 18%
where the time goes in v7:
time: 146 us; the launch traced here: 145 us
  waiting for transfers between devices  82.4 us (56%)
  Pallas kernels  27.8 us (19%)
  starting transfers between devices  24.5 us (17%)
  local copies, waits for them, and re-layouts  7.51 us (5%)
  other arithmetic  2.59 us (2%)
    ppermute x4, waiting for transfers between devices, passed_along(): lax.ppermute(array, axis, [(i, (i + by) % count) for i in range(count)])  39.6 us
    ppermute x6, waiting for transfers between devices, passed(): return lax.ppermute(array, ('tm', 'head'), pairs)  31.7 us
    pallas_call x3, Pallas kernels, local_call(): pl.pallas_call(body, out_shape=outs, in_specs=[SMEM] * len(flags) + [WHOL...  13.6 us
    ppermute x7, waiting for transfers between devices, swapped(): return lax.ppermute(array, axis, [(i, i ^ mask) for i in range(count)])  11.1 us
    pallas_call x1, Pallas kernels, attend(): pl.pallas_call(functools.partial(attend_kernel, len(key_slabs) // 2, 1.0...  10.2 us
    ppermute x6, starting transfers between devices, passed(): return lax.ppermute(array, ('tm', 'head'), pairs)  9.14 us
    ppermute x7, starting transfers between devices, swapped(): return lax.ppermute(array, axis, [(i, i ^ mask) for i in range(count)])  8.49 us
    unnamed x24, local copies, waits for them, and re-layouts  7.34 us
  transfers between devices with their start and end apart: 19, of which 10 were waited for; matrix products, arithmetic and copies ran while one was open for 2% of the time, Pallas kernels for 18%

profile of v7, /device:TPU:1, one launch (start us, length us, event | category | flops | bytes accessed | tf_op | source)
XLA Modules:
  0.0 145.0 jit_solution(9093674040144341150)
XLA Ops:
  0.0 1.5 %copy-done = bf16[768,1280]{1,0:T(8,128)(2,1)S(1)} copy-done((bf16[768,1280]{1,0:T(8,128)(2,1)S(1)}, bf16[768,1280]{1,0:T(8,128)(2,1)}, u32[]{:S(2)}) %copy-start) | copy-done | bytes 1966104
  1.6 2.0 %collective-permute-start.5 = (bf16[768,640]{1,0:T(8,128)(2,1)S(1)}, bf16[768,640]{1,0:T(8,128)(2,1)S(1)}, u32[]{:S(2)}, u32[]{:S(2)}) collective-permute-start(bf16[768,640]{1,0:T(8,128)(2,1)S(1)} %constant_dynamic-slice_fusion), channel_id=1, source_target_pairs={{1,0},{3,2},{4,5},{6,7},{9,8},{11,10},{12,13},{14,15},{17,16},{19,... | collective-permute-start | bytes 2949128 | tf_op jit(solution)/shard_map/ppermute | solution.py:370
  3.7 1.4 collective-permute-start
  5.1 2.1 %collective-permute-start.1 = (bf16[384,6,128]{2,0,1:T(8,128)(2,1)}, bf16[384,6,128]{2,0,1:T(8,128)(2,1)S(1)}, u32[]{:S(2)}, u32[]{:S(2)}) collective-permute-start(bf16[384,6,128]{2,0,1:T(8,128)(2,1)} %param.7), channel_id=1, source_target_pairs={{0,12},{4,0},{8,4},{12,8},{1,13},{5,1},{9,5},{13,9},{2,14},{6,2},{... | collective-permute-start | bytes 1769480 | tf_op jit(solution)/shard_map/ppermute | solution.py:17
  7.8 2.7 %collective-permute-start.3 = (bf16[384,6,128]{2,0,1:T(8,128)(2,1)}, bf16[384,6,128]{2,0,1:T(8,128)(2,1)}, u32[]{:S(2)}, u32[]{:S(2)}) collective-permute-start(bf16[384,6,128]{2,0,1:T(8,128)(2,1)} %param.8), channel_id=1, source_target_pairs={{0,12},{4,0},{8,4},{12,8},{1,13},{5,1},{9,5},{13,9},{2,14},{6,2},{... | collective-permute-start | bytes 1769480 | tf_op jit(solution)/shard_map/ppermute | solution.py:17
  11.7 1.5 %pad_maximum_fusion = bf16[2,768,640]{2,1,0:T(8,128)(2,1)} fusion(bf16[1,768,640]{2,1,0:T(8,128)(2,1)S(1)} %bitcast.24, bf16[1,768,640]{2,1,0:T(8,128)(2,1)S(1)} %fusion.2), kind=kLoop, calls=%fused_computation.2 | loop fusion | flops 983040 | bytes 3932160 | tf_op jit(solution)/shard_map/stack | solution.py:374
  13.2 6.7 %collective-permute-done = bf16[384,6,128]{2,0,1:T(8,128)(2,1)S(1)} collective-permute-done((bf16[384,6,128]{2,0,1:T(8,128)(2,1)}, bf16[384,6,128]{2,0,1:T(8,128)(2,1)S(1)}, u32[]{:S(2)}, u32[]{:S(2)}) %collective-permute-start) | collective-permute-done | bytes 589856 | tf_op jit(solution)/shard_map/ppermute | solution.py:17
  20.7 14.4 %collective-permute-done.1 = bf16[384,6,128]{2,0,1:T(8,128)(2,1)S(1)} collective-permute-done((bf16[384,6,128]{2,0,1:T(8,128)(2,1)}, bf16[384,6,128]{2,0,1:T(8,128)(2,1)S(1)}, u32[]{:S(2)}, u32[]{:S(2)}) %collective-permute-start.1) | collective-permute-done | bytes 589856 | tf_op jit(solution)/shard_map/ppermute | solution.py:17
  36.0 1.3 collective-permute-start.6
  37.4 1.6 %collective-permute-start.11 = (bf16[2,768,256]{2,1,0:T(8,128)(2,1)}, bf16[2,768,256]{2,1,0:T(8,128)(2,1)}, u32[]{:S(2)}, u32[]{:S(2)}) collective-permute-start(bf16[2,768,256]{2,1,0:T(8,128)(2,1)} %fusion.1.refs_6_), channel_id=1, source_target_pairs={{0,8},{2,10},{5,13},{7,15},{8,0},{10,2},{13,5},{15,7},{16,24},{18,... | collective-permute-start | bytes 2359304 | tf_op jit(solution)/shard_map/ppermute | solution.py:370
  39.0 1.7 %collective-permute-start.9 = (bf16[2,768,384]{2,1,0:T(8,128)(2,1)S(1)}, bf16[2,768,384]{2,1,0:T(8,128)(2,1)}, u32[]{:S(2)}, u32[]{:S(2)}) collective-permute-start(bf16[2,768,384]{2,1,0:T(8,128)(2,1)S(1)} %fusion.refs_5_), channel_id=1, source_target_pairs={{0,8},{2,10},{5,13},{7,15},{8,0},{10,2},{13,5},{15,7},{16,24},{18,... | collective-permute-start | bytes 3538952 | tf_op jit(solution)/shard_map/ppermute | solution.py:370
  40.7 4.6 %collective-permute-done.2 = bf16[384,6,128]{2,0,1:T(8,128)(2,1)} collective-permute-done((bf16[384,6,128]{2,0,1:T(8,128)(2,1)}, bf16[384,6,128]{2,0,1:T(8,128)(2,1)}, u32[]{:S(2)}, u32[]{:S(2)}) %collective-permute-start.2) | collective-permute-done | bytes 589856 | tf_op jit(solution)/shard_map/ppermute | solution.py:17
  45.3 13.9 %collective-permute-done.3 = bf16[384,6,128]{2,0,1:T(8,128)(2,1)} collective-permute-done((bf16[384,6,128]{2,0,1:T(8,128)(2,1)}, bf16[384,6,128]{2,0,1:T(8,128)(2,1)}, u32[]{:S(2)}, u32[]{:S(2)}) %collective-permute-start.3) | collective-permute-done | bytes 589856 | tf_op jit(solution)/shard_map/ppermute | solution.py:17
  59.2 1.1 copy-done.4
  60.3 1.1 copy-done.6
  62.4 10.2 %attend.1.refs_1_.refs_2_.refs_3_ = bf16[384,768]{1,0:T(8,128)(2,1)} custom-call(f32[3,1152]{1,0:T(4,128)S(1)} %bitcast.18, bf16[6,384,128]{2,1,0:T(8,128)(2,1)S(1)} %bitcast.19, bf16[6,384,128]{2,1,0:T(8,128)(2,1)S(1)} %bitcast.20, bf16[6,384,128]{2,1,0:T(8,128)(2,1)} %bitcast.5.refs_1_, bf16[6,384,128]{2,1,0:T(8,128)(2,1)S(1)} %bitcast.21, ...), custom_call_target="tpu_custom_call" | custom-call | flops 20000000000 | bytes 10000000 | tf_op jit(solution)/shard_map/attend/pallas_call | solution.py:56
  72.6 1.3 collective-permute-start.4
  73.9 1.3 collective-permute-start.12
  75.2 25.9 %collective-permute-done.6.refs_6_.refs_7_ = bf16[2,768,640]{2,1,0:T(8,128)(2,1)} collective-permute-done((bf16[2,768,640]{2,1,0:T(8,128)(2,1)}, bf16[2,768,640]{2,1,0:T(8,128)(2,1)}, u32[]{:S(2)}, u32[]{:S(2)}) %collective-permute-start.6) | collective-permute-done | bytes 1966112 | tf_op jit(solution)/shard_map/ppermute | solution.py:370
  101.1 1.3 collective-permute-start.10
  104.4 5.1 %collective-permute-done.12.refs_0_ = bf16[2,768,256]{2,1,0:T(8,128)(2,1)} collective-permute-done((bf16[2,768,256]{2,1,0:T(8,128)(2,1)}, bf16[2,768,256]{2,1,0:T(8,128)(2,1)}, u32[]{:S(2)}, u32[]{:S(2)}) %collective-permute-start.12) | collective-permute-done | bytes 786464 | tf_op jit(solution)/shard_map/ppermute | solution.py:370
  109.5 3.5 %early_terms.1.refs_10_.refs_2_ = f32[2,384,384]{2,1,0:T(8,128)S(1)} custom-call(s32[1]{0:T(128)} %bitcast.1.refs_0_, bf16[384,768]{1,0:T(8,128)(2,1)} %attend.1.refs_1_.refs_2_.refs_3_, bf16[384,768]{1,0:T(8,128)(2,1)} %collective-permute-done.4.refs_2_.refs_3_.refs_4_, bf16[384,768]{1,0:T(8,128)(2,1)} %held.4.refs_3_.refs_4_.refs_5_, ...), custom_call_target="tpu_custom_call" | custom-call | bytes 6684672 | tf_op jit(solution)/shard_map/early_terms/pallas_call | solution.py:122
  113.0 5.6 %terms.1 = (f32[384,256]{1,0:T(8,128)S(1)}, bf16[384,256]{1,0:T(8,128)(2,1)}, bf16[384,256]{1,0:T(8,128)(2,1)}, bf16[384,256]{1,0:T(8,128)(2,1)}) custom-call(s32[1]{0:T(128)} %bitcast.1.refs_0_, s32[1]{0:T(128)} %bitcast.2.refs_1_, bf16[384,768]{1,0:T(8,128)(2,1)} %attend.1.refs_1_.refs_2_.refs_3_, ...), custom_call_target="tpu_custom_call" | custom-call | flops 858993459200 | bytes 7667712 | tf_op jit(solution)/shard_map/terms/pallas_call | solution.py:122
  118.6 1.9 %collective-permute-start.16 = (bf16[384,256]{1,0:T(8,128)(2,1)}, bf16[384,256]{1,0:T(8,128)(2,1)}, u32[]{:S(2)}, u32[]{:S(2)}) collective-permute-start(bf16[384,256]{1,0:T(8,128)(2,1)} %get-tuple-element.28.refs_9_), channel_id=1, source_target_pairs={{0,2},{1,3},{2,0},{3,1},{4,6},{5,7},{6,4},{7,5},{8,10},{9,11},{10,... | collective-permute-start | bytes 589832 | tf_op jit(solution)/shard_map/ppermute | solution.py:22
  120.6 1.2 collective-permute-start.17
  122.5 4.5 %late_terms.1 = (f32[384,384]{1,0:T(8,128)S(1)}, bf16[384,384]{1,0:T(8,128)(2,1)}, bf16[384,384]{1,0:T(8,128)(2,1)}, bf16[384,384]{1,0:T(8,128)(2,1)}) custom-call(s32[1]{0:T(128)} %bitcast.1.refs_0_, s32[1]{0:T(128)} %bitcast.2.refs_1_, f32[2,384,384]{2,1,0:T(8,128)S(1)} %early_terms.1.refs_10_.refs_2_, bf16[384,768]{1,0:T(8,128)(2,1)} %attend.1.refs_1_.refs_2_.refs_3_, ...), custom_call_target="tpu_custom_call" | custom-call | flops 858993459200 | bytes 7372800 | tf_op jit(solution)/shard_map/late_terms/pallas_call | solution.py:122
  127.8 1.6 %collective-permute-start.13 = (bf16[384,384]{1,0:T(8,128)(2,1)}, bf16[384,384]{1,0:T(8,128)(2,1)}, u32[]{:S(2)}, u32[]{:S(2)}) collective-permute-start(bf16[384,384]{1,0:T(8,128)(2,1)} %get-tuple-element.30), channel_id=1, source_target_pairs={{0,2},{1,3},{2,0},{3,1},{4,6},{5,7},{6,4},{7,5},{8,10},{9,11},{10,... | collective-permute-start | bytes 884744 | tf_op jit(solution)/shard_map/ppermute | solution.py:22
  129.3 1.5 %collective-permute-start.14 = (bf16[384,384]{1,0:T(8,128)(2,1)}, bf16[384,384]{1,0:T(8,128)(2,1)}, u32[]{:S(2)}, u32[]{:S(2)}) collective-permute-start(bf16[384,384]{1,0:T(8,128)(2,1)} %get-tuple-element.31), channel_id=1, source_target_pairs={{0,16},{16,0},{1,17},{17,1},{2,18},{18,2},{3,19},{19,3},{4,20},{20... | collective-permute-start | bytes 884744 | tf_op jit(solution)/shard_map/ppermute | solution.py:22
  130.9 2.0 %gated.2.refs_4_ = bf16[384,1280]{1,0:T(8,128)(2,1)} custom-call(s32[1]{0:T(128)} %bitcast.video_ref, f32[1,1280]{1,0:T(1,128)S(1)} %reshape.23.gate_ref, f32[384,256]{1,0:T(8,128)S(1)} %get-tuple-element.33.refs_0_, bf16[384,256]{1,0:T(8,128)(2,1)} %get-tuple-element.36.refs_1_, bf16[384,256]{1,0:T(8,128)(2,1)} %get-tuple-element.37.refs_2_, ...), custom_call_target="tpu_custom_call" | custom-call | tf_op jit(solution)/shard_map/gated/pallas_call | solution.py:337
  132.9 4.4 %collective-permute-done.13.refs_1_ = bf16[384,384]{1,0:T(8,128)(2,1)} collective-permute-done((bf16[384,384]{1,0:T(8,128)(2,1)}, bf16[384,384]{1,0:T(8,128)(2,1)}, u32[]{:S(2)}, u32[]{:S(2)}) %collective-permute-start.13) | collective-permute-done | bytes 294944 | tf_op jit(solution)/shard_map/ppermute | solution.py:22
  137.3 5.6 %collective-permute-done.14.refs_2_ = bf16[384,384]{1,0:T(8,128)(2,1)} collective-permute-done((bf16[384,384]{1,0:T(8,128)(2,1)}, bf16[384,384]{1,0:T(8,128)(2,1)}, u32[]{:S(2)}, u32[]{:S(2)}) %collective-permute-start.14) | collective-permute-done | bytes 294944 | tf_op jit(solution)/shard_map/ppermute | solution.py:22
  142.9 2.1 %gated.3 = bf16[384,1280]{1,0:T(8,128)(2,1)} custom-call(s32[1]{0:T(128)} %bitcast.video_ref, f32[1,1280]{1,0:T(1,128)S(1)} %reshape.23.gate_ref, f32[384,384]{1,0:T(8,128)S(1)} %copy-done.3, bf16[384,384]{1,0:T(8,128)(2,1)} %collective-permute-done.13.refs_1_, bf16[384,384]{1,0:T(8,128)(2,1)} %collective-permute-done.14.refs_2_, ...), custom_call_target="tpu_custom_call", output_to_operand_aliasing={{}: (6, {})} | custom-call | tf_op jit(solution)/shard_map/gated/pallas_call | solution.py:337
  (47 shorter events, 8.2 us)
Async XLA Ops:
  0.0 1.5 %copy-start = (bf16[768,1280]{1,0:T(8,128)(2,1)S(1)}, bf16[768,1280]{1,0:T(8,128)(2,1)}, u32[]{:S(2)}) copy-start(bf16[768,1280]{1,0:T(8,128)(2,1)} %param.10) | copy-start | bytes 5898244
  0.0 10.5 %copy-start.10 = (s32[3,9]{1,0:T(4,128)S(1)}, s32[3,9]{1,0:T(4,128)}, u32[]{:S(2)}) copy-start(s32[3,9]{1,0:T(4,128)} %param.9) | copy-start | bytes 328
  1.6 8.9 %collective-permute-start.5 = (bf16[768,640]{1,0:T(8,128)(2,1)S(1)}, bf16[768,640]{1,0:T(8,128)(2,1)S(1)}, u32[]{:S(2)}, u32[]{:S(2)}) collective-permute-start(bf16[768,640]{1,0:T(8,128)(2,1)S(1)} %constant_dynamic-slice_fusion), channel_id=1, source_target_pairs={{1,0},{3,2},{4,5},{6,7},{9,8},{11,10},{12,13},{14,15},{17,16},{19,... | collective-permute-start | bytes 2949128 | tf_op jit(solution)/shard_map/ppermute | solution.py:370
  3.7 16.2 %collective-permute-start = (bf16[384,6,128]{2,0,1:T(8,128)(2,1)}, bf16[384,6,128]{2,0,1:T(8,128)(2,1)S(1)}, u32[]{:S(2)}, u32[]{:S(2)}) collective-permute-start(bf16[384,6,128]{2,0,1:T(8,128)(2,1)} %param.7), channel_id=1, source_target_pairs={{0,4},{4,8},{8,12},{12,0},{1,5},{5,9},{9,13},{13,1},{2,6},{6,10},{... | collective-permute-start | bytes 1769480 | tf_op jit(solution)/shard_map/ppermute | solution.py:17
  5.1 30.0 %collective-permute-start.1 = (bf16[384,6,128]{2,0,1:T(8,128)(2,1)}, bf16[384,6,128]{2,0,1:T(8,128)(2,1)S(1)}, u32[]{:S(2)}, u32[]{:S(2)}) collective-permute-start(bf16[384,6,128]{2,0,1:T(8,128)(2,1)} %param.7), channel_id=1, source_target_pairs={{0,12},{4,0},{8,4},{12,8},{1,13},{5,1},{9,5},{13,9},{2,14},{6,2},{... | collective-permute-start | bytes 1769480 | tf_op jit(solution)/shard_map/ppermute | solution.py:17
  7.2 38.1 %collective-permute-start.2 = (bf16[384,6,128]{2,0,1:T(8,128)(2,1)}, bf16[384,6,128]{2,0,1:T(8,128)(2,1)}, u32[]{:S(2)}, u32[]{:S(2)}) collective-permute-start(bf16[384,6,128]{2,0,1:T(8,128)(2,1)} %param.8), channel_id=1, source_target_pairs={{0,4},{4,8},{8,12},{12,0},{1,5},{5,9},{9,13},{13,1},{2,6},{6,10},{... | collective-permute-start | bytes 1769480 | tf_op jit(solution)/shard_map/ppermute | solution.py:17
  7.8 51.4 %collective-permute-start.3 = (bf16[384,6,128]{2,0,1:T(8,128)(2,1)}, bf16[384,6,128]{2,0,1:T(8,128)(2,1)}, u32[]{:S(2)}, u32[]{:S(2)}) collective-permute-start(bf16[384,6,128]{2,0,1:T(8,128)(2,1)} %param.8), channel_id=1, source_target_pairs={{0,12},{4,0},{8,4},{12,8},{1,13},{5,1},{9,5},{13,9},{2,14},{6,2},{... | collective-permute-start | bytes 1769480 | tf_op jit(solution)/shard_map/ppermute | solution.py:17
  11.7 25.7 %copy-start.9 = (f32[1280]{0:T(1024)S(1)}, f32[1280]{0:T(1024)}, u32[]{:S(2)}) copy-start(f32[1280]{0:T(1024)} %param.11) | copy-start | bytes 15364
  19.9 0.8 copy-start.5
  35.1 0.9 copy-start.7
  36.0 65.1 %collective-permute-start.6 = (bf16[2,768,640]{2,1,0:T(8,128)(2,1)}, bf16[2,768,640]{2,1,0:T(8,128)(2,1)}, u32[]{:S(2)}, u32[]{:S(2)}) collective-permute-start(bf16[2,768,640]{2,1,0:T(8,128)(2,1)} %pad_maximum_fusion), channel_id=1, source_target_pairs={{0,4},{2,6},{5,1},{7,3},{8,12},{10,14},{13,9},{15,11},{16,20},{18,... | collective-permute-start | bytes 5898248 | tf_op jit(solution)/shard_map/ppermute | solution.py:370
  37.4 36.5 %collective-permute-start.11 = (bf16[2,768,256]{2,1,0:T(8,128)(2,1)}, bf16[2,768,256]{2,1,0:T(8,128)(2,1)}, u32[]{:S(2)}, u32[]{:S(2)}) collective-permute-start(bf16[2,768,256]{2,1,0:T(8,128)(2,1)} %fusion.1.refs_6_), channel_id=1, source_target_pairs={{0,8},{2,10},{5,13},{7,15},{8,0},{10,2},{13,5},{15,7},{16,24},{18,... | collective-permute-start | bytes 2359304 | tf_op jit(solution)/shard_map/ppermute | solution.py:370
  39.0 62.1 %collective-permute-start.9 = (bf16[2,768,384]{2,1,0:T(8,128)(2,1)S(1)}, bf16[2,768,384]{2,1,0:T(8,128)(2,1)}, u32[]{:S(2)}, u32[]{:S(2)}) collective-permute-start(bf16[2,768,384]{2,1,0:T(8,128)(2,1)S(1)} %fusion.refs_5_), channel_id=1, source_target_pairs={{0,8},{2,10},{5,13},{7,15},{8,0},{10,2},{13,5},{15,7},{16,24},{18,... | collective-permute-start | bytes 3538952 | tf_op jit(solution)/shard_map/ppermute | solution.py:370
  59.2 1.1 copy-start.4
  60.3 1.1 copy-start.6
  61.3 1.1 copy-start.8
  72.6 30.9 %collective-permute-start.4 = (bf16[384,768]{1,0:T(8,128)(2,1)}, bf16[384,768]{1,0:T(8,128)(2,1)}, u32[]{:S(2)}, u32[]{:S(2)}) collective-permute-start(bf16[384,768]{1,0:T(8,128)(2,1)} %attend.1.refs_1_.refs_2_.refs_3_), channel_id=1, source_target_pairs={{0,16},{16,0},{1,17},{17,1},{2,18},{18,2},{3,19},{19,3},{4,20},{20... | collective-permute-start | bytes 1769480 | tf_op jit(solution)/shard_map/ppermute | solution.py:22
  73.9 35.6 %collective-permute-start.12 = (bf16[2,768,256]{2,1,0:T(8,128)(2,1)}, bf16[2,768,256]{2,1,0:T(8,128)(2,1)}, u32[]{:S(2)}, u32[]{:S(2)}) collective-permute-start(bf16[2,768,256]{2,1,0:T(8,128)(2,1)} %collective-permute-done.11.refs_8_), channel_id=1, source_target_pairs={{0,4},{2,6},{5,1},{7,3},{8,12},{10,14},{13,9},{15,11},{16,20},{18,... | collective-permute-start | bytes 2359304 | tf_op jit(solution)/shard_map/ppermute | solution.py:370
  101.1 2.3 %collective-permute-start.7 = (bf16[384,768]{1,0:T(8,128)(2,1)}, bf16[384,768]{1,0:T(8,128)(2,1)}, u32[]{:S(2)}, u32[]{:S(2)}) collective-permute-start(bf16[384,768]{1,0:T(8,128)(2,1)} %attend.1.refs_1_.refs_2_.refs_3_), channel_id=1, source_target_pairs={{0,1},{1,0},{2,3},{3,2},{4,5},{5,4},{6,7},{7,6},{8,9},{9,8},{10,11... | collective-permute-start | bytes 1769480 | tf_op jit(solution)/shard_map/ppermute | solution.py:22
  101.1 21.4 %collective-permute-start.10 = (bf16[2,768,384]{2,1,0:T(8,128)(2,1)}, bf16[2,768,384]{2,1,0:T(8,128)(2,1)}, u32[]{:S(2)}, u32[]{:S(2)}) collective-permute-start(bf16[2,768,384]{2,1,0:T(8,128)(2,1)} %held.5.refs_7_), channel_id=1, source_target_pairs={{0,4},{2,6},{5,1},{7,3},{8,12},{10,14},{13,9},{15,11},{16,20},{18,... | collective-permute-start | bytes 3538952 | tf_op jit(solution)/shard_map/ppermute | solution.py:370
  103.5 6.1 %collective-permute-start.8 = (bf16[384,768]{1,0:T(8,128)(2,1)}, bf16[384,768]{1,0:T(8,128)(2,1)}, u32[]{:S(2)}, u32[]{:S(2)}) collective-permute-start(bf16[384,768]{1,0:T(8,128)(2,1)} %collective-permute-done.4.refs_2_.refs_3_.refs_4_), channel_id=1, source_target_pairs={{0,1},{1,0},{2,3},{3,2},{4,5},{5,4},{6,7},{7,6},{8,9},{9,8},{10,11... | collective-permute-start | bytes 1769480 | tf_op jit(solution)/shard_map/ppermute | solution.py:22
  109.5 3.5 %copy-start.1 = (bf16[2,768,256]{2,1,0:T(8,128)(2,1)S(1)}, bf16[2,768,256]{2,1,0:T(8,128)(2,1)}, u32[]{:S(2)}) copy-start(bf16[2,768,256]{2,1,0:T(8,128)(2,1)} %fusion.1.refs_6_) | copy-start | bytes 2359300
  118.6 12.2 %collective-permute-start.16 = (bf16[384,256]{1,0:T(8,128)(2,1)}, bf16[384,256]{1,0:T(8,128)(2,1)}, u32[]{:S(2)}, u32[]{:S(2)}) collective-permute-start(bf16[384,256]{1,0:T(8,128)(2,1)} %get-tuple-element.28.refs_9_), channel_id=1, source_target_pairs={{0,2},{1,3},{2,0},{3,1},{4,6},{5,7},{6,4},{7,5},{8,10},{9,11},{10,... | collective-permute-start | bytes 589832 | tf_op jit(solution)/shard_map/ppermute | solution.py:22
  120.6 10.3 %collective-permute-start.17 = (bf16[384,256]{1,0:T(8,128)(2,1)}, bf16[384,256]{1,0:T(8,128)(2,1)}, u32[]{:S(2)}, u32[]{:S(2)}) collective-permute-start(bf16[384,256]{1,0:T(8,128)(2,1)} %get-tuple-element.34), channel_id=1, source_target_pairs={{0,16},{16,0},{1,17},{17,1},{2,18},{18,2},{3,19},{19,3},{4,20},{20... | collective-permute-start | bytes 589832 | tf_op jit(solution)/shard_map/ppermute | solution.py:22
  121.8 9.1 %collective-permute-start.18 = (bf16[384,256]{1,0:T(8,128)(2,1)}, bf16[384,256]{1,0:T(8,128)(2,1)}, u32[]{:S(2)}, u32[]{:S(2)}) collective-permute-start(bf16[384,256]{1,0:T(8,128)(2,1)} %get-tuple-element.35), channel_id=1, source_target_pairs={{0,18},{1,19},{2,16},{3,17},{16,2},{17,3},{18,0},{19,1},{4,22},{5,... | collective-permute-start | bytes 589832 | tf_op jit(solution)/shard_map/ppermute | solution.py:80
  127.0 0.8 copy-start.2
  127.8 9.5 %collective-permute-start.13 = (bf16[384,384]{1,0:T(8,128)(2,1)}, bf16[384,384]{1,0:T(8,128)(2,1)}, u32[]{:S(2)}, u32[]{:S(2)}) collective-permute-start(bf16[384,384]{1,0:T(8,128)(2,1)} %get-tuple-element.30), channel_id=1, source_target_pairs={{0,2},{1,3},{2,0},{3,1},{4,6},{5,7},{6,4},{7,5},{8,10},{9,11},{10,... | collective-permute-start | bytes 884744 | tf_op jit(solution)/shard_map/ppermute | solution.py:22
  129.3 13.6 %collective-permute-start.14 = (bf16[384,384]{1,0:T(8,128)(2,1)}, bf16[384,384]{1,0:T(8,128)(2,1)}, u32[]{:S(2)}, u32[]{:S(2)}) collective-permute-start(bf16[384,384]{1,0:T(8,128)(2,1)} %get-tuple-element.31), channel_id=1, source_target_pairs={{0,16},{16,0},{1,17},{17,1},{2,18},{18,2},{3,19},{19,3},{4,20},{20... | collective-permute-start | bytes 884744 | tf_op jit(solution)/shard_map/ppermute | solution.py:22
  130.9 12.0 %collective-permute-start.15 = (bf16[384,384]{1,0:T(8,128)(2,1)}, bf16[384,384]{1,0:T(8,128)(2,1)}, u32[]{:S(2)}, u32[]{:S(2)}) collective-permute-start(bf16[384,384]{1,0:T(8,128)(2,1)} %get-tuple-element.32), channel_id=1, source_target_pairs={{0,18},{1,19},{2,16},{3,17},{16,2},{17,3},{18,0},{19,1},{4,22},{5,... | collective-permute-start | bytes 884744 | tf_op jit(solution)/shard_map/ppermute | solution.py:80
  130.9 12.0 %copy-start.3 = (f32[384,384]{1,0:T(8,128)S(1)}, f32[384,384]{1,0:T(8,128)}, u32[]{:S(2)}) copy-start(f32[384,384]{1,0:T(8,128)} %copy-done.2) | copy-start | bytes 1769476

commit v8 on v7

--- a/solution.py
+++ b/solution.py
@@ -240,21 +240,24 @@
                 pl.when(role_ref[0] == odd)(copy.start)
         for copy in copies:
             copy.start()
+        kept_refs, given_refs = (near_ref, far_ref), (near_given_ref, far_given_ref)
+        for stays, early_refs in ((1, kept_refs), (0, given_refs)):
+
+            @pl.when(first_ref[0] == stays)
+            def _():
+                for video in (0, 1):
+                    early_refs[video][...] = early_ref[video].astype(early_refs[video].dtype)
+
         for copy in copies + weight_copies(block_refs[0], starts[0], weight, landed):
             copy.wait()
         total = jnp.dot(held_rows[...], weight[...], preferred_element_type=jnp.float32)
-        kept_refs, given_refs = (near_ref, far_ref), (near_given_ref, far_given_ref)
-        for stays, late_refs, early_refs in (
-            (1, given_refs, kept_refs),
-            (0, kept_refs, given_refs),
-        ):
+        for stays, late_refs in ((1, given_refs), (0, kept_refs)):
 
             @pl.when(first_ref[0] == stays)
             def _():
                 for video in (0, 1):
                     late = total[video * rows : (video + 1) * rows]
                     late_refs[video][...] = late.astype(late_refs[video].dtype)
-                    early_refs[video][...] = early_ref[video].astype(early_refs[video].dtype)
 
     kinds = (jnp.float32, jnp.bfloat16, jnp.bfloat16, jnp.bfloat16)
     outs = [jax.ShapeDtypeStruct((rows, width), kind) for kind in kinds]

time: 146 us -> 145 us (level)
  no operation moved by 1% of the time
where the time goes in v8:
time: 145 us
  waiting for transfers between devices  82.4 us (57%)
  Pallas kernels  27.8 us (19%)
  starting transfers between devices  24.5 us (17%)
  local copies, waits for them, and re-layouts  7.51 us (5%)
  other arithmetic  2.59 us (2%)
    ppermute x4, waiting for transfers between devices, passed_along(): lax.ppermute(array, axis, [(i, (i + by) % count) for i in range(count)])  39.6 us
    ppermute x6, waiting for transfers between devices, passed(): return lax.ppermute(array, ('tm', 'head'), pairs)  31.7 us
    pallas_call x3, Pallas kernels, local_call(): pl.pallas_call(body, out_shape=outs, in_specs=[SMEM] * len(flags) + [WHOL...  13.5 us
    ppermute x7, waiting for transfers between devices, swapped(): return lax.ppermute(array, axis, [(i, i ^ mask) for i in range(count)])  11.1 us
    pallas_call x1, Pallas kernels, attend(): pl.pallas_call(functools.partial(attend_kernel, len(key_slabs) // 2, 1.0...  10.2 us
    ppermute x6, starting transfers between devices, passed(): return lax.ppermute(array, ('tm', 'head'), pairs)  9.14 us
    ppermute x7, starting transfers between devices, swapped(): return lax.ppermute(array, axis, [(i, i ^ mask) for i in range(count)])  8.49 us
    unnamed x24, local copies, waits for them, and re-layouts  7.34 us
  transfers between devices with their start and end apart: 19, of which 10 were waited for; matrix products, arithmetic and copies ran while one was open for 2% of the time, Pallas kernels for 18%

profile of v8, /device:TPU:1, one launch (start us, length us, event | category | flops | bytes accessed | tf_op | source)
XLA Modules:
  0.0 144.9 jit_solution(7012884713579223129)
XLA Ops:
  0.0 1.5 %copy-done = bf16[768,1280]{1,0:T(8,128)(2,1)S(1)} copy-done((bf16[768,1280]{1,0:T(8,128)(2,1)S(1)}, bf16[768,1280]{1,0:T(8,128)(2,1)}, u32[]{:S(2)}) %copy-start) | copy-done | bytes 1966104
  1.6 2.0 %collective-permute-start.5 = (bf16[768,640]{1,0:T(8,128)(2,1)S(1)}, bf16[768,640]{1,0:T(8,128)(2,1)S(1)}, u32[]{:S(2)}, u32[]{:S(2)}) collective-permute-start(bf16[768,640]{1,0:T(8,128)(2,1)S(1)} %constant_dynamic-slice_fusion), channel_id=1, source_target_pairs={{1,0},{3,2},{4,5},{6,7},{9,8},{11,10},{12,13},{14,15},{17,16},{19,... | collective-permute-start | bytes 2949128 | tf_op jit(solution)/shard_map/ppermute | solution.py:373
  3.7 1.4 collective-permute-start
  5.1 2.1 %collective-permute-start.1 = (bf16[384,6,128]{2,0,1:T(8,128)(2,1)}, bf16[384,6,128]{2,0,1:T(8,128)(2,1)S(1)}, u32[]{:S(2)}, u32[]{:S(2)}) collective-permute-start(bf16[384,6,128]{2,0,1:T(8,128)(2,1)} %param.7), channel_id=1, source_target_pairs={{0,12},{4,0},{8,4},{12,8},{1,13},{5,1},{9,5},{13,9},{2,14},{6,2},{... | collective-permute-start | bytes 1769480 | tf_op jit(solution)/shard_map/ppermute | solution.py:17
  7.8 2.7 %collective-permute-start.3 = (bf16[384,6,128]{2,0,1:T(8,128)(2,1)}, bf16[384,6,128]{2,0,1:T(8,128)(2,1)}, u32[]{:S(2)}, u32[]{:S(2)}) collective-permute-start(bf16[384,6,128]{2,0,1:T(8,128)(2,1)} %param.8), channel_id=1, source_target_pairs={{0,12},{4,0},{8,4},{12,8},{1,13},{5,1},{9,5},{13,9},{2,14},{6,2},{... | collective-permute-start | bytes 1769480 | tf_op jit(solution)/shard_map/ppermute | solution.py:17
  11.7 1.5 %pad_maximum_fusion = bf16[2,768,640]{2,1,0:T(8,128)(2,1)} fusion(bf16[1,768,640]{2,1,0:T(8,128)(2,1)S(1)} %bitcast.24, bf16[1,768,640]{2,1,0:T(8,128)(2,1)S(1)} %fusion.2), kind=kLoop, calls=%fused_computation.2 | loop fusion | flops 983040 | bytes 3932160 | tf_op jit(solution)/shard_map/stack | solution.py:377
  13.2 6.7 %collective-permute-done = bf16[384,6,128]{2,0,1:T(8,128)(2,1)S(1)} collective-permute-done((bf16[384,6,128]{2,0,1:T(8,128)(2,1)}, bf16[384,6,128]{2,0,1:T(8,128)(2,1)S(1)}, u32[]{:S(2)}, u32[]{:S(2)}) %collective-permute-start) | collective-permute-done | bytes 589856 | tf_op jit(solution)/shard_map/ppermute | solution.py:17
  20.7 14.4 %collective-permute-done.1 = bf16[384,6,128]{2,0,1:T(8,128)(2,1)S(1)} collective-permute-done((bf16[384,6,128]{2,0,1:T(8,128)(2,1)}, bf16[384,6,128]{2,0,1:T(8,128)(2,1)S(1)}, u32[]{:S(2)}, u32[]{:S(2)}) %collective-permute-start.1) | collective-permute-done | bytes 589856 | tf_op jit(solution)/shard_map/ppermute | solution.py:17
  36.0 1.3 collective-permute-start.6
  37.4 1.6 %collective-permute-start.11 = (bf16[2,768,256]{2,1,0:T(8,128)(2,1)}, bf16[2,768,256]{2,1,0:T(8,128)(2,1)}, u32[]{:S(2)}, u32[]{:S(2)}) collective-permute-start(bf16[2,768,256]{2,1,0:T(8,128)(2,1)} %fusion.1.refs_6_), channel_id=1, source_target_pairs={{0,8},{2,10},{5,13},{7,15},{8,0},{10,2},{13,5},{15,7},{16,24},{18,... | collective-permute-start | bytes 2359304 | tf_op jit(solution)/shard_map/ppermute | solution.py:373
  39.0 1.7 %collective-permute-start.9 = (bf16[2,768,384]{2,1,0:T(8,128)(2,1)S(1)}, bf16[2,768,384]{2,1,0:T(8,128)(2,1)}, u32[]{:S(2)}, u32[]{:S(2)}) collective-permute-start(bf16[2,768,384]{2,1,0:T(8,128)(2,1)S(1)} %fusion.refs_5_), channel_id=1, source_target_pairs={{0,8},{2,10},{5,13},{7,15},{8,0},{10,2},{13,5},{15,7},{16,24},{18,... | collective-permute-start | bytes 3538952 | tf_op jit(solution)/shard_map/ppermute | solution.py:373
  40.7 4.6 %collective-permute-done.2 = bf16[384,6,128]{2,0,1:T(8,128)(2,1)} collective-permute-done((bf16[384,6,128]{2,0,1:T(8,128)(2,1)}, bf16[384,6,128]{2,0,1:T(8,128)(2,1)}, u32[]{:S(2)}, u32[]{:S(2)}) %collective-permute-start.2) | collective-permute-done | bytes 589856 | tf_op jit(solution)/shard_map/ppermute | solution.py:17
  45.3 13.9 %collective-permute-done.3 = bf16[384,6,128]{2,0,1:T(8,128)(2,1)} collective-permute-done((bf16[384,6,128]{2,0,1:T(8,128)(2,1)}, bf16[384,6,128]{2,0,1:T(8,128)(2,1)}, u32[]{:S(2)}, u32[]{:S(2)}) %collective-permute-start.3) | collective-permute-done | bytes 589856 | tf_op jit(solution)/shard_map/ppermute | solution.py:17
  59.2 1.1 copy-done.4
  60.3 1.1 copy-done.6
  62.4 10.2 %attend.1.refs_1_.refs_2_.refs_3_ = bf16[384,768]{1,0:T(8,128)(2,1)} custom-call(f32[3,1152]{1,0:T(4,128)S(1)} %bitcast.18, bf16[6,384,128]{2,1,0:T(8,128)(2,1)S(1)} %bitcast.19, bf16[6,384,128]{2,1,0:T(8,128)(2,1)S(1)} %bitcast.20, bf16[6,384,128]{2,1,0:T(8,128)(2,1)} %bitcast.5.refs_1_, bf16[6,384,128]{2,1,0:T(8,128)(2,1)S(1)} %bitcast.21, ...), custom_call_target="tpu_custom_call" | custom-call | flops 20000000000 | bytes 10000000 | tf_op jit(solution)/shard_map/attend/pallas_call | solution.py:56
  72.6 1.3 collective-permute-start.4
  73.9 1.3 collective-permute-start.12
  75.2 25.9 %collective-permute-done.6.refs_6_.refs_7_ = bf16[2,768,640]{2,1,0:T(8,128)(2,1)} collective-permute-done((bf16[2,768,640]{2,1,0:T(8,128)(2,1)}, bf16[2,768,640]{2,1,0:T(8,128)(2,1)}, u32[]{:S(2)}, u32[]{:S(2)}) %collective-permute-start.6) | collective-permute-done | bytes 1966112 | tf_op jit(solution)/shard_map/ppermute | solution.py:373
  101.1 1.3 collective-permute-start.10
  104.4 5.1 %collective-permute-done.12.refs_0_ = bf16[2,768,256]{2,1,0:T(8,128)(2,1)} collective-permute-done((bf16[2,768,256]{2,1,0:T(8,128)(2,1)}, bf16[2,768,256]{2,1,0:T(8,128)(2,1)}, u32[]{:S(2)}, u32[]{:S(2)}) %collective-permute-start.12) | collective-permute-done | bytes 786464 | tf_op jit(solution)/shard_map/ppermute | solution.py:373
  109.5 3.5 %early_terms.1.refs_10_.refs_2_ = f32[2,384,384]{2,1,0:T(8,128)S(1)} custom-call(s32[1]{0:T(128)} %bitcast.1.refs_0_, bf16[384,768]{1,0:T(8,128)(2,1)} %attend.1.refs_1_.refs_2_.refs_3_, bf16[384,768]{1,0:T(8,128)(2,1)} %collective-permute-done.4.refs_2_.refs_3_.refs_4_, bf16[384,768]{1,0:T(8,128)(2,1)} %held.4.refs_3_.refs_4_.refs_5_, ...), custom_call_target="tpu_custom_call" | custom-call | bytes 6684672 | tf_op jit(solution)/shard_map/early_terms/pallas_call | solution.py:122
  113.0 5.6 %terms.1 = (f32[384,256]{1,0:T(8,128)S(1)}, bf16[384,256]{1,0:T(8,128)(2,1)}, bf16[384,256]{1,0:T(8,128)(2,1)}, bf16[384,256]{1,0:T(8,128)(2,1)}) custom-call(s32[1]{0:T(128)} %bitcast.1.refs_0_, s32[1]{0:T(128)} %bitcast.2.refs_1_, bf16[384,768]{1,0:T(8,128)(2,1)} %attend.1.refs_1_.refs_2_.refs_3_, ...), custom_call_target="tpu_custom_call" | custom-call | flops 858993459200 | bytes 7667712 | tf_op jit(solution)/shard_map/terms/pallas_call | solution.py:122
  118.6 1.9 %collective-permute-start.16 = (bf16[384,256]{1,0:T(8,128)(2,1)}, bf16[384,256]{1,0:T(8,128)(2,1)}, u32[]{:S(2)}, u32[]{:S(2)}) collective-permute-start(bf16[384,256]{1,0:T(8,128)(2,1)} %get-tuple-element.28.refs_9_), channel_id=1, source_target_pairs={{0,2},{1,3},{2,0},{3,1},{4,6},{5,7},{6,4},{7,5},{8,10},{9,11},{10,... | collective-permute-start | bytes 589832 | tf_op jit(solution)/shard_map/ppermute | solution.py:22
  120.6 1.2 collective-permute-start.17
  122.5 4.4 %late_terms.1 = (f32[384,384]{1,0:T(8,128)S(1)}, bf16[384,384]{1,0:T(8,128)(2,1)}, bf16[384,384]{1,0:T(8,128)(2,1)}, bf16[384,384]{1,0:T(8,128)(2,1)}) custom-call(s32[1]{0:T(128)} %bitcast.1.refs_0_, s32[1]{0:T(128)} %bitcast.2.refs_1_, f32[2,384,384]{2,1,0:T(8,128)S(1)} %early_terms.1.refs_10_.refs_2_, bf16[384,768]{1,0:T(8,128)(2,1)} %attend.1.refs_1_.refs_2_.refs_3_, ...), custom_call_target="tpu_custom_call" | custom-call | flops 858993459200 | bytes 7372800 | tf_op jit(solution)/shard_map/late_terms/pallas_call | solution.py:122
  127.7 1.6 %collective-permute-start.13 = (bf16[384,384]{1,0:T(8,128)(2,1)}, bf16[384,384]{1,0:T(8,128)(2,1)}, u32[]{:S(2)}, u32[]{:S(2)}) collective-permute-start(bf16[384,384]{1,0:T(8,128)(2,1)} %get-tuple-element.30), channel_id=1, source_target_pairs={{0,2},{1,3},{2,0},{3,1},{4,6},{5,7},{6,4},{7,5},{8,10},{9,11},{10,... | collective-permute-start | bytes 884744 | tf_op jit(solution)/shard_map/ppermute | solution.py:22
  129.3 1.5 %collective-permute-start.14 = (bf16[384,384]{1,0:T(8,128)(2,1)}, bf16[384,384]{1,0:T(8,128)(2,1)}, u32[]{:S(2)}, u32[]{:S(2)}) collective-permute-start(bf16[384,384]{1,0:T(8,128)(2,1)} %get-tuple-element.31), channel_id=1, source_target_pairs={{0,16},{16,0},{1,17},{17,1},{2,18},{18,2},{3,19},{19,3},{4,20},{20... | collective-permute-start | bytes 884744 | tf_op jit(solution)/shard_map/ppermute | solution.py:22
  130.9 2.0 %gated.2.refs_4_ = bf16[384,1280]{1,0:T(8,128)(2,1)} custom-call(s32[1]{0:T(128)} %bitcast.video_ref, f32[1,1280]{1,0:T(1,128)S(1)} %reshape.23.gate_ref, f32[384,256]{1,0:T(8,128)S(1)} %get-tuple-element.33.refs_0_, bf16[384,256]{1,0:T(8,128)(2,1)} %get-tuple-element.36.refs_1_, bf16[384,256]{1,0:T(8,128)(2,1)} %get-tuple-element.37.refs_2_, ...), custom_call_target="tpu_custom_call" | custom-call | tf_op jit(solution)/shard_map/gated/pallas_call | solution.py:340
  132.9 4.4 %collective-permute-done.13.refs_1_ = bf16[384,384]{1,0:T(8,128)(2,1)} collective-permute-done((bf16[384,384]{1,0:T(8,128)(2,1)}, bf16[384,384]{1,0:T(8,128)(2,1)}, u32[]{:S(2)}, u32[]{:S(2)}) %collective-permute-start.13) | collective-permute-done | bytes 294944 | tf_op jit(solution)/shard_map/ppermute | solution.py:22
  137.2 5.6 %collective-permute-done.14.refs_2_ = bf16[384,384]{1,0:T(8,128)(2,1)} collective-permute-done((bf16[384,384]{1,0:T(8,128)(2,1)}, bf16[384,384]{1,0:T(8,128)(2,1)}, u32[]{:S(2)}, u32[]{:S(2)}) %collective-permute-start.14) | collective-permute-done | bytes 294944 | tf_op jit(solution)/shard_map/ppermute | solution.py:22
  142.9 2.1 %gated.3 = bf16[384,1280]{1,0:T(8,128)(2,1)} custom-call(s32[1]{0:T(128)} %bitcast.video_ref, f32[1,1280]{1,0:T(1,128)S(1)} %reshape.23.gate_ref, f32[384,384]{1,0:T(8,128)S(1)} %copy-done.3, bf16[384,384]{1,0:T(8,128)(2,1)} %collective-permute-done.13.refs_1_, bf16[384,384]{1,0:T(8,128)(2,1)} %collective-permute-done.14.refs_2_, ...), custom_call_target="tpu_custom_call", output_to_operand_aliasing={{}: (6, {})} | custom-call | tf_op jit(solution)/shard_map/gated/pallas_call | solution.py:340
  (47 shorter events, 8.2 us)
Async XLA Ops:
  0.0 1.5 %copy-start = (bf16[768,1280]{1,0:T(8,128)(2,1)S(1)}, bf16[768,1280]{1,0:T(8,128)(2,1)}, u32[]{:S(2)}) copy-start(bf16[768,1280]{1,0:T(8,128)(2,1)} %param.10) | copy-start | bytes 5898244
  0.0 10.5 %copy-start.10 = (s32[3,9]{1,0:T(4,128)S(1)}, s32[3,9]{1,0:T(4,128)}, u32[]{:S(2)}) copy-start(s32[3,9]{1,0:T(4,128)} %param.9) | copy-start | bytes 328
  1.6 8.9 %collective-permute-start.5 = (bf16[768,640]{1,0:T(8,128)(2,1)S(1)}, bf16[768,640]{1,0:T(8,128)(2,1)S(1)}, u32[]{:S(2)}, u32[]{:S(2)}) collective-permute-start(bf16[768,640]{1,0:T(8,128)(2,1)S(1)} %constant_dynamic-slice_fusion), channel_id=1, source_target_pairs={{1,0},{3,2},{4,5},{6,7},{9,8},{11,10},{12,13},{14,15},{17,16},{19,... | collective-permute-start | bytes 2949128 | tf_op jit(solution)/shard_map/ppermute | solution.py:373
  3.7 16.2 %collective-permute-start = (bf16[384,6,128]{2,0,1:T(8,128)(2,1)}, bf16[384,6,128]{2,0,1:T(8,128)(2,1)S(1)}, u32[]{:S(2)}, u32[]{:S(2)}) collective-permute-start(bf16[384,6,128]{2,0,1:T(8,128)(2,1)} %param.7), channel_id=1, source_target_pairs={{0,4},{4,8},{8,12},{12,0},{1,5},{5,9},{9,13},{13,1},{2,6},{6,10},{... | collective-permute-start | bytes 1769480 | tf_op jit(solution)/shard_map/ppermute | solution.py:17
  5.1 30.0 %collective-permute-start.1 = (bf16[384,6,128]{2,0,1:T(8,128)(2,1)}, bf16[384,6,128]{2,0,1:T(8,128)(2,1)S(1)}, u32[]{:S(2)}, u32[]{:S(2)}) collective-permute-start(bf16[384,6,128]{2,0,1:T(8,128)(2,1)} %param.7), channel_id=1, source_target_pairs={{0,12},{4,0},{8,4},{12,8},{1,13},{5,1},{9,5},{13,9},{2,14},{6,2},{... | collective-permute-start | bytes 1769480 | tf_op jit(solution)/shard_map/ppermute | solution.py:17
  7.2 38.1 %collective-permute-start.2 = (bf16[384,6,128]{2,0,1:T(8,128)(2,1)}, bf16[384,6,128]{2,0,1:T(8,128)(2,1)}, u32[]{:S(2)}, u32[]{:S(2)}) collective-permute-start(bf16[384,6,128]{2,0,1:T(8,128)(2,1)} %param.8), channel_id=1, source_target_pairs={{0,4},{4,8},{8,12},{12,0},{1,5},{5,9},{9,13},{13,1},{2,6},{6,10},{... | collective-permute-start | bytes 1769480 | tf_op jit(solution)/shard_map/ppermute | solution.py:17
  7.8 51.4 %collective-permute-start.3 = (bf16[384,6,128]{2,0,1:T(8,128)(2,1)}, bf16[384,6,128]{2,0,1:T(8,128)(2,1)}, u32[]{:S(2)}, u32[]{:S(2)}) collective-permute-start(bf16[384,6,128]{2,0,1:T(8,128)(2,1)} %param.8), channel_id=1, source_target_pairs={{0,12},{4,0},{8,4},{12,8},{1,13},{5,1},{9,5},{13,9},{2,14},{6,2},{... | collective-permute-start | bytes 1769480 | tf_op jit(solution)/shard_map/ppermute | solution.py:17
  11.7 25.7 %copy-start.9 = (f32[1280]{0:T(1024)S(1)}, f32[1280]{0:T(1024)}, u32[]{:S(2)}) copy-start(f32[1280]{0:T(1024)} %param.11) | copy-start | bytes 15364
  19.9 0.8 copy-start.5
  35.1 0.9 copy-start.7
  36.0 65.1 %collective-permute-start.6 = (bf16[2,768,640]{2,1,0:T(8,128)(2,1)}, bf16[2,768,640]{2,1,0:T(8,128)(2,1)}, u32[]{:S(2)}, u32[]{:S(2)}) collective-permute-start(bf16[2,768,640]{2,1,0:T(8,128)(2,1)} %pad_maximum_fusion), channel_id=1, source_target_pairs={{0,4},{2,6},{5,1},{7,3},{8,12},{10,14},{13,9},{15,11},{16,20},{18,... | collective-permute-start | bytes 5898248 | tf_op jit(solution)/shard_map/ppermute | solution.py:373
  37.4 36.5 %collective-permute-start.11 = (bf16[2,768,256]{2,1,0:T(8,128)(2,1)}, bf16[2,768,256]{2,1,0:T(8,128)(2,1)}, u32[]{:S(2)}, u32[]{:S(2)}) collective-permute-start(bf16[2,768,256]{2,1,0:T(8,128)(2,1)} %fusion.1.refs_6_), channel_id=1, source_target_pairs={{0,8},{2,10},{5,13},{7,15},{8,0},{10,2},{13,5},{15,7},{16,24},{18,... | collective-permute-start | bytes 2359304 | tf_op jit(solution)/shard_map/ppermute | solution.py:373
  39.0 62.1 %collective-permute-start.9 = (bf16[2,768,384]{2,1,0:T(8,128)(2,1)S(1)}, bf16[2,768,384]{2,1,0:T(8,128)(2,1)}, u32[]{:S(2)}, u32[]{:S(2)}) collective-permute-start(bf16[2,768,384]{2,1,0:T(8,128)(2,1)S(1)} %fusion.refs_5_), channel_id=1, source_target_pairs={{0,8},{2,10},{5,13},{7,15},{8,0},{10,2},{13,5},{15,7},{16,24},{18,... | collective-permute-start | bytes 3538952 | tf_op jit(solution)/shard_map/ppermute | solution.py:373
  59.2 1.1 copy-start.4
  60.3 1.1 copy-start.6
  61.3 1.1 copy-start.8
  72.6 30.9 %collective-permute-start.4 = (bf16[384,768]{1,0:T(8,128)(2,1)}, bf16[384,768]{1,0:T(8,128)(2,1)}, u32[]{:S(2)}, u32[]{:S(2)}) collective-permute-start(bf16[384,768]{1,0:T(8,128)(2,1)} %attend.1.refs_1_.refs_2_.refs_3_), channel_id=1, source_target_pairs={{0,16},{16,0},{1,17},{17,1},{2,18},{18,2},{3,19},{19,3},{4,20},{20... | collective-permute-start | bytes 1769480 | tf_op jit(solution)/shard_map/ppermute | solution.py:22
  73.9 35.6 %collective-permute-start.12 = (bf16[2,768,256]{2,1,0:T(8,128)(2,1)}, bf16[2,768,256]{2,1,0:T(8,128)(2,1)}, u32[]{:S(2)}, u32[]{:S(2)}) collective-permute-start(bf16[2,768,256]{2,1,0:T(8,128)(2,1)} %collective-permute-done.11.refs_8_), channel_id=1, source_target_pairs={{0,4},{2,6},{5,1},{7,3},{8,12},{10,14},{13,9},{15,11},{16,20},{18,... | collective-permute-start | bytes 2359304 | tf_op jit(solution)/shard_map/ppermute | solution.py:373
  101.1 2.3 %collective-permute-start.7 = (bf16[384,768]{1,0:T(8,128)(2,1)}, bf16[384,768]{1,0:T(8,128)(2,1)}, u32[]{:S(2)}, u32[]{:S(2)}) collective-permute-start(bf16[384,768]{1,0:T(8,128)(2,1)} %attend.1.refs_1_.refs_2_.refs_3_), channel_id=1, source_target_pairs={{0,1},{1,0},{2,3},{3,2},{4,5},{5,4},{6,7},{7,6},{8,9},{9,8},{10,11... | collective-permute-start | bytes 1769480 | tf_op jit(solution)/shard_map/ppermute | solution.py:22
  101.1 21.4 %collective-permute-start.10 = (bf16[2,768,384]{2,1,0:T(8,128)(2,1)}, bf16[2,768,384]{2,1,0:T(8,128)(2,1)}, u32[]{:S(2)}, u32[]{:S(2)}) collective-permute-start(bf16[2,768,384]{2,1,0:T(8,128)(2,1)} %held.5.refs_7_), channel_id=1, source_target_pairs={{0,4},{2,6},{5,1},{7,3},{8,12},{10,14},{13,9},{15,11},{16,20},{18,... | collective-permute-start | bytes 3538952 | tf_op jit(solution)/shard_map/ppermute | solution.py:373
  103.5 6.1 %collective-permute-start.8 = (bf16[384,768]{1,0:T(8,128)(2,1)}, bf16[384,768]{1,0:T(8,128)(2,1)}, u32[]{:S(2)}, u32[]{:S(2)}) collective-permute-start(bf16[384,768]{1,0:T(8,128)(2,1)} %collective-permute-done.4.refs_2_.refs_3_.refs_4_), channel_id=1, source_target_pairs={{0,1},{1,0},{2,3},{3,2},{4,5},{5,4},{6,7},{7,6},{8,9},{9,8},{10,11... | collective-permute-start | bytes 1769480 | tf_op jit(solution)/shard_map/ppermute | solution.py:22
  109.5 3.5 %copy-start.1 = (bf16[2,768,256]{2,1,0:T(8,128)(2,1)S(1)}, bf16[2,768,256]{2,1,0:T(8,128)(2,1)}, u32[]{:S(2)}) copy-start(bf16[2,768,256]{2,1,0:T(8,128)(2,1)} %fusion.1.refs_6_) | copy-start | bytes 2359300
  118.6 12.2 %collective-permute-start.16 = (bf16[384,256]{1,0:T(8,128)(2,1)}, bf16[384,256]{1,0:T(8,128)(2,1)}, u32[]{:S(2)}, u32[]{:S(2)}) collective-permute-start(bf16[384,256]{1,0:T(8,128)(2,1)} %get-tuple-element.28.refs_9_), channel_id=1, source_target_pairs={{0,2},{1,3},{2,0},{3,1},{4,6},{5,7},{6,4},{7,5},{8,10},{9,11},{10,... | collective-permute-start | bytes 589832 | tf_op jit(solution)/shard_map/ppermute | solution.py:22
  120.6 10.3 %collective-permute-start.17 = (bf16[384,256]{1,0:T(8,128)(2,1)}, bf16[384,256]{1,0:T(8,128)(2,1)}, u32[]{:S(2)}, u32[]{:S(2)}) collective-permute-start(bf16[384,256]{1,0:T(8,128)(2,1)} %get-tuple-element.34), channel_id=1, source_target_pairs={{0,16},{16,0},{1,17},{17,1},{2,18},{18,2},{3,19},{19,3},{4,20},{20... | collective-permute-start | bytes 589832 | tf_op jit(solution)/shard_map/ppermute | solution.py:22
  121.8 9.0 %collective-permute-start.18 = (bf16[384,256]{1,0:T(8,128)(2,1)}, bf16[384,256]{1,0:T(8,128)(2,1)}, u32[]{:S(2)}, u32[]{:S(2)}) collective-permute-start(bf16[384,256]{1,0:T(8,128)(2,1)} %get-tuple-element.35), channel_id=1, source_target_pairs={{0,18},{1,19},{2,16},{3,17},{16,2},{17,3},{18,0},{19,1},{4,22},{5,... | collective-permute-start | bytes 589832 | tf_op jit(solution)/shard_map/ppermute | solution.py:80
  126.9 0.8 copy-start.2
  127.7 9.5 %collective-permute-start.13 = (bf16[384,384]{1,0:T(8,128)(2,1)}, bf16[384,384]{1,0:T(8,128)(2,1)}, u32[]{:S(2)}, u32[]{:S(2)}) collective-permute-start(bf16[384,384]{1,0:T(8,128)(2,1)} %get-tuple-element.30), channel_id=1, source_target_pairs={{0,2},{1,3},{2,0},{3,1},{4,6},{5,7},{6,4},{7,5},{8,10},{9,11},{10,... | collective-permute-start | bytes 884744 | tf_op jit(solution)/shard_map/ppermute | solution.py:22
  129.3 13.6 %collective-permute-start.14 = (bf16[384,384]{1,0:T(8,128)(2,1)}, bf16[384,384]{1,0:T(8,128)(2,1)}, u32[]{:S(2)}, u32[]{:S(2)}) collective-permute-start(bf16[384,384]{1,0:T(8,128)(2,1)} %get-tuple-element.31), channel_id=1, source_target_pairs={{0,16},{16,0},{1,17},{17,1},{2,18},{18,2},{3,19},{19,3},{4,20},{20... | collective-permute-start | bytes 884744 | tf_op jit(solution)/shard_map/ppermute | solution.py:22
  130.8 12.0 %collective-permute-start.15 = (bf16[384,384]{1,0:T(8,128)(2,1)}, bf16[384,384]{1,0:T(8,128)(2,1)}, u32[]{:S(2)}, u32[]{:S(2)}) collective-permute-start(bf16[384,384]{1,0:T(8,128)(2,1)} %get-tuple-element.32), channel_id=1, source_target_pairs={{0,18},{1,19},{2,16},{3,17},{16,2},{17,3},{18,0},{19,1},{4,22},{5,... | collective-permute-start | bytes 884744 | tf_op jit(solution)/shard_map/ppermute | solution.py:80
  130.9 12.0 %copy-start.3 = (f32[384,384]{1,0:T(8,128)S(1)}, f32[384,384]{1,0:T(8,128)}, u32[]{:S(2)}) copy-start(f32[384,384]{1,0:T(8,128)} %copy-done.2) | copy-start | bytes 1769476
